TPU v7x, 512 devices: a whole 4x8x8 slice. The times are simulated.
512 devices in a mesh: dp: 64 (over y_hi, z, core), tensor: 8 (over y_lo, x).
Axes of the slice: x: 4, y: 8 (y_hi: 4, y_lo: 2; y = y_hi * 2 + y_lo), z: 8, core: 2. Of those that a mesh axis runs over, the one named last changes fastest.
Arguments:
- activations: bfloat16 [40960, 2048], P('dp', 'tensor'), may hold values from -6 to 6
- cotangent: bfloat16 [40960, 2048], P('dp', 'tensor'), may hold values from -6 to 6
- kv_weight: bfloat16 [64, 2048, 2048], P('dp', None, 'tensor'), may hold values from -6 to 6
- momentum: bfloat16 [64, 2048, 2048], P('dp', None, 'tensor'), may hold values from -6 to 6
- alive_mask: int32 [64], P('dp'), may hold values 0 or 1
Outputs:
- new_weight: bfloat16 [64, 2048, 2048], P('dp', None, 'tensor')
- new_momentum: bfloat16 [64, 2048, 2048], P('dp', None, 'tensor')
- input_grad: bfloat16 [40960, 2048], P(('dp', 'tensor'))
All inputs are finite; a program needn't handle non-finite values. No bound on the sum of `alive_mask` on one device may be relied on, other than what follows from the above.
Results may differ from a plain program's by a relative error of at most 0.017.
Values may be sent and summed in bfloat16 or wider, within the bound.
No kernel may reach another device: no remote copies, remote signals or barrier semaphores. Data moves between devices by JAX's collectives and lax.ppermute only.
A program may use at most 64 MiB of HBM per device.

v0:
```python
import math

import jax
import jax.numpy as jnp
from jax import lax
from jax.sharding import PartitionSpec as P

GROUP = 8


step_size = 0.25
decay_factor = 0.9


def partner_2(value, axis, stride):
    return lax.ppermute(value, axis, [(i, i ^ 1 << stride) for i in range(lax.axis_size(axis))])


def body(activations, cotangent, kv_weight, momentum, alive_mask):
    weight = kv_weight[0]
    features = weight.shape[0]
    unit_scale = 1.0 / math.sqrt(features)
    gradient = (
        lax.dot_general(
            lax.all_gather(activations, "tensor", axis=1, tiled=True),
            cotangent,
            (((0,), (0,)), ((), ())),
            preferred_element_type=jnp.float32,
        )
        * unit_scale
    )
    moment_new = decay_factor * momentum[0].astype(jnp.float32) + gradient
    weight_new = weight.astype(jnp.float32) - step_size * moment_new
    live_flag = alive_mask.astype(jnp.float32)
    contrib = weight_new * live_flag[0]
    levels = GROUP.bit_length() - 1
    running, count_sum = (contrib, live_flag)
    for bit_pos in range(levels):
        partner, partner_count = partner_2((running, count_sum), "dp", bit_pos)
        running = running + partner
        count_sum = count_sum + partner_count
    average = (running / jnp.maximum(count_sum, 1.0)).astype(jnp.bfloat16)
    averaged = jnp.where(live_flag[0] > 0.5, average.astype(jnp.float32), weight_new).astype(
        jnp.bfloat16
    )
    summed = lax.psum_scatter(
        (
            lax.dot_general(
                cotangent, weight, (((1,), (1,)), ((), ())), preferred_element_type=jnp.float32
            )
            * unit_scale
        ).astype(jnp.bfloat16),
        "tensor",
        scatter_dimension=0,
        tiled=True,
    )
    return (averaged[None], moment_new.astype(jnp.bfloat16)[None], summed)


def solution(mesh):
    return jax.shard_map(
        body,
        mesh=mesh,
        in_specs=(
            P("dp", "tensor"),
            P("dp", "tensor"),
            P("dp", None, "tensor"),
            P("dp", None, "tensor"),
            P("dp"),
        ),
        out_specs=(P("dp", None, "tensor"), P("dp", None, "tensor"), P(("dp", "tensor"), None)),
        check_vma=False,
    )
```

profile of v0, /device:TPU:1, one launch (start us, length us, event | category | flops | bytes accessed | tf_op | source)
XLA Modules:
  0.0 239.1 jit_solution(11715579744722914655)
XLA Ops:
  7.2 0.0 copy-start
  7.2 0.0 all-gather.2.cloned.1.call-start
  7.2 0.7 all-gather.2.cloned.1.call-update
  7.9 0.0 reduce-scatter.2.cloned.1.call-start
  8.6 58.0 %all-gather.2.cloned.1.call-done = bf16[640,2048]{1,0:T(8,128)(2,1)} async-done(((bf16[640,256]{1,0:T(8,128)(2,1)}), bf16[640,2048]{1,0:T(8,128)(2,1)}) %all-gather.2.cloned.1.call-update) | async-done | bytes 2621456 | tf_op jit(solution)/shard_map/all_gather | solution.py:25
  66.6 0.0 copy-done
  66.6 0.0 copy-start.1
  66.6 4.9 %fusion.1 = (f32[2048,256]{1,0:T(8,128)S(1)}, f32[2048,256]{1,0:T(8,128)}) fusion(bf16[1,2048,256]{2,1,0:T(8,128)(2,1)} %param.7, f32[]{:T(128)} %bitcast, bf16[640,2048]{1,0:T(8,128)(2,1)} %all-gather.2.cloned.1.call-done, bf16[640,256]{1,0:T(8,128)(2,1)S(1)} %copy-done, bf16[1,2048,256]{2,1,0:T(8,128)(2,1)} %param.8), kind=kOutput, calls=%fused_computation.6 | convolution fusion | flops 675282944 | bytes 9240580 | tf_op jit(solution)/shard_map/dot_general | solution.py:24
  71.5 5.7 %collective-permute-start = (f32[2048,256]{1,0:T(8,128)S(1)}, f32[2048,256]{1,0:T(8,128)}, u32[]{:S(2)}, u32[]{:S(2)}) collective-permute-start(f32[2048,256]{1,0:T(8,128)S(1)} %get-tuple-element.5), channel_id=1, source_target_pairs={{0,8},{8,0},{16,24},{24,16},{32,40},{40,32},{48,56},{56,48},{64,72... | collective-permute-start | bytes 6291464 | tf_op jit(solution)/shard_map/ppermute | solution.py:16
  77.2 0.0 copy-done.1
  77.2 2.4 %multiply_convert_fusion = bf16[640,2048]{1,0:T(8,128)(2,1)} fusion(bf16[640,256]{1,0:T(8,128)(2,1)S(1)} %copy-done, bf16[1,2048,256]{2,1,0:T(8,128)(2,1)S(1)} %copy-done.1), kind=kOutput, calls=%fused_computation | convolution fusion | flops 673710080 | bytes 3997696 | tf_op jit(solution)/shard_map/dot_general | solution.py:48
  79.6 0.0 reduce-scatter.2.cloned.1.call-update
  79.6 1.5 collective-permute-done
  81.1 1.9 add.24
  82.9 2.5 %collective-permute-start.1 = (f32[2048,256]{1,0:T(8,128)S(1)}, f32[2048,256]{1,0:T(8,128)S(1)}, u32[]{:S(2)}, u32[]{:S(2)}) collective-permute-start(f32[2048,256]{1,0:T(8,128)S(1)} %add.24), channel_id=1, source_target_pairs={{0,16},{8,24},{16,0},{24,8},{32,48},{40,56},{48,32},{56,40},{64,80... | collective-permute-start | bytes 6291464 | tf_op jit(solution)/shard_map/ppermute | solution.py:16
  85.5 46.2 %collective-permute-done.1 = f32[2048,256]{1,0:T(8,128)S(1)} collective-permute-done((f32[2048,256]{1,0:T(8,128)S(1)}, f32[2048,256]{1,0:T(8,128)S(1)}, u32[]{:S(2)}, u32[]{:S(2)}) %collective-permute-start.1) | collective-permute-done | bytes 2097184 | tf_op jit(solution)/shard_map/ppermute | solution.py:16
  131.7 0.3 add.25
  132.0 3.6 %collective-permute-start.2 = (f32[2048,256]{1,0:T(8,128)S(1)}, f32[2048,256]{1,0:T(8,128)}, u32[]{:S(2)}, u32[]{:S(2)}) collective-permute-start(f32[2048,256]{1,0:T(8,128)S(1)} %add.25), channel_id=1, source_target_pairs={{0,32},{8,40},{16,48},{24,56},{32,0},{40,8},{48,16},{56,24},{64,96... | collective-permute-start | bytes 6291464 | tf_op jit(solution)/shard_map/ppermute | solution.py:16
  135.6 4.2 %collective-permute-start.3 = (f32[1]{0:T(128)}, f32[1]{0:T(128)}, u32[]{:S(2)}, u32[]{:S(2)}) collective-permute-start(f32[1]{0:T(128)} %convert_element_type.25), channel_id=1, source_target_pairs={{0,8},{8,0},{16,24},{24,16},{32,40},{40,32},{48,56},{56,48},{64,72... | collective-permute-start | bytes 20 | tf_op jit(solution)/shard_map/ppermute | solution.py:16
  139.8 0.0 collective-permute-done.3
  140.4 39.0 %collective-permute-start.4 = (f32[1]{0:T(128)}, f32[1]{0:T(128)}, u32[]{:S(2)}, u32[]{:S(2)}) collective-permute-start(f32[1]{0:T(128)} %add.27), channel_id=1, source_target_pairs={{0,16},{8,24},{16,0},{24,8},{32,48},{40,56},{48,32},{56,40},{64,80... | collective-permute-start | bytes 20 | tf_op jit(solution)/shard_map/ppermute | solution.py:16
  179.4 0.0 collective-permute-done.4
  180.0 4.9 %collective-permute-start.5 = (f32[1]{0:T(128)}, f32[1]{0:T(128)}, u32[]{:S(2)}, u32[]{:S(2)}) collective-permute-start(f32[1]{0:T(128)} %add.28), channel_id=1, source_target_pairs={{0,32},{8,40},{16,48},{24,56},{32,0},{40,8},{48,16},{56,24},{64,96... | collective-permute-start | bytes 20 | tf_op jit(solution)/shard_map/ppermute | solution.py:16
  184.9 41.9 %collective-permute-done.5 = f32[1]{0:T(128)} collective-permute-done((f32[1]{0:T(128)}, f32[1]{0:T(128)}, u32[]{:S(2)}, u32[]{:S(2)}) %collective-permute-start.5) | collective-permute-done | bytes 36 | tf_op jit(solution)/shard_map/ppermute | solution.py:16
  227.5 0.0 collective-permute-done.2
  227.5 4.7 %convert_bitcast_fusion = (bf16[1,2048,256]{2,1,0:T(8,128)(2,1)}, bf16[1,2048,256]{2,1,0:T(8,128)(2,1)}) fusion(f32[2048,256]{1,0:T(8,128)} %get-tuple-element.6, bf16[1,2048,256]{2,1,0:T(8,128)(2,1)S(1)} %copy-done.1, f32[]{:T(128)} %bitcast.3, f32[2048,256]{1,0:T(8,128)S(1)} %add.25, f32[2048,256]{1,0:T(8,128)} %collective-permute-done.2, pred[]{:T(512)S(6)} %gt.3), kind=kLoop, calls=%fused_computation.8 | loop fusion | flops 5242880 | bytes 9437189 | tf_op jit(solution)/shard_map/broadcast_in_dim | solution.py:57
  232.2 0.0 reduce-scatter.2.cloned.1.call-done
Async XLA Ops:
  7.2 59.4 %copy-start = (bf16[640,256]{1,0:T(8,128)(2,1)S(1)}, bf16[640,256]{1,0:T(8,128)(2,1)}, u32[]{:S(2)}) copy-start(bf16[640,256]{1,0:T(8,128)(2,1)} %param.6) | copy-start | bytes 983044
  7.2 59.4 %all-gather.2.cloned.1.call-start = ((), (), s32[]{:S(2)}) async-start(), calls=%async_computation.1 | async-start | bytes 2949120 | tf_op jit(solution)/shard_map/all_gather | solution.py:25
  7.9 224.3 %reduce-scatter.2.cloned.1.call-start = ((), (), s32[]{:S(2)}) async-start(), calls=%async_computation.2 | async-start | bytes 2949120 | tf_op jit(solution)/shard_map/reduce_scatter | solution.py:46
  66.6 10.6 %copy-start.1 = (bf16[1,2048,256]{2,1,0:T(8,128)(2,1)S(1)}, bf16[1,2048,256]{2,1,0:T(8,128)(2,1)}, u32[]{:S(2)}) copy-start(bf16[1,2048,256]{2,1,0:T(8,128)(2,1)} %param.7) | copy-start | bytes 3145732
  71.5 9.6 %collective-permute-start = (f32[2048,256]{1,0:T(8,128)S(1)}, f32[2048,256]{1,0:T(8,128)}, u32[]{:S(2)}, u32[]{:S(2)}) collective-permute-start(f32[2048,256]{1,0:T(8,128)S(1)} %get-tuple-element.5), channel_id=1, source_target_pairs={{0,8},{8,0},{16,24},{24,16},{32,40},{40,32},{48,56},{56,48},{64,72... | collective-permute-start | bytes 6291464 | tf_op jit(solution)/shard_map/ppermute | solution.py:16
  82.9 48.7 %collective-permute-start.1 = (f32[2048,256]{1,0:T(8,128)S(1)}, f32[2048,256]{1,0:T(8,128)S(1)}, u32[]{:S(2)}, u32[]{:S(2)}) collective-permute-start(f32[2048,256]{1,0:T(8,128)S(1)} %add.24), channel_id=1, source_target_pairs={{0,16},{8,24},{16,0},{24,8},{32,48},{40,56},{48,32},{56,40},{64,80... | collective-permute-start | bytes 6291464 | tf_op jit(solution)/shard_map/ppermute | solution.py:16
  132.0 95.5 %collective-permute-start.2 = (f32[2048,256]{1,0:T(8,128)S(1)}, f32[2048,256]{1,0:T(8,128)}, u32[]{:S(2)}, u32[]{:S(2)}) collective-permute-start(f32[2048,256]{1,0:T(8,128)S(1)} %add.25), channel_id=1, source_target_pairs={{0,32},{8,40},{16,48},{24,56},{32,0},{40,8},{48,16},{56,24},{64,96... | collective-permute-start | bytes 6291464 | tf_op jit(solution)/shard_map/ppermute | solution.py:16
  135.6 4.2 %collective-permute-start.3 = (f32[1]{0:T(128)}, f32[1]{0:T(128)}, u32[]{:S(2)}, u32[]{:S(2)}) collective-permute-start(f32[1]{0:T(128)} %convert_element_type.25), channel_id=1, source_target_pairs={{0,8},{8,0},{16,24},{24,16},{32,40},{40,32},{48,56},{56,48},{64,72... | collective-permute-start | bytes 20 | tf_op jit(solution)/shard_map/ppermute | solution.py:16
  140.4 39.0 %collective-permute-start.4 = (f32[1]{0:T(128)}, f32[1]{0:T(128)}, u32[]{:S(2)}, u32[]{:S(2)}) collective-permute-start(f32[1]{0:T(128)} %add.27), channel_id=1, source_target_pairs={{0,16},{8,24},{16,0},{24,8},{32,48},{40,56},{48,32},{56,40},{64,80... | collective-permute-start | bytes 20 | tf_op jit(solution)/shard_map/ppermute | solution.py:16
  180.0 46.9 %collective-permute-start.5 = (f32[1]{0:T(128)}, f32[1]{0:T(128)}, u32[]{:S(2)}, u32[]{:S(2)}) collective-permute-start(f32[1]{0:T(128)} %add.28), channel_id=1, source_target_pairs={{0,32},{8,40},{16,48},{24,56},{32,0},{40,8},{48,16},{56,24},{64,96... | collective-permute-start | bytes 20 | tf_op jit(solution)/shard_map/ppermute | solution.py:16
Sparse Core Ops, SparseCore 0:
  10.0 56.5 all-gather.1
  79.7 44.8 reduce-scatter.1
where the time goes:
time: 240 us; the launch traced here: 239 us
  waiting for transfers between devices  148 us (62%)
  starting transfers between devices  60 us (25%)
  between operations  16.6 us (7%)
  matrix products  7.3 us (3%)
  other arithmetic  6.88 us (3%)
    ppermute x6, waiting for transfers between devices, partner_2(): lax.ppermute(value, axis, [(i, i ^ 1 << stride) for i in range(lax.axis_s...  89.6 us
    ppermute x6, starting transfers between devices, partner_2(): lax.ppermute(value, axis, [(i, i ^ 1 << stride) for i in range(lax.axis_s...  59.9 us
    all_gather x1, waiting for transfers between devices, body(): lax.all_gather(activations, 'tensor', axis=1, tiled=True)  58 us
    dot_general x1, matrix products, body(): lax.dot_general(lax.all_gather(activations, 'tensor', axis=1, tiled=True)...  4.91 us
  transfers between devices with their start and end apart: 8, of which 4 were waited for; matrix products, arithmetic and copies ran while one was open for 4% of the time, Pallas kernels for 0%

commit v1 on v0

v1 whole, which is shorter than its diff:
```python
import functools
import math

import jax
import jax.numpy as jnp
from jax import lax
from jax.experimental import pallas as pl
from jax.experimental.pallas import tpu as pltpu
from jax.sharding import PartitionSpec as P

GROUP = 8
step_size = 0.25
decay_factor = 0.9
bf16 = jnp.bfloat16
f32 = jnp.float32

EARLY = (0, 4, 1, 3)
LATE = (7, 5, 2, 6)
PAD = 16
VMEM = pl.BlockSpec(memory_space=pltpu.VMEM)
ANY = pl.BlockSpec(memory_space=pl.ANY)
SMEM = pl.BlockSpec(memory_space=pltpu.SMEM)
PARAMS = pltpu.CompilerParams(vmem_limit_bytes=16 * 1024 * 1024)


def tensor_swap(value, k):
    return lax.ppermute(value, "tensor", [(t, t ^ k) for t in range(lax.axis_size("tensor"))])


def core_swap(value):
    return lax.ppermute(value, "dp", [(r, r ^ 1) for r in range(lax.axis_size("dp"))])


def chip_exchange(value):
    groups = [
        [g * GROUP + 2 * z + c for z in range(GROUP // 2)]
        for g in range(lax.axis_size("dp") // GROUP)
        for c in range(2)
    ]
    return lax.all_to_all(value, "dp", 0, 0, axis_index_groups=groups, tiled=True)


def update_kernel(scale, first, info, *refs):
    n = 4
    acts, (cot, weight, mom) = refs[:n], refs[n : n + 3]
    if first:
        mom_out, own, keep, send = refs[n + 3 : n + 7]
    else:
        mom_out, own, keep, send = refs[n + 4 : n + 8]
    w_buf, m_buf, o_buf, sems = refs[-4:]
    size = w_buf.shape[1]

    def rows(b):
        return pl.ds(pl.multiple_of(info[b] * size, size), size)

    def loads(b):
        return (
            pltpu.make_async_copy(weight.at[rows(b)], w_buf.at[b], sems.at[0, b]),
            pltpu.make_async_copy(mom.at[rows(b)], m_buf.at[b], sems.at[1, b]),
        )

    def store(b):
        return pltpu.make_async_copy(o_buf.at[b], mom_out.at[rows(b)], sems.at[2, b])

    for b in range(n):
        for copy in loads(b):
            copy.start()
    core, alive = info[n], info[n + 1]
    flag = jnp.where(alive > 0, 1.0, 0.0).astype(f32)
    cot_value = cot[...]
    for b in range(n):
        grad = lax.dot_general(
            acts[b][...], cot_value, (((0,), (0,)), ((), ())), preferred_element_type=f32
        )
        for copy in loads(b):
            copy.wait()
        moment = decay_factor * m_buf[b].astype(f32) + grad * scale
        o_buf[b] = moment.astype(bf16)
        store(b).start()
        new = w_buf[b].astype(f32) - step_size * moment
        own[b] = new.astype(bf16)
        part = (new * flag).astype(bf16)
        place = pl.ds((b % 2) * size, size)

        @pl.when(core == b // 2)
        def _():
            keep[place, :] = part

        @pl.when(core != b // 2)
        def _():
            send[place, :] = part

    if first:
        tail = pl.ds(2 * size, PAD)
        keep[tail, :] = jnp.full((PAD, keep.shape[1]), flag, f32).astype(bf16)
        send[tail, :] = jnp.full((PAD, keep.shape[1]), flag, f32).astype(bf16)
    for b in range(n):
        store(b).wait()


def update(scale, info, acts, cot, weight, mom, mom_out):
    first = mom_out is None
    width = cot.shape[1]
    size = acts[0].shape[1]
    half = 2 * size + (PAD if first else 0)
    extra = () if first else (mom_out,)
    return pl.pallas_call(
        functools.partial(update_kernel, scale, first),
        out_shape=(
            jax.ShapeDtypeStruct(weight.shape, bf16),
            jax.ShapeDtypeStruct((4, size, width), bf16),
            jax.ShapeDtypeStruct((half, width), bf16),
            jax.ShapeDtypeStruct((half, width), bf16),
        ),
        in_specs=[SMEM] + [VMEM] * 5 + [ANY] * (2 + len(extra)),
        out_specs=(ANY, VMEM, VMEM, VMEM),
        scratch_shapes=[
            pltpu.VMEM((4, size, width), bf16),
            pltpu.VMEM((4, size, width), bf16),
            pltpu.VMEM((4, size, width), bf16),
            pltpu.SemaphoreType.DMA((3, 4)),
        ],
        input_output_aliases={} if first else {8: 0},
        compiler_params=PARAMS,
        cost_estimate=pl.CostEstimate(
            flops=2 * 4 * cot.shape[0] * size * width, bytes_accessed=4_000_000, transcendentals=0
        ),
    )(info, *acts, cot, weight, mom, *extra)


def place_kernel(info, *refs):
    ins, out, sems = refs[:6], refs[6], refs[7]
    size = ins[0].shape[1]
    core, alive = info[8], info[9]

    def copy(source, b):
        return pltpu.make_async_copy(
            source, out.at[pl.ds(pl.multiple_of(info[b] * size, size), size)], sems.at[b]
        )

    for b in range(8):
        own, mine, other = ins[3 * (b // 4) : 3 * (b // 4) + 3]
        at = pl.ds((b % 2) * size, size)
        is_mine = core == (b % 4) // 2

        @pl.when(alive <= 0)
        def _():
            copy(own.at[b % 4], b).start()

        @pl.when((alive > 0) & is_mine)
        def _():
            copy(mine.at[at], b).start()

        @pl.when((alive > 0) & jnp.logical_not(is_mine))
        def _():
            copy(other.at[at], b).start()

    for b in range(8):
        copy(ins[0].at[0], b).wait()


def place(info, parts, shape):
    return pl.pallas_call(
        place_kernel,
        out_shape=jax.ShapeDtypeStruct(shape, bf16),
        in_specs=[SMEM] + [VMEM] * 6,
        out_specs=ANY,
        scratch_shapes=[pltpu.SemaphoreType.DMA((8,))],
        compiler_params=PARAMS,
        cost_estimate=pl.CostEstimate(flops=0, bytes_accessed=2_000_000, transcendentals=0),
    )(info, *parts)


def body(activations, cotangent, kv_weight, momentum, alive_mask):
    weight, mom = kv_weight[0], momentum[0]
    features, width = weight.shape
    scale = 1.0 / math.sqrt(features)
    t = lax.axis_index("tensor")
    core = lax.rem(lax.axis_index("dp"), 2)
    alive = alive_mask[0]
    tail = jnp.stack([core, alive])
    early = jnp.stack([t ^ k for k in EARLY])
    late = jnp.stack([t ^ k for k in LATE])

    a_y = tensor_swap(activations, 4)
    a_p = tensor_swap(activations, 1)
    a_q = tensor_swap(activations, 3)
    a_qy = tensor_swap(a_y, 3)
    a_yp = tensor_swap(a_p, 4)
    a_pq = tensor_swap(a_q, 1)
    a_ypq = tensor_swap(a_pq, 4)

    partial = (
        lax.dot_general(cotangent, weight, (((1,), (1,)), ((), ())), preferred_element_type=f32)
        * scale
    ).astype(bf16)

    mom_1, own_1, keep_1, send_1 = update(
        scale, jnp.concatenate([early, tail]), (activations, a_y, a_p, a_q), cotangent, weight, mom, None
    )
    half = keep_1.shape[0] - PAD
    quarter = half // 4
    sum_1 = keep_1.astype(f32) + core_swap(send_1).astype(f32)
    flags = jnp.broadcast_to(sum_1[None, half:], (4, PAD, width))
    out_1 = jnp.concatenate([sum_1[:half].reshape(4, quarter, width), flags], axis=1).astype(bf16)
    got_1 = chip_exchange(out_1).astype(f32).sum(0)
    count = jnp.maximum(got_1[quarter : quarter + 1, :1], 1.0)
    mean_1 = (got_1[:quarter] / count).astype(bf16)

    new_momentum, own_2, keep_2, send_2 = update(
        scale, jnp.concatenate([late, tail]), (a_qy, a_yp, a_pq, a_ypq), cotangent, weight, mom, mom_1
    )
    sum_2 = keep_2.astype(f32) + core_swap(send_2).astype(f32)
    got_2 = chip_exchange(sum_2.astype(bf16).reshape(4, quarter, width)).astype(f32).sum(0)
    mean_2 = (got_2 / count).astype(bf16)

    mine_1 = chip_exchange(jnp.broadcast_to(mean_1[None], (4, quarter, width))).reshape(half, width)
    other_1 = core_swap(mine_1)
    mine_2 = chip_exchange(jnp.broadcast_to(mean_2[None], (4, quarter, width))).reshape(half, width)
    other_2 = core_swap(mine_2)

    new_weight = place(
        jnp.concatenate([early, late, tail]),
        (own_1, mine_1, other_1, own_2, mine_2, other_2),
        weight.shape,
    )

    members = lax.axis_size("tensor")
    partial, _ = lax.optimization_barrier((partial, own_2))
    parts = lax.all_to_all(
        partial.reshape(members, partial.shape[0] // members, features), "tensor", 0, 0, tiled=True
    )
    input_grad = parts.astype(f32).sum(0).astype(bf16)
    return new_weight[None], new_momentum[None], input_grad


def solution(mesh):
    return jax.shard_map(
        body,
        mesh=mesh,
        in_specs=(
            P("dp", "tensor"),
            P("dp", "tensor"),
            P("dp", None, "tensor"),
            P("dp", None, "tensor"),
            P("dp"),
        ),
        out_specs=(P("dp", None, "tensor"), P("dp", None, "tensor"), P(("dp", "tensor"), None)),
        check_vma=False,
    )
```

time: 240 us -> 148 us (0.62)
  waiting for transfers between devices: 148 us -> 46.5 us
  between operations: 16.6 us -> 2.2 us
  Pallas kernels: 0 us -> 13.4 us
  local copies, waits for them, and re-layouts: 0.01 us -> 8.32 us
  starting transfers between devices: 60 us -> 66.1 us
  matrix products: 7.3 us -> 2.45 us
    ppermute x6 -> x11, waiting for transfers between devices: 89.6 us -> 8.07 us  [the longest x7 6.66 us: tensor_swap(): lax.ppermute(value, 'tensor', [(t, t ^ k) for t in range(lax.axis_size('t...]
    all_gather x1 -> x0, waiting for transfers between devices: 58 us -> none  [body(): lax.all_gather(activations, 'tensor', axis=1, tiled=True)]
    all_to_all x0 -> x5, waiting for transfers between devices: none -> 38.4 us  [the longest x4 19.9 us: chip_exchange(): lax.all_to_all(value, 'dp', 0, 0, axis_index_groups=groups, tiled=True)]
    all_to_all x0 -> x5, starting transfers between devices: none -> 22.2 us  [the longest x4 17.8 us: chip_exchange(): lax.all_to_all(value, 'dp', 0, 0, axis_index_groups=groups, tiled=True)]
    ppermute x6 -> x11, starting transfers between devices: 59.9 us -> 43.9 us  [the longest x7 25.4 us: tensor_swap(): lax.ppermute(value, 'tensor', [(t, t ^ k) for t in range(lax.axis_size('t...]
    pallas_call x0 -> x3, Pallas kernels: none -> 13.4 us  [the longest x2 11.8 us: update(): pl.pallas_call(functools.partial(update_kernel, scale, first), out_shape=...]
    unnamed x4 -> x20, local copies, waits for them, and re-layouts: 0.01 us -> 6.08 us
    dot_general x1 -> x0, matrix products: 4.91 us -> none  [body(): lax.dot_general(lax.all_gather(activations, 'tensor', axis=1, tiled=True)...]
  transfers between devices with their start and end apart: 8 -> 16, of which waited for: 4 -> 9; matrix products, arithmetic and copies ran while one was open for 4% -> 5% of each run, Pallas kernels for 0% -> 5%
where the time goes in v1:
time: 148 us; the launch traced here: 146 us
  starting transfers between devices  66.1 us (45%)
  waiting for transfers between devices  46.5 us (31%)
  Pallas kernels  13.4 us (9%)
  local copies, waits for them, and re-layouts  8.32 us (6%)
  other arithmetic  6.6 us (4%)
  matrix products  2.45 us (2%)
  between operations  2.2 us (1%)
    ppermute x7, starting transfers between devices, tensor_swap(): lax.ppermute(value, 'tensor', [(t, t ^ k) for t in range(lax.axis_size('t...  25.4 us
    all_to_all x4, waiting for transfers between devices, chip_exchange(): lax.all_to_all(value, 'dp', 0, 0, axis_index_groups=groups, tiled=True)  19.9 us
    all_to_all x1, waiting for transfers between devices, body(): lax.all_to_all(partial.reshape(members, partial.shape[0] // members, feat...  18.5 us
    ppermute x4, starting transfers between devices, core_swap(): lax.ppermute(value, 'dp', [(r, r ^ 1) for r in range(lax.axis_size('dp'))])  18.4 us
    all_to_all x4, starting transfers between devices, chip_exchange(): lax.all_to_all(value, 'dp', 0, 0, axis_index_groups=groups, tiled=True)  17.8 us
    pallas_call x2, Pallas kernels, update(): pl.pallas_call(functools.partial(update_kernel, scale, first), out_shape=...  11.8 us
    ppermute x7, waiting for transfers between devices, tensor_swap(): lax.ppermute(value, 'tensor', [(t, t ^ k) for t in range(lax.axis_size('t...  6.66 us
    unnamed x20, local copies, waits for them, and re-layouts  6.08 us
  transfers between devices with their start and end apart: 16, of which 9 were waited for; matrix products, arithmetic and copies ran while one was open for 5% of the time, Pallas kernels for 5%

profile of v1, /device:TPU:1, one launch (start us, length us, event | category | flops | bytes accessed | tf_op | source)
XLA Modules:
  0.0 145.5 jit_solution(3903079875034301672)
XLA Ops:
  0.6 5.2 %collective-permute-start.2 = (bf16[640,256]{1,0:T(8,128)(2,1)}, bf16[640,256]{1,0:T(8,128)(2,1)}, u32[]{:S(2)}, u32[]{:S(2)}) collective-permute-start(bf16[640,256]{1,0:T(8,128)(2,1)} %refs_0_.1), channel_id=1, source_target_pairs={{0,3},{1,2},{2,1},{3,0},{4,7},{5,6},{6,5},{7,4},{8,11},{9,10},{10,... | collective-permute-start | bytes 983048 | tf_op jit(solution)/shard_map/ppermute | solution.py:27
  5.9 1.9 %collective-permute-start.1 = (bf16[640,256]{1,0:T(8,128)(2,1)}, bf16[640,256]{1,0:T(8,128)(2,1)}, u32[]{:S(2)}, u32[]{:S(2)}) collective-permute-start(bf16[640,256]{1,0:T(8,128)(2,1)} %refs_0_.1), channel_id=1, source_target_pairs={{0,1},{1,0},{2,3},{3,2},{4,5},{5,4},{6,7},{7,6},{8,9},{9,8},{10,11... | collective-permute-start | bytes 983048 | tf_op jit(solution)/shard_map/ppermute | solution.py:27
  7.8 3.2 %collective-permute-start = (bf16[640,256]{1,0:T(8,128)(2,1)}, bf16[640,256]{1,0:T(8,128)(2,1)}, u32[]{:S(2)}, u32[]{:S(2)}) collective-permute-start(bf16[640,256]{1,0:T(8,128)(2,1)} %refs_0_.1), channel_id=1, source_target_pairs={{0,4},{1,5},{2,6},{3,7},{4,0},{5,1},{6,2},{7,3},{8,12},{9,13},{10,... | collective-permute-start | bytes 983048 | tf_op jit(solution)/shard_map/ppermute | solution.py:27
  11.0 0.0 collective-permute-done.2.refs_3_
  11.0 4.3 %collective-permute-start.7 = (bf16[640,256]{1,0:T(8,128)(2,1)}, bf16[640,256]{1,0:T(8,128)(2,1)S(1)}, u32[]{:S(2)}, u32[]{:S(2)}) collective-permute-start(bf16[640,256]{1,0:T(8,128)(2,1)} %collective-permute-done.2.refs_3_), channel_id=1, source_target_pairs={{0,1},{1,0},{2,3},{3,2},{4,5},{5,4},{6,7},{7,6},{8,9},{9,8},{10,11... | collective-permute-start | bytes 983048 | tf_op jit(solution)/shard_map/ppermute | solution.py:27
  16.0 0.1 concatenate.17.info
  16.1 0.0 collective-permute-done.1.refs_2_
  16.1 0.2 collective-permute-done.refs_1_
  16.3 0.0 copy-start
  16.3 1.2 copy-done
  17.5 0.0 copy-start.2
  17.5 1.2 copy-done.2
  18.7 0.0 copy-start.4
  18.7 1.0 copy-done.4
  19.7 0.0 copy-start.8
  19.7 1.0 copy-done.8
  20.7 0.0 copy-start.1
  20.7 6.0 %shard_map.76 = (bf16[2048,256]{1,0:T(8,128)(2,1)}, bf16[4,256,256]{2,1,0:T(8,128)(2,1)S(1)}, bf16[528,256]{1,0:T(8,128)(2,1)S(1)}, bf16[528,256]{1,0:T(8,128)(2,1)}) custom-call(s32[6]{0:T(128)S(1)} %concatenate.17.info, bf16[640,256]{1,0:T(8,128)(2,1)S(1)} %copy-done.8, bf16[640,256]{1,0:T(8,128)(2,1)} %collective-permute-done.refs_1_, ...), custom_call_target="tpu_custom_call" | custom-call | flops 335544320 | bytes 4000000 | tf_op jit(solution)/shard_map/pallas_call | solution.py:107
  26.7 6.3 %collective-permute-start.3 = (bf16[528,256]{1,0:T(8,128)(2,1)}, bf16[528,256]{1,0:T(8,128)(2,1)}, u32[]{:S(2)}, u32[]{:S(2)}) collective-permute-start(bf16[528,256]{1,0:T(8,128)(2,1)} %get-tuple-element.14), channel_id=1, source_target_pairs={{0,8},{8,0},{16,24},{24,16},{32,40},{40,32},{48,56},{56,48},{64,72... | collective-permute-start | bytes 811016 | tf_op jit(solution)/shard_map/ppermute | solution.py:31
  33.0 2.7 %collective-permute-start.6 = (bf16[640,256]{1,0:T(8,128)(2,1)}, bf16[640,256]{1,0:T(8,128)(2,1)}, u32[]{:S(2)}, u32[]{:S(2)}) collective-permute-start(bf16[640,256]{1,0:T(8,128)(2,1)} %collective-permute-done.1.refs_2_), channel_id=1, source_target_pairs={{0,4},{1,5},{2,6},{3,7},{4,0},{5,1},{6,2},{7,3},{8,12},{9,13},{10,... | collective-permute-start | bytes 983048 | tf_op jit(solution)/shard_map/ppermute | solution.py:27
  35.6 4.7 %collective-permute-start.5 = (bf16[640,256]{1,0:T(8,128)(2,1)}, bf16[640,256]{1,0:T(8,128)(2,1)}, u32[]{:S(2)}, u32[]{:S(2)}) collective-permute-start(bf16[640,256]{1,0:T(8,128)(2,1)} %collective-permute-done.refs_1_), channel_id=1, source_target_pairs={{0,3},{1,2},{2,1},{3,0},{4,7},{5,6},{6,5},{7,4},{8,11},{9,10},{10,... | collective-permute-start | bytes 983048 | tf_op jit(solution)/shard_map/ppermute | solution.py:27
  40.4 0.0 collective-permute-done.7.refs_2_
  40.4 0.0 copy-start.6
  40.4 3.4 %collective-permute-start.8 = (bf16[640,256]{1,0:T(8,128)(2,1)S(1)}, bf16[640,256]{1,0:T(8,128)(2,1)}, u32[]{:S(2)}, u32[]{:S(2)}) collective-permute-start(bf16[640,256]{1,0:T(8,128)(2,1)S(1)} %collective-permute-done.7.refs_2_), channel_id=1, source_target_pairs={{0,4},{1,5},{2,6},{3,7},{4,0},{5,1},{6,2},{7,3},{8,12},{9,13},{10,... | collective-permute-start | bytes 983048 | tf_op jit(solution)/shard_map/ppermute | solution.py:27
  43.8 0.1 concatenate.19.info
  43.9 0.0 collective-permute-done.3
  43.9 1.0 convert_add_fusion
  44.9 0.0 collective-permute-done.6.refs_1_
  44.9 3.5 %collective-permute-done.5.refs_0_ = bf16[640,256]{1,0:T(8,128)(2,1)} collective-permute-done((bf16[640,256]{1,0:T(8,128)(2,1)}, bf16[640,256]{1,0:T(8,128)(2,1)}, u32[]{:S(2)}, u32[]{:S(2)}) %collective-permute-start.5) | collective-permute-done | bytes 327712 | tf_op jit(solution)/shard_map/ppermute | solution.py:27
  48.4 3.0 %collective-permute-done.8.refs_3_ = bf16[640,256]{1,0:T(8,128)(2,1)} collective-permute-done((bf16[640,256]{1,0:T(8,128)(2,1)S(1)}, bf16[640,256]{1,0:T(8,128)(2,1)}, u32[]{:S(2)}, u32[]{:S(2)}) %collective-permute-start.8) | collective-permute-done | bytes 327712 | tf_op jit(solution)/shard_map/ppermute | solution.py:27
  51.4 0.0 copy-done.6
  51.4 0.0 copy-done.1
  51.4 0.0 copy-done.3
  51.4 0.0 copy-done.5
  51.4 0.0 copy-start.7
  51.4 1.0 copy-done.7
  52.4 5.8 %shard_map.77 = (bf16[2048,256]{1,0:T(8,128)(2,1)}, bf16[4,256,256]{2,1,0:T(8,128)(2,1)S(1)}, bf16[512,256]{1,0:T(8,128)(2,1)S(1)}, bf16[512,256]{1,0:T(8,128)(2,1)}) custom-call(s32[6]{0:T(128)S(1)} %concatenate.19.info, bf16[640,256]{1,0:T(8,128)(2,1)} %collective-permute-done.5.refs_0_, ...), custom_call_target="tpu_custom_call", output_to_operand_aliasing={{0}: (8, {})} | custom-call | flops 335544320 | bytes 4000000 | tf_op jit(solution)/shard_map/pallas_call | solution.py:107
  58.2 0.0 copy-start.9
  58.3 0.7 copy-done.9
  59.0 3.0 %collective-permute-start.9 = (bf16[512,256]{1,0:T(8,128)(2,1)}, bf16[512,256]{1,0:T(8,128)(2,1)S(1)}, u32[]{:S(2)}, u32[]{:S(2)}) collective-permute-start(bf16[512,256]{1,0:T(8,128)(2,1)} %get-tuple-element.18), channel_id=1, source_target_pairs={{0,8},{8,0},{16,24},{24,16},{32,40},{40,32},{48,56},{56,48},{64,72... | collective-permute-start | bytes 786440 | tf_op jit(solution)/shard_map/ppermute | solution.py:31
  62.0 0.7 pad_maximum_fusion
  62.7 6.2 %all-to-all-start = ((bf16[4,144,256]{2,1,0:T(8,128)(2,1)}), bf16[4,144,256]{2,1,0:T(8,128)(2,1)S(1)}, u32[]{:S(2)}, u32[]{:S(2)}) async-start(bf16[4,144,256]{2,1,0:T(8,128)(2,1)} %pad_maximum_fusion), calls=%async_computation | async-start | bytes 589824 | tf_op jit(solution)/shard_map/all_to_all | solution.py:40
  69.0 0.0 collective-permute-done.9
  69.0 1.7 %add_convert_fusion = bf16[512,256]{1,0:T(8,128)(2,1)} fusion(bf16[512,256]{1,0:T(8,128)(2,1)S(1)} %collective-permute-done.9, bf16[512,256]{1,0:T(8,128)(2,1)} %copy-done.9), kind=kLoop, calls=%fused_computation.5 | loop fusion | flops 524288 | bytes 786432 | tf_op jit(solution)/shard_map/convert_element_type | solution.py:214
  70.7 6.8 %all-to-all-done = bf16[4,144,256]{2,1,0:T(8,128)(2,1)S(1)} async-done(((bf16[4,144,256]{2,1,0:T(8,128)(2,1)}), bf16[4,144,256]{2,1,0:T(8,128)(2,1)S(1)}, u32[]{:S(2)}, u32[]{:S(2)}) %all-to-all-start) | async-done | bytes 294944 | tf_op jit(solution)/shard_map/all_to_all | solution.py:40
  77.5 3.4 %all-to-all-start.2 = ((bf16[4,128,256]{2,1,0:T(8,128)(2,1)}), bf16[4,128,256]{2,1,0:T(8,128)(2,1)S(1)}, u32[]{:S(2)}, u32[]{:S(2)}) async-start(bf16[4,128,256]{2,1,0:T(8,128)(2,1)} %bitcast.14), calls=%async_computation.2 | async-start | bytes 524288 | tf_op jit(solution)/shard_map/all_to_all | solution.py:40
  80.9 0.5 slice.20
  82.1 4.4 %all-to-all-done.2 = bf16[4,128,256]{2,1,0:T(8,128)(2,1)S(1)} async-done(((bf16[4,128,256]{2,1,0:T(8,128)(2,1)}), bf16[4,128,256]{2,1,0:T(8,128)(2,1)S(1)}, u32[]{:S(2)}, u32[]{:S(2)}) %all-to-all-start.2) | async-done | bytes 262176 | tf_op jit(solution)/shard_map/all_to_all | solution.py:40
  86.5 0.7 broadcast_in_dim.11
  87.3 4.8 %all-to-all-start.1 = ((bf16[4,128,256]{2,1,0:T(8,128)(2,1)}), bf16[4,128,256]{2,1,0:T(8,128)(2,1)S(1)}, u32[]{:S(2)}, u32[]{:S(2)}) async-start(bf16[4,128,256]{2,1,0:T(8,128)(2,1)} %broadcast_in_dim.11), calls=%async_computation.1 | async-start | bytes 524288 | tf_op jit(solution)/shard_map/all_to_all | solution.py:40
  92.1 5.6 %all-to-all-done.1 = bf16[4,128,256]{2,1,0:T(8,128)(2,1)S(1)} async-done(((bf16[4,128,256]{2,1,0:T(8,128)(2,1)}), bf16[4,128,256]{2,1,0:T(8,128)(2,1)S(1)}, u32[]{:S(2)}, u32[]{:S(2)}) %all-to-all-start.1) | async-done | bytes 262176 | tf_op jit(solution)/shard_map/all_to_all | solution.py:40
  97.7 0.7 broadcast_in_dim.12
  98.4 3.4 %all-to-all-start.3 = ((bf16[4,128,256]{2,1,0:T(8,128)(2,1)}), bf16[4,128,256]{2,1,0:T(8,128)(2,1)S(1)}, u32[]{:S(2)}, u32[]{:S(2)}) async-start(bf16[4,128,256]{2,1,0:T(8,128)(2,1)} %broadcast_in_dim.12), calls=%async_computation.3 | async-start | bytes 524288 | tf_op jit(solution)/shard_map/all_to_all | solution.py:40
  101.8 2.5 %multiply_convert_fusion = bf16[640,2048]{1,0:T(8,128)(2,1)} fusion(bf16[640,256]{1,0:T(8,128)(2,1)S(1)} %copy-done.5, bf16[1,2048,256]{2,1,0:T(8,128)(2,1)S(1)} %copy-done.1), kind=kOutput, calls=%fused_computation | convolution fusion | flops 673710080 | bytes 3997696 | tf_op jit(solution)/shard_map/dot_general | solution.py:194
  104.2 3.1 %all-to-all-done.3 = bf16[4,128,256]{2,1,0:T(8,128)(2,1)S(1)} async-done(((bf16[4,128,256]{2,1,0:T(8,128)(2,1)}), bf16[4,128,256]{2,1,0:T(8,128)(2,1)S(1)}, u32[]{:S(2)}, u32[]{:S(2)}) %all-to-all-start.3) | async-done | bytes 262176 | tf_op jit(solution)/shard_map/all_to_all | solution.py:40
  107.4 4.4 %all-to-all-start.4 = ((bf16[8,80,2048]{2,1,0:T(8,128)(2,1)}), bf16[8,80,2048]{2,1,0:T(8,128)(2,1)}, u32[]{:S(2)}, u32[]{:S(2)}) async-start(bf16[8,80,2048]{2,1,0:T(8,128)(2,1)} %bitcast.30), calls=%async_computation.4 | async-start | bytes 5242880 | tf_op jit(solution)/shard_map/all_to_all | solution.py:230
  111.8 7.2 %collective-permute-start.4 = (bf16[512,256]{1,0:T(8,128)(2,1)S(1)}, bf16[512,256]{1,0:T(8,128)(2,1)S(1)}, u32[]{:S(2)}, u32[]{:S(2)}) collective-permute-start(bf16[512,256]{1,0:T(8,128)(2,1)S(1)} %bitcast.26), channel_id=1, source_target_pairs={{0,8},{8,0},{16,24},{24,16},{32,40},{40,32},{48,56},{56,48},{64,72... | collective-permute-start | bytes 786440 | tf_op jit(solution)/shard_map/ppermute | solution.py:31
  119.0 1.9 %collective-permute-start.10 = (bf16[512,256]{1,0:T(8,128)(2,1)S(1)}, bf16[512,256]{1,0:T(8,128)(2,1)S(1)}, u32[]{:S(2)}, u32[]{:S(2)}) collective-permute-start(bf16[512,256]{1,0:T(8,128)(2,1)S(1)} %bitcast.28), channel_id=1, source_target_pairs={{0,8},{8,0},{16,24},{24,16},{32,40},{40,32},{48,56},{56,48},{64,72... | collective-permute-start | bytes 786440 | tf_op jit(solution)/shard_map/ppermute | solution.py:31
  120.9 0.1 concatenate.16.info
  121.0 0.0 collective-permute-done.4.refs_2_
  121.0 1.4 collective-permute-done.10.refs_5_
  122.4 1.6 %shard_map.78 = bf16[2048,256]{1,0:T(8,128)(2,1)} custom-call(s32[10]{0:T(128)S(1)} %concatenate.16.info, bf16[4,256,256]{2,1,0:T(8,128)(2,1)S(1)} %get-tuple-element.12.refs_0_, bf16[512,256]{1,0:T(8,128)(2,1)S(1)} %bitcast.27, bf16[512,256]{1,0:T(8,128)(2,1)S(1)} %collective-permute-done.4.refs_2_, bf16[4,256,256]{2,1,0:T(8,128)(2,1)S(1)} %get-tuple-element.16.refs_3_, ...), custom_call_target="tpu_custom_call" | custom-call | bytes 2000000 | tf_op jit(solution)/shard_map/pallas_call | solution.py:163
  124.0 18.5 %all-to-all-done.4 = bf16[8,80,2048]{2,1,0:T(8,128)(2,1)} async-done(((bf16[8,80,2048]{2,1,0:T(8,128)(2,1)}), bf16[8,80,2048]{2,1,0:T(8,128)(2,1)}, u32[]{:S(2)}, u32[]{:S(2)}) %all-to-all-start.4) | async-done | bytes 2621472 | tf_op jit(solution)/shard_map/all_to_all | solution.py:230
  142.5 3.0 %reduce_sum.32 = bf16[80,2048]{1,0:T(8,128)(2,1)} reduce(bf16[8,80,2048]{2,1,0:T(8,128)(2,1)} %all-to-all-done.4, bf16[]{:T(256)} %constant.33.clone.1), dimensions={0}, to_apply=%region_2.0 | reduce | flops 1146880 | bytes 2949122 | tf_op jit(solution)/shard_map/reduce_sum | solution.py:233
  (9 shorter events, 0.1 us)
Async XLA Ops:
  0.6 10.4 %collective-permute-start.2 = (bf16[640,256]{1,0:T(8,128)(2,1)}, bf16[640,256]{1,0:T(8,128)(2,1)}, u32[]{:S(2)}, u32[]{:S(2)}) collective-permute-start(bf16[640,256]{1,0:T(8,128)(2,1)} %refs_0_.1), channel_id=1, source_target_pairs={{0,3},{1,2},{2,1},{3,0},{4,7},{5,6},{6,5},{7,4},{8,11},{9,10},{10,... | collective-permute-start | bytes 983048 | tf_op jit(solution)/shard_map/ppermute | solution.py:27
  5.9 10.2 %collective-permute-start.1 = (bf16[640,256]{1,0:T(8,128)(2,1)}, bf16[640,256]{1,0:T(8,128)(2,1)}, u32[]{:S(2)}, u32[]{:S(2)}) collective-permute-start(bf16[640,256]{1,0:T(8,128)(2,1)} %refs_0_.1), channel_id=1, source_target_pairs={{0,1},{1,0},{2,3},{3,2},{4,5},{5,4},{6,7},{7,6},{8,9},{9,8},{10,11... | collective-permute-start | bytes 983048 | tf_op jit(solution)/shard_map/ppermute | solution.py:27
  7.8 8.5 %collective-permute-start = (bf16[640,256]{1,0:T(8,128)(2,1)}, bf16[640,256]{1,0:T(8,128)(2,1)}, u32[]{:S(2)}, u32[]{:S(2)}) collective-permute-start(bf16[640,256]{1,0:T(8,128)(2,1)} %refs_0_.1), channel_id=1, source_target_pairs={{0,4},{1,5},{2,6},{3,7},{4,0},{5,1},{6,2},{7,3},{8,12},{9,13},{10,... | collective-permute-start | bytes 983048 | tf_op jit(solution)/shard_map/ppermute | solution.py:27
  11.0 29.4 %collective-permute-start.7 = (bf16[640,256]{1,0:T(8,128)(2,1)}, bf16[640,256]{1,0:T(8,128)(2,1)S(1)}, u32[]{:S(2)}, u32[]{:S(2)}) collective-permute-start(bf16[640,256]{1,0:T(8,128)(2,1)} %collective-permute-done.2.refs_3_), channel_id=1, source_target_pairs={{0,1},{1,0},{2,3},{3,2},{4,5},{5,4},{6,7},{7,6},{8,9},{9,8},{10,11... | collective-permute-start | bytes 983048 | tf_op jit(solution)/shard_map/ppermute | solution.py:27
  16.3 1.2 copy-start
  17.5 1.2 copy-start.2
  18.7 1.0 copy-start.4
  19.7 1.0 copy-start.8
  20.7 30.7 %copy-start.1 = (bf16[1,2048,256]{2,1,0:T(8,128)(2,1)S(1)}, bf16[1,2048,256]{2,1,0:T(8,128)(2,1)}, u32[]{:S(2)}) copy-start(bf16[1,2048,256]{2,1,0:T(8,128)(2,1)} %param.7) | copy-start | bytes 3145732
  20.7 30.7 %copy-start.3 = (bf16[1,2048,256]{2,1,0:T(8,128)(2,1)S(1)}, bf16[1,2048,256]{2,1,0:T(8,128)(2,1)}, u32[]{:S(2)}) copy-start(bf16[1,2048,256]{2,1,0:T(8,128)(2,1)} %param.8) | copy-start | bytes 3145732
  20.7 30.7 %copy-start.5 = (bf16[640,256]{1,0:T(8,128)(2,1)S(1)}, bf16[640,256]{1,0:T(8,128)(2,1)}, u32[]{:S(2)}) copy-start(bf16[640,256]{1,0:T(8,128)(2,1)} %refs_4_.3) | copy-start | bytes 983044
  26.7 17.2 %collective-permute-start.3 = (bf16[528,256]{1,0:T(8,128)(2,1)}, bf16[528,256]{1,0:T(8,128)(2,1)}, u32[]{:S(2)}, u32[]{:S(2)}) collective-permute-start(bf16[528,256]{1,0:T(8,128)(2,1)} %get-tuple-element.14), channel_id=1, source_target_pairs={{0,8},{8,0},{16,24},{24,16},{32,40},{40,32},{48,56},{56,48},{64,72... | collective-permute-start | bytes 811016 | tf_op jit(solution)/shard_map/ppermute | solution.py:31
  33.0 12.0 %collective-permute-start.6 = (bf16[640,256]{1,0:T(8,128)(2,1)}, bf16[640,256]{1,0:T(8,128)(2,1)}, u32[]{:S(2)}, u32[]{:S(2)}) collective-permute-start(bf16[640,256]{1,0:T(8,128)(2,1)} %collective-permute-done.1.refs_2_), channel_id=1, source_target_pairs={{0,4},{1,5},{2,6},{3,7},{4,0},{5,1},{6,2},{7,3},{8,12},{9,13},{10,... | collective-permute-start | bytes 983048 | tf_op jit(solution)/shard_map/ppermute | solution.py:27
  35.6 12.8 %collective-permute-start.5 = (bf16[640,256]{1,0:T(8,128)(2,1)}, bf16[640,256]{1,0:T(8,128)(2,1)}, u32[]{:S(2)}, u32[]{:S(2)}) collective-permute-start(bf16[640,256]{1,0:T(8,128)(2,1)} %collective-permute-done.refs_1_), channel_id=1, source_target_pairs={{0,3},{1,2},{2,1},{3,0},{4,7},{5,6},{6,5},{7,4},{8,11},{9,10},{10,... | collective-permute-start | bytes 983048 | tf_op jit(solution)/shard_map/ppermute | solution.py:27
  40.4 11.0 %copy-start.6 = (bf16[640,256]{1,0:T(8,128)(2,1)}, bf16[640,256]{1,0:T(8,128)(2,1)S(1)}, u32[]{:S(2)}) copy-start(bf16[640,256]{1,0:T(8,128)(2,1)S(1)} %collective-permute-done.7.refs_2_) | copy-start | bytes 983044
  40.4 11.0 %collective-permute-start.8 = (bf16[640,256]{1,0:T(8,128)(2,1)S(1)}, bf16[640,256]{1,0:T(8,128)(2,1)}, u32[]{:S(2)}, u32[]{:S(2)}) collective-permute-start(bf16[640,256]{1,0:T(8,128)(2,1)S(1)} %collective-permute-done.7.refs_2_), channel_id=1, source_target_pairs={{0,4},{1,5},{2,6},{3,7},{4,0},{5,1},{6,2},{7,3},{8,12},{9,13},{10,... | collective-permute-start | bytes 983048 | tf_op jit(solution)/shard_map/ppermute | solution.py:27
  51.4 1.0 copy-start.7
  58.2 0.7 copy-start.9
  59.0 10.0 %collective-permute-start.9 = (bf16[512,256]{1,0:T(8,128)(2,1)}, bf16[512,256]{1,0:T(8,128)(2,1)S(1)}, u32[]{:S(2)}, u32[]{:S(2)}) collective-permute-start(bf16[512,256]{1,0:T(8,128)(2,1)} %get-tuple-element.18), channel_id=1, source_target_pairs={{0,8},{8,0},{16,24},{24,16},{32,40},{40,32},{48,56},{56,48},{64,72... | collective-permute-start | bytes 786440 | tf_op jit(solution)/shard_map/ppermute | solution.py:31
  62.7 14.8 %all-to-all-start = ((bf16[4,144,256]{2,1,0:T(8,128)(2,1)}), bf16[4,144,256]{2,1,0:T(8,128)(2,1)S(1)}, u32[]{:S(2)}, u32[]{:S(2)}) async-start(bf16[4,144,256]{2,1,0:T(8,128)(2,1)} %pad_maximum_fusion), calls=%async_computation | async-start | bytes 589824 | tf_op jit(solution)/shard_map/all_to_all | solution.py:40
  77.5 9.1 %all-to-all-start.2 = ((bf16[4,128,256]{2,1,0:T(8,128)(2,1)}), bf16[4,128,256]{2,1,0:T(8,128)(2,1)S(1)}, u32[]{:S(2)}, u32[]{:S(2)}) async-start(bf16[4,128,256]{2,1,0:T(8,128)(2,1)} %bitcast.14), calls=%async_computation.2 | async-start | bytes 524288 | tf_op jit(solution)/shard_map/all_to_all | solution.py:40
  87.3 10.4 %all-to-all-start.1 = ((bf16[4,128,256]{2,1,0:T(8,128)(2,1)}), bf16[4,128,256]{2,1,0:T(8,128)(2,1)S(1)}, u32[]{:S(2)}, u32[]{:S(2)}) async-start(bf16[4,128,256]{2,1,0:T(8,128)(2,1)} %broadcast_in_dim.11), calls=%async_computation.1 | async-start | bytes 524288 | tf_op jit(solution)/shard_map/all_to_all | solution.py:40
  98.4 9.0 %all-to-all-start.3 = ((bf16[4,128,256]{2,1,0:T(8,128)(2,1)}), bf16[4,128,256]{2,1,0:T(8,128)(2,1)S(1)}, u32[]{:S(2)}, u32[]{:S(2)}) async-start(bf16[4,128,256]{2,1,0:T(8,128)(2,1)} %broadcast_in_dim.12), calls=%async_computation.3 | async-start | bytes 524288 | tf_op jit(solution)/shard_map/all_to_all | solution.py:40
  107.4 35.1 %all-to-all-start.4 = ((bf16[8,80,2048]{2,1,0:T(8,128)(2,1)}), bf16[8,80,2048]{2,1,0:T(8,128)(2,1)}, u32[]{:S(2)}, u32[]{:S(2)}) async-start(bf16[8,80,2048]{2,1,0:T(8,128)(2,1)} %bitcast.30), calls=%async_computation.4 | async-start | bytes 5242880 | tf_op jit(solution)/shard_map/all_to_all | solution.py:230
  111.8 9.2 %collective-permute-start.4 = (bf16[512,256]{1,0:T(8,128)(2,1)S(1)}, bf16[512,256]{1,0:T(8,128)(2,1)S(1)}, u32[]{:S(2)}, u32[]{:S(2)}) collective-permute-start(bf16[512,256]{1,0:T(8,128)(2,1)S(1)} %bitcast.26), channel_id=1, source_target_pairs={{0,8},{8,0},{16,24},{24,16},{32,40},{40,32},{48,56},{56,48},{64,72... | collective-permute-start | bytes 786440 | tf_op jit(solution)/shard_map/ppermute | solution.py:31
  119.0 3.4 %collective-permute-start.10 = (bf16[512,256]{1,0:T(8,128)(2,1)S(1)}, bf16[512,256]{1,0:T(8,128)(2,1)S(1)}, u32[]{:S(2)}, u32[]{:S(2)}) collective-permute-start(bf16[512,256]{1,0:T(8,128)(2,1)S(1)} %bitcast.28), channel_id=1, source_target_pairs={{0,8},{8,0},{16,24},{24,16},{32,40},{40,32},{48,56},{56,48},{64,72... | collective-permute-start | bytes 786440 | tf_op jit(solution)/shard_map/ppermute | solution.py:31

commit v2 on v1

v2 whole, which is shorter than its diff:
```python
import functools
import math

import jax
import jax.numpy as jnp
from jax import lax
from jax.experimental import pallas as pl
from jax.experimental.pallas import tpu as pltpu
from jax.sharding import PartitionSpec as P

GROUP = 8
step_size = 0.25
decay_factor = 0.9
bf16 = jnp.bfloat16
f32 = jnp.float32

EARLY = (0, 4, 1, 3)
LATE = (5, 2, 7, 6)
PAD = 16
VMEM = pl.BlockSpec(memory_space=pltpu.VMEM)
ANY = pl.BlockSpec(memory_space=pl.ANY)
SMEM = pl.BlockSpec(memory_space=pltpu.SMEM)
PARAMS = pltpu.CompilerParams(vmem_limit_bytes=56 * 1024 * 1024)
CHEAP = pl.CostEstimate(flops=1000, bytes_accessed=1000, transcendentals=0)


def tensor_swap(value, k):
    return lax.ppermute(value, "tensor", [(t, t ^ k) for t in range(lax.axis_size("tensor"))])


def core_swap(value):
    return lax.ppermute(value, "dp", [(r, r ^ 1) for r in range(lax.axis_size("dp"))])


def chip_swap(value, k):
    return lax.ppermute(value, "dp", [(r, r ^ (2 * k)) for r in range(lax.axis_size("dp"))])


def after(value, *earlier):
    return lax.optimization_barrier((value, *earlier))[0]


def update_kernel(scale, first, info, *refs):
    n = 4
    acts, (cot, weight, mom) = refs[:n], refs[n : n + 3]
    mom_out, keep, send, own = refs[n + 3 : n + 7] if first else refs[n + 6 : n + 10]
    a_buf, c_buf, w_buf, m_buf, o_buf, n_buf, p_buf, f_buf, sems = refs[-9:]
    size = w_buf.shape[1]
    width = w_buf.shape[2]
    core, chip, alive = info[n], info[n + 1], info[n + 2]

    def rows(b):
        return pl.ds(pl.multiple_of(info[b] * size, size), size)

    def loads(b):
        return (
            pltpu.make_async_copy(acts[b], a_buf.at[b], sems.at[0, b]),
            pltpu.make_async_copy(weight.at[rows(b)], w_buf.at[b], sems.at[1, b]),
            pltpu.make_async_copy(mom.at[rows(b)], m_buf.at[b], sems.at[2, b]),
        )

    def stores(b):
        return (
            pltpu.make_async_copy(o_buf.at[b], mom_out.at[rows(b)], sems.at[3, b]),
            pltpu.make_async_copy(n_buf.at[b], own.at[b], sems.at[4, b]),
        )

    def hand_over(b, target):
        place = (b % 2 + (0 if first else 2)) ^ chip
        return pltpu.make_async_copy(
            p_buf.at[b], target.at[place, pl.ds(0, size)], sems.at[5, b]
        )

    def flags(k):
        return tuple(
            pltpu.make_async_copy(f_buf, target.at[k, pl.ds(size, PAD)], sems.at[6 + i, k])
            for i, target in enumerate((keep, send))
        )

    load_cot = pltpu.make_async_copy(cot, c_buf, sems.at[8, 0])
    load_cot.start()
    for b in range(n):
        for copy in loads(b):
            copy.start()
    flag = jnp.where(alive > 0, 1.0, 0.0).astype(f32)
    if first:
        f_buf[...] = jnp.full((PAD, width), flag, f32).astype(bf16)
        for k in range(4):
            for copy in flags(k):
                copy.start()
    load_cot.wait()
    for b in range(n):
        for copy in loads(b):
            copy.wait()
        grad = lax.dot_general(
            a_buf[b], c_buf[...], (((0,), (0,)), ((), ())), preferred_element_type=f32
        )
        moment = decay_factor * m_buf[b].astype(f32) + grad * scale
        o_buf[b] = moment.astype(bf16)
        new = w_buf[b].astype(f32) - step_size * moment
        n_buf[b] = new.astype(bf16)
        p_buf[b] = (new * flag).astype(bf16)
        for copy in stores(b):
            copy.start()

        @pl.when(core == b // 2)
        def _():
            hand_over(b, keep).start()

        @pl.when(core != b // 2)
        def _():
            hand_over(b, send).start()

    for b in range(n):
        for copy in stores(b):
            copy.wait()
        hand_over(b, keep).wait()
    if first:
        for k in range(4):
            for copy in flags(k):
                copy.wait()


def update(scale, info, acts, cot, weight, mom, done=()):
    first = not done
    rows, size = acts[0].shape
    width = cot.shape[1]
    block = pltpu.VMEM((4, size, width), bf16)
    return pl.pallas_call(
        functools.partial(update_kernel, scale, first),
        out_shape=(
            jax.ShapeDtypeStruct(weight.shape, bf16),
            jax.ShapeDtypeStruct((4, size + PAD, width), bf16),
            jax.ShapeDtypeStruct((4, size + PAD, width), bf16),
            jax.ShapeDtypeStruct((4, size, width), bf16),
        ),
        in_specs=[SMEM] + [ANY] * (7 + len(done)),
        out_specs=(ANY, ANY, ANY, ANY),
        scratch_shapes=[
            pltpu.VMEM((4, rows, size), bf16),
            pltpu.VMEM((rows, width), bf16),
            block,
            block,
            block,
            block,
            block,
            pltpu.VMEM((PAD, width), bf16),
            pltpu.SemaphoreType.DMA((9, 4)),
        ],
        input_output_aliases={} if first else {8: 0, 9: 1, 10: 2},
        compiler_params=PARAMS,
        cost_estimate=CHEAP,
    )(info, *acts, cot, weight, mom, *done)


def partial_kernel(scale, cot, weight, out, c_buf, w_buf, buf, sems):
    tiles = 4
    size = weight.shape[0] // tiles

    def load(n):
        at = pl.ds(n * size, size)
        return pltpu.make_async_copy(weight.at[at], w_buf.at[at], sems.at[n])

    def store(n):
        return pltpu.make_async_copy(buf.at[n], out.at[:, pl.ds(n * size, size)], sems.at[tiles + n])

    load_cot = pltpu.make_async_copy(cot, c_buf, sems.at[2 * tiles])
    load_cot.start()
    for n in range(tiles):
        load(n).start()
    load_cot.wait()
    for n in range(tiles):
        load(n).wait()
        value = lax.dot_general(
            c_buf[...],
            w_buf[n * size : (n + 1) * size, :],
            (((1,), (1,)), ((), ())),
            preferred_element_type=f32,
        )
        buf[n] = (value * scale).astype(bf16)
        store(n).start()
    for n in range(tiles):
        store(n).wait()


def partials(scale, cot, weight):
    rows, features = cot.shape[0], weight.shape[0]
    return pl.pallas_call(
        functools.partial(partial_kernel, scale),
        out_shape=jax.ShapeDtypeStruct((rows, features), bf16),
        in_specs=[ANY, ANY],
        out_specs=ANY,
        scratch_shapes=[
            pltpu.VMEM(cot.shape, bf16),
            pltpu.VMEM(weight.shape, bf16),
            pltpu.VMEM((4, rows, features // 4), bf16),
            pltpu.SemaphoreType.DMA((9,)),
        ],
        compiler_params=PARAMS,
        cost_estimate=CHEAP,
    )(cot, weight)


def place_kernel(info, own_1, own_2, mine, other, out, sems):
    size = mine.shape[1]
    core, chip, alive = info[8], info[9], info[10]

    def copy(source, b):
        at = pl.ds(pl.multiple_of(info[b] * size, size), size)
        return pltpu.make_async_copy(source, out.at[at], sems.at[b])

    for b in range(8):
        own = own_1 if b < 4 else own_2
        slot = (b % 2 + 2 * (b // 4)) ^ chip
        is_mine = core == (b % 4) // 2

        @pl.when(alive <= 0)
        def _():
            copy(own.at[b % 4], b).start()

        @pl.when((alive > 0) & is_mine)
        def _():
            copy(mine.at[slot], b).start()

        @pl.when((alive > 0) & jnp.logical_not(is_mine))
        def _():
            copy(other.at[slot], b).start()

    for b in range(8):
        copy(mine.at[0], b).wait()


def place(info, parts, shape):
    return pl.pallas_call(
        place_kernel,
        out_shape=jax.ShapeDtypeStruct(shape, bf16),
        in_specs=[SMEM] + [VMEM] * 4,
        out_specs=ANY,
        scratch_shapes=[pltpu.SemaphoreType.DMA((8,))],
        compiler_params=PARAMS,
        cost_estimate=CHEAP,
    )(info, *parts)


def body(activations, cotangent, kv_weight, momentum, alive_mask):
    weight, mom = kv_weight[0], momentum[0]
    features, width = weight.shape
    scale = 1.0 / math.sqrt(features)
    t = lax.axis_index("tensor")
    core = lax.rem(lax.axis_index("dp"), 2)
    alive = alive_mask[0]
    chip = lax.rem(lax.axis_index("dp") // 2, GROUP // 2)
    tail = jnp.stack([core, chip, alive])
    early = jnp.stack([t ^ k for k in EARLY])
    late = jnp.stack([t ^ k for k in LATE])

    a_y = tensor_swap(activations, 4)
    a_p = tensor_swap(activations, 1)
    a_q = tensor_swap(activations, 3)
    share = partials(scale, cotangent, weight)
    a_y, a_p, a_q, share = lax.optimization_barrier((a_y, a_p, a_q, share))

    a_yp = tensor_swap(a_p, 4)
    a_pq = tensor_swap(a_q, 1)
    a_qy = tensor_swap(a_y, 3)
    a_ypq = tensor_swap(after(activations, a_q), 6)
    *done, own_1 = update(
        scale,
        jnp.concatenate([early, tail]),
        (activations, a_y, a_p, a_q),
        cotangent,
        weight,
        mom,
    )
    a_yp, a_pq, a_qy, a_ypq, share, *done = lax.optimization_barrier(
        (a_yp, a_pq, a_qy, a_ypq, share, *done)
    )
    new_momentum, keep, send, own_2 = update(
        scale, jnp.concatenate([late, tail]), (a_yp, a_pq, a_qy, a_ypq), cotangent, weight, mom, done
    )

    members = lax.axis_size("tensor")
    share = after(share, send)
    shares = lax.all_to_all(
        share.reshape(members, share.shape[0] // members, features), "tensor", 0, 0, tiled=True
    )

    arrived = core_swap(send)
    sums = [(keep[k].astype(f32) + arrived[k].astype(f32)).astype(bf16) for k in range(4)]
    size = sums[0].shape[0] - PAD
    got = sums[0].astype(f32)
    for k in (1, 2, 3):
        got = got + chip_swap(sums[k], k).astype(f32)
    count = jnp.maximum(got[size : size + 1], 1.0)
    mean = (got[:size] / count).astype(bf16)
    mine = jnp.stack([mean] + [chip_swap(mean, k) for k in (1, 2, 3)])
    other = core_swap(mine)
    new_weight = place(jnp.concatenate([early, late, tail]), (own_1, own_2, mine, other), weight.shape)
    input_grad = shares.astype(f32).sum(0).astype(bf16)
    return new_weight[None], new_momentum[None], input_grad


def solution(mesh):
    return jax.shard_map(
        body,
        mesh=mesh,
        in_specs=(
            P("dp", "tensor"),
            P("dp", "tensor"),
            P("dp", None, "tensor"),
            P("dp", None, "tensor"),
            P("dp"),
        ),
        out_specs=(P("dp", None, "tensor"), P("dp", None, "tensor"), P(("dp", "tensor"), None)),
        check_vma=False,
    )
```

time: 148 us -> 102 us (0.69)
  waiting for transfers between devices: 46.5 us -> 21.2 us
  starting transfers between devices: 66.1 us -> 59 us
  local copies, waits for them, and re-layouts: 8.32 us -> 2.66 us
  other arithmetic: 6.6 us -> 1.58 us
  matrix products: 2.45 us -> 0 us
  Pallas kernels: 13.4 us -> 14.9 us
    all_to_all x5 -> x1, waiting for transfers between devices: 38.4 us -> 0.01 us  [body(): lax.all_to_all(share.reshape(members, share.shape[0] // members, features...]
    all_to_all x5 -> x1, starting transfers between devices: 22.2 us -> 4.13 us  [body(): lax.all_to_all(share.reshape(members, share.shape[0] // members, features...]
    ppermute x0 -> x6, starting transfers between devices: none -> 17.9 us  [chip_swap(): lax.ppermute(value, 'dp', [(r, r ^ 2 * k) for r in range(lax.axis_size('d...]
    ppermute x0 -> x6, waiting for transfers between devices: none -> 15.3 us  [chip_swap(): lax.ppermute(value, 'dp', [(r, r ^ 2 * k) for r in range(lax.axis_size('d...]
    unnamed x20, local copies, waits for them, and re-layouts: 6.08 us -> 0.75 us
    ppermute x4 -> x2, starting transfers between devices: 18.4 us -> 13.4 us  [core_swap(): lax.ppermute(value, 'dp', [(r, r ^ 1) for r in range(lax.axis_size('dp'))])]
    ppermute x7, waiting for transfers between devices: 6.66 us -> 3.11 us  [tensor_swap(): lax.ppermute(value, 'tensor', [(t, t ^ k) for t in range(lax.axis_size('t...]
    pallas_call x0 -> x1, Pallas kernels: none -> 3.47 us  [partials(): pl.pallas_call(functools.partial(partial_kernel, scale), out_shape=jax.Sh...]
  transfers between devices with their start and end apart: 16 -> 16, of which waited for: 9 -> 10; matrix products, arithmetic and copies ran while one was open for 5% -> 2% of each run, Pallas kernels for 5% -> 10%
where the time goes in v2:
time: 102 us; the launch traced here: 101 us
  starting transfers between devices  59 us (58%)
  waiting for transfers between devices  21.2 us (21%)
  Pallas kernels  14.9 us (15%)
  local copies, waits for them, and re-layouts  2.66 us (3%)
  between operations  1.6 us (2%)
  other arithmetic  1.58 us (2%)
    ppermute x7, starting transfers between devices, tensor_swap(): lax.ppermute(value, 'tensor', [(t, t ^ k) for t in range(lax.axis_size('t...  23.5 us
    ppermute x6, starting transfers between devices, chip_swap(): lax.ppermute(value, 'dp', [(r, r ^ 2 * k) for r in range(lax.axis_size('d...  17.9 us
    ppermute x6, waiting for transfers between devices, chip_swap(): lax.ppermute(value, 'dp', [(r, r ^ 2 * k) for r in range(lax.axis_size('d...  15.3 us
    ppermute x2, starting transfers between devices, core_swap(): lax.ppermute(value, 'dp', [(r, r ^ 1) for r in range(lax.axis_size('dp'))])  13.4 us
    pallas_call x2, Pallas kernels, update(): pl.pallas_call(functools.partial(update_kernel, scale, first), out_shape=...  8.86 us
    all_to_all x1, starting transfers between devices, body(): lax.all_to_all(share.reshape(members, share.shape[0] // members, features...  4.13 us
    pallas_call x1, Pallas kernels, partials(): pl.pallas_call(functools.partial(partial_kernel, scale), out_shape=jax.Sh...  3.47 us
    ppermute x7, waiting for transfers between devices, tensor_swap(): lax.ppermute(value, 'tensor', [(t, t ^ k) for t in range(lax.axis_size('t...  3.11 us
  transfers between devices with their start and end apart: 16, of which 10 were waited for; matrix products, arithmetic and copies ran while one was open for 2% of the time, Pallas kernels for 10%

profile of v2, /device:TPU:1, one launch (start us, length us, event | category | flops | bytes accessed | tf_op | source)
XLA Modules:
  0.0 100.9 jit_solution(11976701420292892102)
XLA Ops:
  0.6 0.0 copy-start.6
  0.6 5.3 %collective-permute-start.2 = (bf16[640,256]{1,0:T(8,128)(2,1)}, bf16[640,256]{1,0:T(8,128)(2,1)S(1)}, u32[]{:S(2)}, u32[]{:S(2)}) collective-permute-start(bf16[640,256]{1,0:T(8,128)(2,1)} %refs_0_.1), channel_id=1, source_target_pairs={{0,3},{1,2},{2,1},{3,0},{4,7},{5,6},{6,5},{7,4},{8,11},{9,10},{10,... | collective-permute-start | bytes 983048 | tf_op jit(solution)/shard_map/ppermute | solution.py:28
  6.0 1.9 %collective-permute-start.1 = (bf16[640,256]{1,0:T(8,128)(2,1)}, bf16[640,256]{1,0:T(8,128)(2,1)S(1)}, u32[]{:S(2)}, u32[]{:S(2)}) collective-permute-start(bf16[640,256]{1,0:T(8,128)(2,1)} %refs_0_.1), channel_id=1, source_target_pairs={{0,1},{1,0},{2,3},{3,2},{4,5},{5,4},{6,7},{7,6},{8,9},{9,8},{10,11... | collective-permute-start | bytes 983048 | tf_op jit(solution)/shard_map/ppermute | solution.py:28
  7.9 3.2 %collective-permute-start = (bf16[640,256]{1,0:T(8,128)(2,1)}, bf16[640,256]{1,0:T(8,128)(2,1)S(1)}, u32[]{:S(2)}, u32[]{:S(2)}) collective-permute-start(bf16[640,256]{1,0:T(8,128)(2,1)} %refs_0_.1), channel_id=1, source_target_pairs={{0,4},{1,5},{2,6},{3,7},{4,0},{5,1},{6,2},{7,3},{8,12},{9,13},{10,... | collective-permute-start | bytes 983048 | tf_op jit(solution)/shard_map/ppermute | solution.py:28
  11.1 3.5 %shard_map.76 = bf16[640,2048]{1,0:T(8,128)(2,1)} custom-call(bf16[640,256]{1,0:T(8,128)(2,1)} %refs_4_.3, bf16[2048,256]{1,0:T(8,128)(2,1)} %bitcast.32), custom_call_target="tpu_custom_call" | custom-call | flops 1000 | bytes 1000 | tf_op jit(solution)/shard_map/pallas_call | solution.py:188
  14.6 0.0 collective-permute-done.2.refs_3_
  14.6 0.0 copy-start.7
  14.6 0.0 collective-permute-done.1.refs_2_
  14.7 0.0 copy-start.8
  14.7 1.8 %collective-permute-done.refs_1_ = bf16[640,256]{1,0:T(8,128)(2,1)S(1)} collective-permute-done((bf16[640,256]{1,0:T(8,128)(2,1)}, bf16[640,256]{1,0:T(8,128)(2,1)S(1)}, u32[]{:S(2)}, u32[]{:S(2)}) %collective-permute-start) | collective-permute-done | bytes 327712 | tf_op jit(solution)/shard_map/ppermute | solution.py:28
  16.4 0.0 copy-done.6
  16.4 0.0 copy-start.9
  16.4 4.1 %collective-permute-start.6 = (bf16[640,256]{1,0:T(8,128)(2,1)S(1)}, bf16[640,256]{1,0:T(8,128)(2,1)S(1)}, u32[]{:S(2)}, u32[]{:S(2)}) collective-permute-start(bf16[640,256]{1,0:T(8,128)(2,1)S(1)} %copy-done.6), channel_id=1, source_target_pairs={{0,6},{1,7},{2,4},{3,5},{4,2},{5,3},{6,0},{7,1},{8,14},{9,15},{10,... | collective-permute-start | bytes 983048 | tf_op jit(solution)/shard_map/ppermute | solution.py:28
  20.5 5.1 %collective-permute-start.5 = (bf16[640,256]{1,0:T(8,128)(2,1)S(1)}, bf16[640,256]{1,0:T(8,128)(2,1)S(1)}, u32[]{:S(2)}, u32[]{:S(2)}) collective-permute-start(bf16[640,256]{1,0:T(8,128)(2,1)S(1)} %collective-permute-done.refs_1_), channel_id=1, source_target_pairs={{0,3},{1,2},{2,1},{3,0},{4,7},{5,6},{6,5},{7,4},{8,11},{9,10},{10,... | collective-permute-start | bytes 983048 | tf_op jit(solution)/shard_map/ppermute | solution.py:28
  25.6 1.9 %collective-permute-start.3 = (bf16[640,256]{1,0:T(8,128)(2,1)S(1)}, bf16[640,256]{1,0:T(8,128)(2,1)S(1)}, u32[]{:S(2)}, u32[]{:S(2)}) collective-permute-start(bf16[640,256]{1,0:T(8,128)(2,1)S(1)} %collective-permute-done.1.refs_2_), channel_id=1, source_target_pairs={{0,4},{1,5},{2,6},{3,7},{4,0},{5,1},{6,2},{7,3},{8,12},{9,13},{10,... | collective-permute-start | bytes 983048 | tf_op jit(solution)/shard_map/ppermute | solution.py:28
  27.6 1.9 %collective-permute-start.4 = (bf16[640,256]{1,0:T(8,128)(2,1)S(1)}, bf16[640,256]{1,0:T(8,128)(2,1)S(1)}, u32[]{:S(2)}, u32[]{:S(2)}) collective-permute-start(bf16[640,256]{1,0:T(8,128)(2,1)S(1)} %collective-permute-done.2.refs_3_), channel_id=1, source_target_pairs={{0,1},{1,0},{2,3},{3,2},{4,5},{5,4},{6,7},{7,6},{8,9},{9,8},{10,11... | collective-permute-start | bytes 983048 | tf_op jit(solution)/shard_map/ppermute | solution.py:28
  30.2 0.7 concatenate.14.info
  30.8 0.6 concatenate.13.info
  31.5 0.0 copy-done.7
  31.5 0.0 copy-done.8
  31.5 0.0 copy-done.9
  31.5 4.4 %shard_map.77 = (bf16[2048,256]{1,0:T(8,128)(2,1)}, bf16[4,272,256]{2,1,0:T(8,128)(2,1)}, bf16[4,272,256]{2,1,0:T(8,128)(2,1)}, bf16[4,256,256]{2,1,0:T(8,128)(2,1)}) custom-call(s32[7]{0:T(128)} %concatenate.13.info, bf16[640,256]{1,0:T(8,128)(2,1)} %refs_0_.1, bf16[640,256]{1,0:T(8,128)(2,1)} %copy-done.9, bf16[640,256]{1,0:T(8,128)(2,1)} %copy-done.8, ...), custom_call_target="tpu_custom_call" | custom-call | flops 1000 | bytes 1000 | tf_op jit(solution)/shard_map/pallas_call | solution.py:129
  35.9 0.0 collective-permute-done.6.refs_3_
  35.9 0.0 copy-start.2
  35.9 0.0 collective-permute-done.5.refs_2_
  35.9 0.0 copy-start.3
  36.0 0.8 collective-permute-done.3.refs_0_
  36.8 0.0 copy-start.4
  36.8 0.5 collective-permute-done.4.refs_1_
  37.3 0.0 copy-start.5
  37.3 0.0 copy-done.2
  37.3 0.0 copy-done.3
  37.3 0.2 copy-done.4
  37.5 0.5 copy-done.5
  38.0 4.4 %shard_map.78 = (bf16[2048,256]{1,0:T(8,128)(2,1)}, bf16[4,272,256]{2,1,0:T(8,128)(2,1)}, bf16[4,272,256]{2,1,0:T(8,128)(2,1)}, bf16[4,256,256]{2,1,0:T(8,128)(2,1)}) custom-call(s32[7]{0:T(128)} %concatenate.14.info, bf16[640,256]{1,0:T(8,128)(2,1)} %copy-done.4, ...), custom_call_target="tpu_custom_call", output_to_operand_aliasing={{0}: (8, {}), {1}: (9, {}), {2}: (10, {})} | custom-call | flops 1000 | bytes 1000 | tf_op jit(solution)/shard_map/pallas_call | solution.py:129
  42.4 0.0 copy-start
  42.5 4.1 %all-to-all-start = ((bf16[8,80,2048]{2,1,0:T(8,128)(2,1)}), bf16[8,80,2048]{2,1,0:T(8,128)(2,1)S(1)}, u32[]{:S(2)}, u32[]{:S(2)}) async-start(bf16[8,80,2048]{2,1,0:T(8,128)(2,1)} %bitcast.23), calls=%async_computation | async-start | bytes 5242880 | tf_op jit(solution)/shard_map/all_to_all | solution.py:284
  46.6 8.7 %collective-permute-start.7 = (bf16[4,272,256]{2,1,0:T(8,128)(2,1)}, bf16[4,272,256]{2,1,0:T(8,128)(2,1)S(1)}, u32[]{:S(2)}, u32[]{:S(2)}) collective-permute-start(bf16[4,272,256]{2,1,0:T(8,128)(2,1)} %get-tuple-element.43), channel_id=1, source_target_pairs={{0,8},{8,0},{16,24},{24,16},{32,40},{40,32},{48,56},{56,48},{64,72... | collective-permute-start | bytes 1671176 | tf_op jit(solution)/shard_map/ppermute | solution.py:32
  55.3 1.8 %collective-permute-done.7 = bf16[4,272,256]{2,1,0:T(8,128)(2,1)S(1)} collective-permute-done((bf16[4,272,256]{2,1,0:T(8,128)(2,1)}, bf16[4,272,256]{2,1,0:T(8,128)(2,1)S(1)}, u32[]{:S(2)}, u32[]{:S(2)}) %collective-permute-start.7) | collective-permute-done | bytes 557088 | tf_op jit(solution)/shard_map/ppermute | solution.py:32
  57.1 0.0 copy-done
  57.1 0.1 fusion.4
  57.2 1.9 %collective-permute-start.8 = (bf16[272,256]{1,0:T(8,128)(2,1)S(1)}, bf16[272,256]{1,0:T(8,128)(2,1)S(1)}, u32[]{:S(2)}, u32[]{:S(2)}) collective-permute-start(bf16[272,256]{1,0:T(8,128)(2,1)S(1)} %get-tuple-element.47), channel_id=1, source_target_pairs={{0,16},{8,24},{16,0},{24,8},{32,48},{40,56},{48,32},{56,40},{64,80... | collective-permute-start | bytes 417800 | tf_op jit(solution)/shard_map/ppermute | solution.py:36
  59.1 4.5 %collective-permute-start.10 = (bf16[272,256]{1,0:T(8,128)(2,1)S(1)}, bf16[272,256]{1,0:T(8,128)(2,1)S(1)}, u32[]{:S(2)}, u32[]{:S(2)}) collective-permute-start(bf16[272,256]{1,0:T(8,128)(2,1)S(1)} %get-tuple-element.48), channel_id=1, source_target_pairs={{0,48},{8,56},{16,32},{24,40},{32,16},{40,24},{48,0},{56,8},{64,11... | collective-permute-start | bytes 417800 | tf_op jit(solution)/shard_map/ppermute | solution.py:36
  63.7 2.2 %collective-permute-start.9 = (bf16[272,256]{1,0:T(8,128)(2,1)S(1)}, bf16[272,256]{1,0:T(8,128)(2,1)S(1)}, u32[]{:S(2)}, u32[]{:S(2)}) collective-permute-start(bf16[272,256]{1,0:T(8,128)(2,1)S(1)} %get-tuple-element.49), channel_id=1, source_target_pairs={{0,32},{8,40},{16,48},{24,56},{32,0},{40,8},{48,16},{56,24},{64,96... | collective-permute-start | bytes 417800 | tf_op jit(solution)/shard_map/ppermute | solution.py:36
  65.9 0.0 collective-permute-done.8
  65.9 2.7 %collective-permute-done.10 = bf16[272,256]{1,0:T(8,128)(2,1)S(1)} collective-permute-done((bf16[272,256]{1,0:T(8,128)(2,1)S(1)}, bf16[272,256]{1,0:T(8,128)(2,1)S(1)}, u32[]{:S(2)}, u32[]{:S(2)}) %collective-permute-start.10) | collective-permute-done | bytes 139296 | tf_op jit(solution)/shard_map/ppermute | solution.py:36
  68.6 7.9 %collective-permute-done.9 = bf16[272,256]{1,0:T(8,128)(2,1)S(1)} collective-permute-done((bf16[272,256]{1,0:T(8,128)(2,1)S(1)}, bf16[272,256]{1,0:T(8,128)(2,1)S(1)}, u32[]{:S(2)}, u32[]{:S(2)}) %collective-permute-start.9) | collective-permute-done | bytes 139296 | tf_op jit(solution)/shard_map/ppermute | solution.py:36
  76.5 0.1 fusion.1
  76.6 1.9 %collective-permute-start.12 = (bf16[256,256]{1,0:T(8,128)(2,1)S(1)}, bf16[256,256]{1,0:T(8,128)(2,1)S(1)}, u32[]{:S(2)}, u32[]{:S(2)}) collective-permute-start(bf16[256,256]{1,0:T(8,128)(2,1)S(1)} %fusion.2), channel_id=1, source_target_pairs={{0,32},{8,40},{16,48},{24,56},{32,0},{40,8},{48,16},{56,24},{64,96... | collective-permute-start | bytes 393224 | tf_op jit(solution)/shard_map/ppermute | solution.py:36
  78.5 4.4 %collective-permute-start.11 = (bf16[256,256]{1,0:T(8,128)(2,1)S(1)}, bf16[256,256]{1,0:T(8,128)(2,1)S(1)}, u32[]{:S(2)}, u32[]{:S(2)}) collective-permute-start(bf16[256,256]{1,0:T(8,128)(2,1)S(1)} %fusion.2), channel_id=1, source_target_pairs={{0,16},{8,24},{16,0},{24,8},{32,48},{40,56},{48,32},{56,40},{64,80... | collective-permute-start | bytes 393224 | tf_op jit(solution)/shard_map/ppermute | solution.py:36
  83.0 2.9 %collective-permute-start.13 = (bf16[256,256]{1,0:T(8,128)(2,1)S(1)}, bf16[256,256]{1,0:T(8,128)(2,1)S(1)}, u32[]{:S(2)}, u32[]{:S(2)}) collective-permute-start(bf16[256,256]{1,0:T(8,128)(2,1)S(1)} %fusion.2), channel_id=1, source_target_pairs={{0,48},{8,56},{16,32},{24,40},{32,16},{40,24},{48,0},{56,8},{64,11... | collective-permute-start | bytes 393224 | tf_op jit(solution)/shard_map/ppermute | solution.py:36
  85.9 1.6 %collective-permute-done.12 = bf16[256,256]{1,0:T(8,128)(2,1)S(1)} collective-permute-done((bf16[256,256]{1,0:T(8,128)(2,1)S(1)}, bf16[256,256]{1,0:T(8,128)(2,1)S(1)}, u32[]{:S(2)}, u32[]{:S(2)}) %collective-permute-start.12) | collective-permute-done | bytes 131104 | tf_op jit(solution)/shard_map/ppermute | solution.py:36
  87.6 1.3 %collective-permute-done.11 = bf16[256,256]{1,0:T(8,128)(2,1)S(1)} collective-permute-done((bf16[256,256]{1,0:T(8,128)(2,1)S(1)}, bf16[256,256]{1,0:T(8,128)(2,1)S(1)}, u32[]{:S(2)}, u32[]{:S(2)}) %collective-permute-start.11) | collective-permute-done | bytes 131104 | tf_op jit(solution)/shard_map/ppermute | solution.py:36
  88.8 1.8 %collective-permute-done.13 = bf16[256,256]{1,0:T(8,128)(2,1)S(1)} collective-permute-done((bf16[256,256]{1,0:T(8,128)(2,1)S(1)}, bf16[256,256]{1,0:T(8,128)(2,1)S(1)}, u32[]{:S(2)}, u32[]{:S(2)}) %collective-permute-start.13) | collective-permute-done | bytes 131104 | tf_op jit(solution)/shard_map/ppermute | solution.py:36
  90.6 0.1 pad_maximum_fusion.mine
  90.7 0.0 copy-start.1
  90.7 4.7 %collective-permute-start.14 = (bf16[4,256,256]{2,1,0:T(8,128)(2,1)S(1)}, bf16[4,256,256]{2,1,0:T(8,128)(2,1)}, u32[]{:S(2)}, u32[]{:S(2)}) collective-permute-start(bf16[4,256,256]{2,1,0:T(8,128)(2,1)S(1)} %pad_maximum_fusion.mine), channel_id=1, source_target_pairs={{0,8},{8,0},{16,24},{24,16},{32,40},{40,32},{48,56},{56,48},{64,72... | collective-permute-start | bytes 1572872 | tf_op jit(solution)/shard_map/ppermute | solution.py:32
  95.4 0.6 concatenate.12.info
  96.0 1.0 %collective-permute-done.14.other = bf16[4,256,256]{2,1,0:T(8,128)(2,1)} collective-permute-done((bf16[4,256,256]{2,1,0:T(8,128)(2,1)S(1)}, bf16[4,256,256]{2,1,0:T(8,128)(2,1)}, u32[]{:S(2)}, u32[]{:S(2)}) %collective-permute-start.14) | collective-permute-done | bytes 524320 | tf_op jit(solution)/shard_map/ppermute | solution.py:32
  97.1 0.0 copy-done.1
  97.1 2.6 %shard_map.79 = bf16[2048,256]{1,0:T(8,128)(2,1)} custom-call(s32[11]{0:T(128)} %concatenate.12.info, bf16[4,256,256]{2,1,0:T(8,128)(2,1)} %get-tuple-element.28.own_1, bf16[4,256,256]{2,1,0:T(8,128)(2,1)} %get-tuple-element.41.own_2, bf16[4,256,256]{2,1,0:T(8,128)(2,1)} %copy-done.1, bf16[4,256,256]{2,1,0:T(8,128)(2,1)} %collective-permute-done.14.other), custom_call_target="tpu_custom_call" | custom-call | flops 1000 | bytes 1000 | tf_op jit(solution)/shard_map/pallas_call | solution.py:234
  99.6 0.0 all-to-all-done
  99.7 1.3 %reduce_sum.12 = bf16[80,2048]{1,0:T(8,128)(2,1)} reduce(bf16[8,80,2048]{2,1,0:T(8,128)(2,1)S(1)} %all-to-all-done, bf16[]{:T(256)} %constant.41.clone.1), dimensions={0}, to_apply=%region_0.1 | reduce | flops 1146880 | bytes 2949122 | tf_op jit(solution)/shard_map/reduce_sum | solution.py:299
  (3 shorter events, 0.1 us)
Async XLA Ops:
  0.6 15.8 %copy-start.6 = (bf16[640,256]{1,0:T(8,128)(2,1)S(1)}, bf16[640,256]{1,0:T(8,128)(2,1)}, u32[]{:S(2)}) copy-start(bf16[640,256]{1,0:T(8,128)(2,1)} %refs_0_.1) | copy-start | bytes 983044
  0.6 14.0 %collective-permute-start.2 = (bf16[640,256]{1,0:T(8,128)(2,1)}, bf16[640,256]{1,0:T(8,128)(2,1)S(1)}, u32[]{:S(2)}, u32[]{:S(2)}) collective-permute-start(bf16[640,256]{1,0:T(8,128)(2,1)} %refs_0_.1), channel_id=1, source_target_pairs={{0,3},{1,2},{2,1},{3,0},{4,7},{5,6},{6,5},{7,4},{8,11},{9,10},{10,... | collective-permute-start | bytes 983048 | tf_op jit(solution)/shard_map/ppermute | solution.py:28
  6.0 8.7 %collective-permute-start.1 = (bf16[640,256]{1,0:T(8,128)(2,1)}, bf16[640,256]{1,0:T(8,128)(2,1)S(1)}, u32[]{:S(2)}, u32[]{:S(2)}) collective-permute-start(bf16[640,256]{1,0:T(8,128)(2,1)} %refs_0_.1), channel_id=1, source_target_pairs={{0,1},{1,0},{2,3},{3,2},{4,5},{5,4},{6,7},{7,6},{8,9},{9,8},{10,11... | collective-permute-start | bytes 983048 | tf_op jit(solution)/shard_map/ppermute | solution.py:28
  7.9 8.5 %collective-permute-start = (bf16[640,256]{1,0:T(8,128)(2,1)}, bf16[640,256]{1,0:T(8,128)(2,1)S(1)}, u32[]{:S(2)}, u32[]{:S(2)}) collective-permute-start(bf16[640,256]{1,0:T(8,128)(2,1)} %refs_0_.1), channel_id=1, source_target_pairs={{0,4},{1,5},{2,6},{3,7},{4,0},{5,1},{6,2},{7,3},{8,12},{9,13},{10,... | collective-permute-start | bytes 983048 | tf_op jit(solution)/shard_map/ppermute | solution.py:28
  14.6 16.8 %copy-start.7 = (bf16[640,256]{1,0:T(8,128)(2,1)}, bf16[640,256]{1,0:T(8,128)(2,1)S(1)}, u32[]{:S(2)}) copy-start(bf16[640,256]{1,0:T(8,128)(2,1)S(1)} %collective-permute-done.2.refs_3_) | copy-start | bytes 983044
  14.7 16.8 %copy-start.8 = (bf16[640,256]{1,0:T(8,128)(2,1)}, bf16[640,256]{1,0:T(8,128)(2,1)S(1)}, u32[]{:S(2)}) copy-start(bf16[640,256]{1,0:T(8,128)(2,1)S(1)} %collective-permute-done.1.refs_2_) | copy-start | bytes 983044
  16.4 15.0 %copy-start.9 = (bf16[640,256]{1,0:T(8,128)(2,1)}, bf16[640,256]{1,0:T(8,128)(2,1)S(1)}, u32[]{:S(2)}) copy-start(bf16[640,256]{1,0:T(8,128)(2,1)S(1)} %collective-permute-done.refs_1_) | copy-start | bytes 983044
  16.4 19.5 %collective-permute-start.6 = (bf16[640,256]{1,0:T(8,128)(2,1)S(1)}, bf16[640,256]{1,0:T(8,128)(2,1)S(1)}, u32[]{:S(2)}, u32[]{:S(2)}) collective-permute-start(bf16[640,256]{1,0:T(8,128)(2,1)S(1)} %copy-done.6), channel_id=1, source_target_pairs={{0,6},{1,7},{2,4},{3,5},{4,2},{5,3},{6,0},{7,1},{8,14},{9,15},{10,... | collective-permute-start | bytes 983048 | tf_op jit(solution)/shard_map/ppermute | solution.py:28
  20.5 15.4 %collective-permute-start.5 = (bf16[640,256]{1,0:T(8,128)(2,1)S(1)}, bf16[640,256]{1,0:T(8,128)(2,1)S(1)}, u32[]{:S(2)}, u32[]{:S(2)}) collective-permute-start(bf16[640,256]{1,0:T(8,128)(2,1)S(1)} %collective-permute-done.refs_1_), channel_id=1, source_target_pairs={{0,3},{1,2},{2,1},{3,0},{4,7},{5,6},{6,5},{7,4},{8,11},{9,10},{10,... | collective-permute-start | bytes 983048 | tf_op jit(solution)/shard_map/ppermute | solution.py:28
  25.6 11.1 %collective-permute-start.3 = (bf16[640,256]{1,0:T(8,128)(2,1)S(1)}, bf16[640,256]{1,0:T(8,128)(2,1)S(1)}, u32[]{:S(2)}, u32[]{:S(2)}) collective-permute-start(bf16[640,256]{1,0:T(8,128)(2,1)S(1)} %collective-permute-done.1.refs_2_), channel_id=1, source_target_pairs={{0,4},{1,5},{2,6},{3,7},{4,0},{5,1},{6,2},{7,3},{8,12},{9,13},{10,... | collective-permute-start | bytes 983048 | tf_op jit(solution)/shard_map/ppermute | solution.py:28
  27.6 9.8 %collective-permute-start.4 = (bf16[640,256]{1,0:T(8,128)(2,1)S(1)}, bf16[640,256]{1,0:T(8,128)(2,1)S(1)}, u32[]{:S(2)}, u32[]{:S(2)}) collective-permute-start(bf16[640,256]{1,0:T(8,128)(2,1)S(1)} %collective-permute-done.2.refs_3_), channel_id=1, source_target_pairs={{0,1},{1,0},{2,3},{3,2},{4,5},{5,4},{6,7},{7,6},{8,9},{9,8},{10,11... | collective-permute-start | bytes 983048 | tf_op jit(solution)/shard_map/ppermute | solution.py:28
  35.9 1.4 %copy-start.2 = (bf16[640,256]{1,0:T(8,128)(2,1)}, bf16[640,256]{1,0:T(8,128)(2,1)S(1)}, u32[]{:S(2)}) copy-start(bf16[640,256]{1,0:T(8,128)(2,1)S(1)} %collective-permute-done.6.refs_3_) | copy-start | bytes 983044
  35.9 1.4 %copy-start.3 = (bf16[640,256]{1,0:T(8,128)(2,1)}, bf16[640,256]{1,0:T(8,128)(2,1)S(1)}, u32[]{:S(2)}) copy-start(bf16[640,256]{1,0:T(8,128)(2,1)S(1)} %collective-permute-done.5.refs_2_) | copy-start | bytes 983044
  36.8 0.7 copy-start.4
  37.3 0.7 copy-start.5
  42.4 14.6 %copy-start = (bf16[4,272,256]{2,1,0:T(8,128)(2,1)S(1)}, bf16[4,272,256]{2,1,0:T(8,128)(2,1)}, u32[]{:S(2)}) copy-start(bf16[4,272,256]{2,1,0:T(8,128)(2,1)} %get-tuple-element.42) | copy-start | bytes 1671172
  42.5 57.2 %all-to-all-start = ((bf16[8,80,2048]{2,1,0:T(8,128)(2,1)}), bf16[8,80,2048]{2,1,0:T(8,128)(2,1)S(1)}, u32[]{:S(2)}, u32[]{:S(2)}) async-start(bf16[8,80,2048]{2,1,0:T(8,128)(2,1)} %bitcast.23), calls=%async_computation | async-start | bytes 5242880 | tf_op jit(solution)/shard_map/all_to_all | solution.py:284
  46.6 10.5 %collective-permute-start.7 = (bf16[4,272,256]{2,1,0:T(8,128)(2,1)}, bf16[4,272,256]{2,1,0:T(8,128)(2,1)S(1)}, u32[]{:S(2)}, u32[]{:S(2)}) collective-permute-start(bf16[4,272,256]{2,1,0:T(8,128)(2,1)} %get-tuple-element.43), channel_id=1, source_target_pairs={{0,8},{8,0},{16,24},{24,16},{32,40},{40,32},{48,56},{56,48},{64,72... | collective-permute-start | bytes 1671176 | tf_op jit(solution)/shard_map/ppermute | solution.py:32
  57.2 8.7 %collective-permute-start.8 = (bf16[272,256]{1,0:T(8,128)(2,1)S(1)}, bf16[272,256]{1,0:T(8,128)(2,1)S(1)}, u32[]{:S(2)}, u32[]{:S(2)}) collective-permute-start(bf16[272,256]{1,0:T(8,128)(2,1)S(1)} %get-tuple-element.47), channel_id=1, source_target_pairs={{0,16},{8,24},{16,0},{24,8},{32,48},{40,56},{48,32},{56,40},{64,80... | collective-permute-start | bytes 417800 | tf_op jit(solution)/shard_map/ppermute | solution.py:36
  59.1 9.4 %collective-permute-start.10 = (bf16[272,256]{1,0:T(8,128)(2,1)S(1)}, bf16[272,256]{1,0:T(8,128)(2,1)S(1)}, u32[]{:S(2)}, u32[]{:S(2)}) collective-permute-start(bf16[272,256]{1,0:T(8,128)(2,1)S(1)} %get-tuple-element.48), channel_id=1, source_target_pairs={{0,48},{8,56},{16,32},{24,40},{32,16},{40,24},{48,0},{56,8},{64,11... | collective-permute-start | bytes 417800 | tf_op jit(solution)/shard_map/ppermute | solution.py:36
  63.7 12.8 %collective-permute-start.9 = (bf16[272,256]{1,0:T(8,128)(2,1)S(1)}, bf16[272,256]{1,0:T(8,128)(2,1)S(1)}, u32[]{:S(2)}, u32[]{:S(2)}) collective-permute-start(bf16[272,256]{1,0:T(8,128)(2,1)S(1)} %get-tuple-element.49), channel_id=1, source_target_pairs={{0,32},{8,40},{16,48},{24,56},{32,0},{40,8},{48,16},{56,24},{64,96... | collective-permute-start | bytes 417800 | tf_op jit(solution)/shard_map/ppermute | solution.py:36
  76.6 11.0 %collective-permute-start.12 = (bf16[256,256]{1,0:T(8,128)(2,1)S(1)}, bf16[256,256]{1,0:T(8,128)(2,1)S(1)}, u32[]{:S(2)}, u32[]{:S(2)}) collective-permute-start(bf16[256,256]{1,0:T(8,128)(2,1)S(1)} %fusion.2), channel_id=1, source_target_pairs={{0,32},{8,40},{16,48},{24,56},{32,0},{40,8},{48,16},{56,24},{64,96... | collective-permute-start | bytes 393224 | tf_op jit(solution)/shard_map/ppermute | solution.py:36
  78.5 10.3 %collective-permute-start.11 = (bf16[256,256]{1,0:T(8,128)(2,1)S(1)}, bf16[256,256]{1,0:T(8,128)(2,1)S(1)}, u32[]{:S(2)}, u32[]{:S(2)}) collective-permute-start(bf16[256,256]{1,0:T(8,128)(2,1)S(1)} %fusion.2), channel_id=1, source_target_pairs={{0,16},{8,24},{16,0},{24,8},{32,48},{40,56},{48,32},{56,40},{64,80... | collective-permute-start | bytes 393224 | tf_op jit(solution)/shard_map/ppermute | solution.py:36
  83.0 7.7 %collective-permute-start.13 = (bf16[256,256]{1,0:T(8,128)(2,1)S(1)}, bf16[256,256]{1,0:T(8,128)(2,1)S(1)}, u32[]{:S(2)}, u32[]{:S(2)}) collective-permute-start(bf16[256,256]{1,0:T(8,128)(2,1)S(1)} %fusion.2), channel_id=1, source_target_pairs={{0,48},{8,56},{16,32},{24,40},{32,16},{40,24},{48,0},{56,8},{64,11... | collective-permute-start | bytes 393224 | tf_op jit(solution)/shard_map/ppermute | solution.py:36
  90.7 6.4 %copy-start.1 = (bf16[4,256,256]{2,1,0:T(8,128)(2,1)}, bf16[4,256,256]{2,1,0:T(8,128)(2,1)S(1)}, u32[]{:S(2)}) copy-start(bf16[4,256,256]{2,1,0:T(8,128)(2,1)S(1)} %pad_maximum_fusion.mine) | copy-start | bytes 1572868
  90.7 6.4 %collective-permute-start.14 = (bf16[4,256,256]{2,1,0:T(8,128)(2,1)S(1)}, bf16[4,256,256]{2,1,0:T(8,128)(2,1)}, u32[]{:S(2)}, u32[]{:S(2)}) collective-permute-start(bf16[4,256,256]{2,1,0:T(8,128)(2,1)S(1)} %pad_maximum_fusion.mine), channel_id=1, source_target_pairs={{0,8},{8,0},{16,24},{24,16},{32,40},{40,32},{48,56},{56,48},{64,72... | collective-permute-start | bytes 1572872 | tf_op jit(solution)/shard_map/ppermute | solution.py:32

commit v3 on v2

--- a/solution.py
+++ b/solution.py
@@ -42,15 +42,16 @@
 
 def update_kernel(scale, first, info, *refs):
     n = 4
+    base = 0 if first else n
     acts, (cot, weight, mom) = refs[:n], refs[n : n + 3]
     mom_out, keep, send, own = refs[n + 3 : n + 7] if first else refs[n + 6 : n + 10]
     a_buf, c_buf, w_buf, m_buf, o_buf, n_buf, p_buf, f_buf, sems = refs[-9:]
     size = w_buf.shape[1]
     width = w_buf.shape[2]
-    core, chip, alive = info[n], info[n + 1], info[n + 2]
+    core, chip, alive = info[8], info[9], info[10]
 
     def rows(b):
-        return pl.ds(pl.multiple_of(info[b] * size, size), size)
+        return pl.ds(pl.multiple_of(info[base + b] * size, size), size)
 
     def loads(b):
         return (
@@ -250,9 +251,7 @@
     core = lax.rem(lax.axis_index("dp"), 2)
     alive = alive_mask[0]
     chip = lax.rem(lax.axis_index("dp") // 2, GROUP // 2)
-    tail = jnp.stack([core, chip, alive])
-    early = jnp.stack([t ^ k for k in EARLY])
-    late = jnp.stack([t ^ k for k in LATE])
+    info = jnp.stack([t ^ k for k in EARLY + LATE] + [core, chip, alive])
 
     a_y = tensor_swap(activations, 4)
     a_p = tensor_swap(activations, 1)
@@ -266,7 +265,7 @@
     a_ypq = tensor_swap(after(activations, a_q), 6)
     *done, own_1 = update(
         scale,
-        jnp.concatenate([early, tail]),
+        info,
         (activations, a_y, a_p, a_q),
         cotangent,
         weight,
@@ -276,7 +275,7 @@
         (a_yp, a_pq, a_qy, a_ypq, share, *done)
     )
     new_momentum, keep, send, own_2 = update(
-        scale, jnp.concatenate([late, tail]), (a_yp, a_pq, a_qy, a_ypq), cotangent, weight, mom, done
+        scale, info, (a_yp, a_pq, a_qy, a_ypq), cotangent, weight, mom, done
     )
 
     members = lax.axis_size("tensor")
@@ -289,14 +288,15 @@
     sums = [(keep[k].astype(f32) + arrived[k].astype(f32)).astype(bf16) for k in range(4)]
     size = sums[0].shape[0] - PAD
     got = sums[0].astype(f32)
-    for k in (1, 2, 3):
+    for k in (3, 2, 1):
         got = got + chip_swap(sums[k], k).astype(f32)
     count = jnp.maximum(got[size : size + 1], 1.0)
     mean = (got[:size] / count).astype(bf16)
     mine = jnp.stack([mean] + [chip_swap(mean, k) for k in (1, 2, 3)])
     other = core_swap(mine)
-    new_weight = place(jnp.concatenate([early, late, tail]), (own_1, own_2, mine, other), weight.shape)
     input_grad = shares.astype(f32).sum(0).astype(bf16)
+    mine, input_grad = lax.optimization_barrier((mine, input_grad))
+    new_weight = place(info, (own_1, own_2, mine, other), weight.shape)
     return new_weight[None], new_momentum[None], input_grad
 
 

time: 102 us -> 97.1 us (0.952)
  waiting for transfers between devices: 21.2 us -> 17.7 us
  local copies, waits for them, and re-layouts: 2.66 us -> 1.43 us
    ppermute x6, waiting for transfers between devices: 15.3 us -> 11.8 us  [chip_swap(): lax.ppermute(value, 'dp', [(r, r ^ 2 * k) for r in range(lax.axis_size('d...]
    concatenate x3 -> x0, local copies, waits for them, and re-layouts: 1.91 us -> none  [the longest x1 0.67 us: body(): jnp.concatenate([late, tail])]
  transfers between devices with their start and end apart: 16 -> 16, of which waited for: 10 -> 10; matrix products, arithmetic and copies ran while one was open for 2% -> 2% of each run, Pallas kernels for 10% -> 8%
where the time goes in v3:
time: 97.1 us; the launch traced here: 96.4 us
  starting transfers between devices  59.2 us (61%)
  waiting for transfers between devices  17.7 us (18%)
  Pallas kernels  14.9 us (15%)
  between operations  1.59 us (2%)
  other arithmetic  1.58 us (2%)
  local copies, waits for them, and re-layouts  1.43 us (1%)
    ppermute x7, starting transfers between devices, tensor_swap(): lax.ppermute(value, 'tensor', [(t, t ^ k) for t in range(lax.axis_size('t...  23.5 us
    ppermute x6, starting transfers between devices, chip_swap(): lax.ppermute(value, 'dp', [(r, r ^ 2 * k) for r in range(lax.axis_size('d...  18.5 us
    ppermute x2, starting transfers between devices, core_swap(): lax.ppermute(value, 'dp', [(r, r ^ 1) for r in range(lax.axis_size('dp'))])  13 us
    ppermute x6, waiting for transfers between devices, chip_swap(): lax.ppermute(value, 'dp', [(r, r ^ 2 * k) for r in range(lax.axis_size('d...  11.8 us
    pallas_call x2, Pallas kernels, update(): pl.pallas_call(functools.partial(update_kernel, scale, first), out_shape=...  8.86 us
    all_to_all x1, starting transfers between devices, body(): lax.all_to_all(share.reshape(members, share.shape[0] // members, features...  4.13 us
    ppermute x7, waiting for transfers between devices, tensor_swap(): lax.ppermute(value, 'tensor', [(t, t ^ k) for t in range(lax.axis_size('t...  3.74 us
    pallas_call x1, Pallas kernels, partials(): pl.pallas_call(functools.partial(partial_kernel, scale), out_shape=jax.Sh...  3.47 us
  transfers between devices with their start and end apart: 16, of which 10 were waited for; matrix products, arithmetic and copies ran while one was open for 2% of the time, Pallas kernels for 8%

profile of v3, /device:TPU:1, one launch (start us, length us, event | category | flops | bytes accessed | tf_op | source)
XLA Modules:
  0.0 96.4 jit_solution(10032344334484446990)
XLA Ops:
  0.6 0.0 copy-start.6
  0.6 5.3 %collective-permute-start.2 = (bf16[640,256]{1,0:T(8,128)(2,1)}, bf16[640,256]{1,0:T(8,128)(2,1)S(1)}, u32[]{:S(2)}, u32[]{:S(2)}) collective-permute-start(bf16[640,256]{1,0:T(8,128)(2,1)} %refs_0_.1), channel_id=1, source_target_pairs={{0,3},{1,2},{2,1},{3,0},{4,7},{5,6},{6,5},{7,4},{8,11},{9,10},{10,... | collective-permute-start | bytes 983048 | tf_op jit(solution)/shard_map/ppermute | solution.py:28
  6.0 1.9 %collective-permute-start.1 = (bf16[640,256]{1,0:T(8,128)(2,1)}, bf16[640,256]{1,0:T(8,128)(2,1)S(1)}, u32[]{:S(2)}, u32[]{:S(2)}) collective-permute-start(bf16[640,256]{1,0:T(8,128)(2,1)} %refs_0_.1), channel_id=1, source_target_pairs={{0,1},{1,0},{2,3},{3,2},{4,5},{5,4},{6,7},{7,6},{8,9},{9,8},{10,11... | collective-permute-start | bytes 983048 | tf_op jit(solution)/shard_map/ppermute | solution.py:28
  7.9 3.2 %collective-permute-start = (bf16[640,256]{1,0:T(8,128)(2,1)}, bf16[640,256]{1,0:T(8,128)(2,1)S(1)}, u32[]{:S(2)}, u32[]{:S(2)}) collective-permute-start(bf16[640,256]{1,0:T(8,128)(2,1)} %refs_0_.1), channel_id=1, source_target_pairs={{0,4},{1,5},{2,6},{3,7},{4,0},{5,1},{6,2},{7,3},{8,12},{9,13},{10,... | collective-permute-start | bytes 983048 | tf_op jit(solution)/shard_map/ppermute | solution.py:28
  11.1 3.5 %shard_map.76 = bf16[640,2048]{1,0:T(8,128)(2,1)} custom-call(bf16[640,256]{1,0:T(8,128)(2,1)} %refs_4_.3, bf16[2048,256]{1,0:T(8,128)(2,1)} %bitcast.32), custom_call_target="tpu_custom_call" | custom-call | flops 1000 | bytes 1000 | tf_op jit(solution)/shard_map/pallas_call | solution.py:189
  14.6 0.0 collective-permute-done.2.refs_3_
  14.6 0.0 copy-start.7
  14.6 0.0 collective-permute-done.1.refs_2_
  14.7 0.0 copy-start.8
  14.7 1.8 %collective-permute-done.refs_1_ = bf16[640,256]{1,0:T(8,128)(2,1)S(1)} collective-permute-done((bf16[640,256]{1,0:T(8,128)(2,1)}, bf16[640,256]{1,0:T(8,128)(2,1)S(1)}, u32[]{:S(2)}, u32[]{:S(2)}) %collective-permute-start) | collective-permute-done | bytes 327712 | tf_op jit(solution)/shard_map/ppermute | solution.py:28
  16.4 0.0 copy-done.6
  16.4 0.0 copy-start.9
  16.4 4.1 %collective-permute-start.6 = (bf16[640,256]{1,0:T(8,128)(2,1)S(1)}, bf16[640,256]{1,0:T(8,128)(2,1)S(1)}, u32[]{:S(2)}, u32[]{:S(2)}) collective-permute-start(bf16[640,256]{1,0:T(8,128)(2,1)S(1)} %copy-done.6), channel_id=1, source_target_pairs={{0,6},{1,7},{2,4},{3,5},{4,2},{5,3},{6,0},{7,1},{8,14},{9,15},{10,... | collective-permute-start | bytes 983048 | tf_op jit(solution)/shard_map/ppermute | solution.py:28
  20.5 5.1 %collective-permute-start.5 = (bf16[640,256]{1,0:T(8,128)(2,1)S(1)}, bf16[640,256]{1,0:T(8,128)(2,1)S(1)}, u32[]{:S(2)}, u32[]{:S(2)}) collective-permute-start(bf16[640,256]{1,0:T(8,128)(2,1)S(1)} %collective-permute-done.refs_1_), channel_id=1, source_target_pairs={{0,3},{1,2},{2,1},{3,0},{4,7},{5,6},{6,5},{7,4},{8,11},{9,10},{10,... | collective-permute-start | bytes 983048 | tf_op jit(solution)/shard_map/ppermute | solution.py:28
  25.6 1.9 %collective-permute-start.3 = (bf16[640,256]{1,0:T(8,128)(2,1)S(1)}, bf16[640,256]{1,0:T(8,128)(2,1)S(1)}, u32[]{:S(2)}, u32[]{:S(2)}) collective-permute-start(bf16[640,256]{1,0:T(8,128)(2,1)S(1)} %collective-permute-done.1.refs_2_), channel_id=1, source_target_pairs={{0,4},{1,5},{2,6},{3,7},{4,0},{5,1},{6,2},{7,3},{8,12},{9,13},{10,... | collective-permute-start | bytes 983048 | tf_op jit(solution)/shard_map/ppermute | solution.py:28
  27.6 1.9 %collective-permute-start.4 = (bf16[640,256]{1,0:T(8,128)(2,1)S(1)}, bf16[640,256]{1,0:T(8,128)(2,1)S(1)}, u32[]{:S(2)}, u32[]{:S(2)}) collective-permute-start(bf16[640,256]{1,0:T(8,128)(2,1)S(1)} %collective-permute-done.2.refs_3_), channel_id=1, source_target_pairs={{0,1},{1,0},{2,3},{3,2},{4,5},{5,4},{6,7},{7,6},{8,9},{9,8},{10,11... | collective-permute-start | bytes 983048 | tf_op jit(solution)/shard_map/ppermute | solution.py:28
  30.2 0.7 stack.58.info
  30.8 0.0 copy-done.7
  30.8 0.0 copy-done.8
  30.8 0.0 copy-done.9
  30.8 4.4 %shard_map.77 = (bf16[2048,256]{1,0:T(8,128)(2,1)}, bf16[4,272,256]{2,1,0:T(8,128)(2,1)}, bf16[4,272,256]{2,1,0:T(8,128)(2,1)}, bf16[4,256,256]{2,1,0:T(8,128)(2,1)}) custom-call(s32[11]{0:T(128)} %stack.58.info, bf16[640,256]{1,0:T(8,128)(2,1)} %refs_0_.1, bf16[640,256]{1,0:T(8,128)(2,1)} %copy-done.9, bf16[640,256]{1,0:T(8,128)(2,1)} %copy-done.8, ...), custom_call_target="tpu_custom_call" | custom-call | flops 1000 | bytes 1000 | tf_op jit(solution)/shard_map/pallas_call | solution.py:130
  35.3 0.0 collective-permute-done.6.refs_3_
  35.3 0.0 copy-start.2
  35.3 0.5 collective-permute-done.5.refs_2_
  35.8 0.0 copy-start.3
  35.8 1.0 %collective-permute-done.3.refs_0_ = bf16[640,256]{1,0:T(8,128)(2,1)S(1)} collective-permute-done((bf16[640,256]{1,0:T(8,128)(2,1)S(1)}, bf16[640,256]{1,0:T(8,128)(2,1)S(1)}, u32[]{:S(2)}, u32[]{:S(2)}) %collective-permute-start.3) | collective-permute-done | bytes 327712 | tf_op jit(solution)/shard_map/ppermute | solution.py:28
  36.8 0.0 copy-start.4
  36.8 0.5 collective-permute-done.4.refs_1_
  37.3 0.0 copy-start.5
  37.3 0.0 copy-done.2
  37.3 0.0 copy-done.3
  37.3 0.2 copy-done.4
  37.5 0.5 copy-done.5
  38.0 4.4 %shard_map.78 = (bf16[2048,256]{1,0:T(8,128)(2,1)}, bf16[4,272,256]{2,1,0:T(8,128)(2,1)}, bf16[4,272,256]{2,1,0:T(8,128)(2,1)}, bf16[4,256,256]{2,1,0:T(8,128)(2,1)}) custom-call(s32[11]{0:T(128)} %stack.58.info, bf16[640,256]{1,0:T(8,128)(2,1)} %copy-done.4, ...), custom_call_target="tpu_custom_call", output_to_operand_aliasing={{0}: (8, {}), {1}: (9, {}), {2}: (10, {})} | custom-call | flops 1000 | bytes 1000 | tf_op jit(solution)/shard_map/pallas_call | solution.py:130
  42.4 0.0 copy-start
  42.5 4.1 %all-to-all-start = ((bf16[8,80,2048]{2,1,0:T(8,128)(2,1)}), bf16[8,80,2048]{2,1,0:T(8,128)(2,1)S(1)}, u32[]{:S(2)}, u32[]{:S(2)}) async-start(bf16[8,80,2048]{2,1,0:T(8,128)(2,1)} %bitcast.21), calls=%async_computation | async-start | bytes 5242880 | tf_op jit(solution)/shard_map/all_to_all | solution.py:283
  46.6 8.1 %collective-permute-start.7 = (bf16[4,272,256]{2,1,0:T(8,128)(2,1)}, bf16[4,272,256]{2,1,0:T(8,128)(2,1)S(1)}, u32[]{:S(2)}, u32[]{:S(2)}) collective-permute-start(bf16[4,272,256]{2,1,0:T(8,128)(2,1)} %get-tuple-element.45), channel_id=1, source_target_pairs={{0,8},{8,0},{16,24},{24,16},{32,40},{40,32},{48,56},{56,48},{64,72... | collective-permute-start | bytes 1671176 | tf_op jit(solution)/shard_map/ppermute | solution.py:32
  54.7 1.8 %collective-permute-done.7 = bf16[4,272,256]{2,1,0:T(8,128)(2,1)S(1)} collective-permute-done((bf16[4,272,256]{2,1,0:T(8,128)(2,1)}, bf16[4,272,256]{2,1,0:T(8,128)(2,1)S(1)}, u32[]{:S(2)}, u32[]{:S(2)}) %collective-permute-start.7) | collective-permute-done | bytes 557088 | tf_op jit(solution)/shard_map/ppermute | solution.py:32
  56.5 0.0 copy-done
  56.5 0.1 fusion.4
  56.6 5.1 %collective-permute-start.8 = (bf16[272,256]{1,0:T(8,128)(2,1)S(1)}, bf16[272,256]{1,0:T(8,128)(2,1)S(1)}, u32[]{:S(2)}, u32[]{:S(2)}) collective-permute-start(bf16[272,256]{1,0:T(8,128)(2,1)S(1)} %get-tuple-element.51), channel_id=1, source_target_pairs={{0,48},{8,56},{16,32},{24,40},{32,16},{40,24},{48,0},{56,8},{64,11... | collective-permute-start | bytes 417800 | tf_op jit(solution)/shard_map/ppermute | solution.py:36
  61.7 1.9 %collective-permute-start.10 = (bf16[272,256]{1,0:T(8,128)(2,1)S(1)}, bf16[272,256]{1,0:T(8,128)(2,1)S(1)}, u32[]{:S(2)}, u32[]{:S(2)}) collective-permute-start(bf16[272,256]{1,0:T(8,128)(2,1)S(1)} %get-tuple-element.52), channel_id=1, source_target_pairs={{0,16},{8,24},{16,0},{24,8},{32,48},{40,56},{48,32},{56,40},{64,80... | collective-permute-start | bytes 417800 | tf_op jit(solution)/shard_map/ppermute | solution.py:36
  63.7 2.2 %collective-permute-start.9 = (bf16[272,256]{1,0:T(8,128)(2,1)S(1)}, bf16[272,256]{1,0:T(8,128)(2,1)S(1)}, u32[]{:S(2)}, u32[]{:S(2)}) collective-permute-start(bf16[272,256]{1,0:T(8,128)(2,1)S(1)} %get-tuple-element.53), channel_id=1, source_target_pairs={{0,32},{8,40},{16,48},{24,56},{32,0},{40,8},{48,16},{56,24},{64,96... | collective-permute-start | bytes 417800 | tf_op jit(solution)/shard_map/ppermute | solution.py:36
  65.9 0.0 collective-permute-done.8
  65.9 2.8 %collective-permute-done.10 = bf16[272,256]{1,0:T(8,128)(2,1)S(1)} collective-permute-done((bf16[272,256]{1,0:T(8,128)(2,1)S(1)}, bf16[272,256]{1,0:T(8,128)(2,1)S(1)}, u32[]{:S(2)}, u32[]{:S(2)}) %collective-permute-start.10) | collective-permute-done | bytes 139296 | tf_op jit(solution)/shard_map/ppermute | solution.py:36
  68.7 5.4 %collective-permute-done.9 = bf16[272,256]{1,0:T(8,128)(2,1)S(1)} collective-permute-done((bf16[272,256]{1,0:T(8,128)(2,1)S(1)}, bf16[272,256]{1,0:T(8,128)(2,1)S(1)}, u32[]{:S(2)}, u32[]{:S(2)}) %collective-permute-start.9) | collective-permute-done | bytes 139296 | tf_op jit(solution)/shard_map/ppermute | solution.py:36
  74.1 0.1 fusion.1
  74.2 1.9 %collective-permute-start.12 = (bf16[256,256]{1,0:T(8,128)(2,1)S(1)}, bf16[256,256]{1,0:T(8,128)(2,1)S(1)}, u32[]{:S(2)}, u32[]{:S(2)}) collective-permute-start(bf16[256,256]{1,0:T(8,128)(2,1)S(1)} %fusion.2), channel_id=1, source_target_pairs={{0,32},{8,40},{16,48},{24,56},{32,0},{40,8},{48,16},{56,24},{64,96... | collective-permute-start | bytes 393224 | tf_op jit(solution)/shard_map/ppermute | solution.py:36
  76.2 2.3 %collective-permute-start.11 = (bf16[256,256]{1,0:T(8,128)(2,1)S(1)}, bf16[256,256]{1,0:T(8,128)(2,1)S(1)}, u32[]{:S(2)}, u32[]{:S(2)}) collective-permute-start(bf16[256,256]{1,0:T(8,128)(2,1)S(1)} %fusion.2), channel_id=1, source_target_pairs={{0,16},{8,24},{16,0},{24,8},{32,48},{40,56},{48,32},{56,40},{64,80... | collective-permute-start | bytes 393224 | tf_op jit(solution)/shard_map/ppermute | solution.py:36
  78.4 5.1 %collective-permute-start.13 = (bf16[256,256]{1,0:T(8,128)(2,1)S(1)}, bf16[256,256]{1,0:T(8,128)(2,1)S(1)}, u32[]{:S(2)}, u32[]{:S(2)}) collective-permute-start(bf16[256,256]{1,0:T(8,128)(2,1)S(1)} %fusion.2), channel_id=1, source_target_pairs={{0,48},{8,56},{16,32},{24,40},{32,16},{40,24},{48,0},{56,8},{64,11... | collective-permute-start | bytes 393224 | tf_op jit(solution)/shard_map/ppermute | solution.py:36
  83.6 0.0 collective-permute-done.12
  83.6 1.2 %collective-permute-done.11 = bf16[256,256]{1,0:T(8,128)(2,1)S(1)} collective-permute-done((bf16[256,256]{1,0:T(8,128)(2,1)S(1)}, bf16[256,256]{1,0:T(8,128)(2,1)S(1)}, u32[]{:S(2)}, u32[]{:S(2)}) %collective-permute-start.11) | collective-permute-done | bytes 131104 | tf_op jit(solution)/shard_map/ppermute | solution.py:36
  84.7 2.4 %collective-permute-done.13 = bf16[256,256]{1,0:T(8,128)(2,1)S(1)} collective-permute-done((bf16[256,256]{1,0:T(8,128)(2,1)S(1)}, bf16[256,256]{1,0:T(8,128)(2,1)S(1)}, u32[]{:S(2)}, u32[]{:S(2)}) %collective-permute-start.13) | collective-permute-done | bytes 131104 | tf_op jit(solution)/shard_map/ppermute | solution.py:36
  87.1 0.1 pad_maximum_fusion.mine
  87.2 0.0 copy-start.1
  87.2 4.9 %collective-permute-start.14 = (bf16[4,256,256]{2,1,0:T(8,128)(2,1)S(1)}, bf16[4,256,256]{2,1,0:T(8,128)(2,1)}, u32[]{:S(2)}, u32[]{:S(2)}) collective-permute-start(bf16[4,256,256]{2,1,0:T(8,128)(2,1)S(1)} %pad_maximum_fusion.mine), channel_id=1, source_target_pairs={{0,8},{8,0},{16,24},{24,16},{32,40},{40,32},{48,56},{56,48},{64,72... | collective-permute-start | bytes 1572872 | tf_op jit(solution)/shard_map/ppermute | solution.py:32
  92.2 0.0 all-to-all-done
  92.2 1.3 %reduce_sum.12 = bf16[80,2048]{1,0:T(8,128)(2,1)} reduce(bf16[8,80,2048]{2,1,0:T(8,128)(2,1)S(1)} %all-to-all-done, bf16[]{:T(256)} %constant.41.clone.1), dimensions={0}, to_apply=%region_0.1 | reduce | flops 1146880 | bytes 2949122 | tf_op jit(solution)/shard_map/reduce_sum | solution.py:297
  93.5 0.4 collective-permute-done.14.other
  93.8 0.0 copy-done.1
  93.8 2.6 %shard_map.79 = bf16[2048,256]{1,0:T(8,128)(2,1)} custom-call(s32[11]{0:T(128)} %stack.58.info, bf16[4,256,256]{2,1,0:T(8,128)(2,1)} %get-tuple-element.30.own_1, bf16[4,256,256]{2,1,0:T(8,128)(2,1)} %get-tuple-element.43.own_2, bf16[4,256,256]{2,1,0:T(8,128)(2,1)} %copy-done.1, bf16[4,256,256]{2,1,0:T(8,128)(2,1)} %collective-permute-done.14.other), custom_call_target="tpu_custom_call" | custom-call | flops 1000 | bytes 1000 | tf_op jit(solution)/shard_map/pallas_call | solution.py:235
  (3 shorter events, 0.1 us)
Async XLA Ops:
  0.6 15.8 %copy-start.6 = (bf16[640,256]{1,0:T(8,128)(2,1)S(1)}, bf16[640,256]{1,0:T(8,128)(2,1)}, u32[]{:S(2)}) copy-start(bf16[640,256]{1,0:T(8,128)(2,1)} %refs_0_.1) | copy-start | bytes 983044
  0.6 14.0 %collective-permute-start.2 = (bf16[640,256]{1,0:T(8,128)(2,1)}, bf16[640,256]{1,0:T(8,128)(2,1)S(1)}, u32[]{:S(2)}, u32[]{:S(2)}) collective-permute-start(bf16[640,256]{1,0:T(8,128)(2,1)} %refs_0_.1), channel_id=1, source_target_pairs={{0,3},{1,2},{2,1},{3,0},{4,7},{5,6},{6,5},{7,4},{8,11},{9,10},{10,... | collective-permute-start | bytes 983048 | tf_op jit(solution)/shard_map/ppermute | solution.py:28
  6.0 8.7 %collective-permute-start.1 = (bf16[640,256]{1,0:T(8,128)(2,1)}, bf16[640,256]{1,0:T(8,128)(2,1)S(1)}, u32[]{:S(2)}, u32[]{:S(2)}) collective-permute-start(bf16[640,256]{1,0:T(8,128)(2,1)} %refs_0_.1), channel_id=1, source_target_pairs={{0,1},{1,0},{2,3},{3,2},{4,5},{5,4},{6,7},{7,6},{8,9},{9,8},{10,11... | collective-permute-start | bytes 983048 | tf_op jit(solution)/shard_map/ppermute | solution.py:28
  7.9 8.5 %collective-permute-start = (bf16[640,256]{1,0:T(8,128)(2,1)}, bf16[640,256]{1,0:T(8,128)(2,1)S(1)}, u32[]{:S(2)}, u32[]{:S(2)}) collective-permute-start(bf16[640,256]{1,0:T(8,128)(2,1)} %refs_0_.1), channel_id=1, source_target_pairs={{0,4},{1,5},{2,6},{3,7},{4,0},{5,1},{6,2},{7,3},{8,12},{9,13},{10,... | collective-permute-start | bytes 983048 | tf_op jit(solution)/shard_map/ppermute | solution.py:28
  14.6 16.2 %copy-start.7 = (bf16[640,256]{1,0:T(8,128)(2,1)}, bf16[640,256]{1,0:T(8,128)(2,1)S(1)}, u32[]{:S(2)}) copy-start(bf16[640,256]{1,0:T(8,128)(2,1)S(1)} %collective-permute-done.2.refs_3_) | copy-start | bytes 983044
  14.7 16.2 %copy-start.8 = (bf16[640,256]{1,0:T(8,128)(2,1)}, bf16[640,256]{1,0:T(8,128)(2,1)S(1)}, u32[]{:S(2)}) copy-start(bf16[640,256]{1,0:T(8,128)(2,1)S(1)} %collective-permute-done.1.refs_2_) | copy-start | bytes 983044
  16.4 14.4 %copy-start.9 = (bf16[640,256]{1,0:T(8,128)(2,1)}, bf16[640,256]{1,0:T(8,128)(2,1)S(1)}, u32[]{:S(2)}) copy-start(bf16[640,256]{1,0:T(8,128)(2,1)S(1)} %collective-permute-done.refs_1_) | copy-start | bytes 983044
  16.4 18.9 %collective-permute-start.6 = (bf16[640,256]{1,0:T(8,128)(2,1)S(1)}, bf16[640,256]{1,0:T(8,128)(2,1)S(1)}, u32[]{:S(2)}, u32[]{:S(2)}) collective-permute-start(bf16[640,256]{1,0:T(8,128)(2,1)S(1)} %copy-done.6), channel_id=1, source_target_pairs={{0,6},{1,7},{2,4},{3,5},{4,2},{5,3},{6,0},{7,1},{8,14},{9,15},{10,... | collective-permute-start | bytes 983048 | tf_op jit(solution)/shard_map/ppermute | solution.py:28
  20.5 15.2 %collective-permute-start.5 = (bf16[640,256]{1,0:T(8,128)(2,1)S(1)}, bf16[640,256]{1,0:T(8,128)(2,1)S(1)}, u32[]{:S(2)}, u32[]{:S(2)}) collective-permute-start(bf16[640,256]{1,0:T(8,128)(2,1)S(1)} %collective-permute-done.refs_1_), channel_id=1, source_target_pairs={{0,3},{1,2},{2,1},{3,0},{4,7},{5,6},{6,5},{7,4},{8,11},{9,10},{10,... | collective-permute-start | bytes 983048 | tf_op jit(solution)/shard_map/ppermute | solution.py:28
  25.6 11.1 %collective-permute-start.3 = (bf16[640,256]{1,0:T(8,128)(2,1)S(1)}, bf16[640,256]{1,0:T(8,128)(2,1)S(1)}, u32[]{:S(2)}, u32[]{:S(2)}) collective-permute-start(bf16[640,256]{1,0:T(8,128)(2,1)S(1)} %collective-permute-done.1.refs_2_), channel_id=1, source_target_pairs={{0,4},{1,5},{2,6},{3,7},{4,0},{5,1},{6,2},{7,3},{8,12},{9,13},{10,... | collective-permute-start | bytes 983048 | tf_op jit(solution)/shard_map/ppermute | solution.py:28
  27.6 9.8 %collective-permute-start.4 = (bf16[640,256]{1,0:T(8,128)(2,1)S(1)}, bf16[640,256]{1,0:T(8,128)(2,1)S(1)}, u32[]{:S(2)}, u32[]{:S(2)}) collective-permute-start(bf16[640,256]{1,0:T(8,128)(2,1)S(1)} %collective-permute-done.2.refs_3_), channel_id=1, source_target_pairs={{0,1},{1,0},{2,3},{3,2},{4,5},{5,4},{6,7},{7,6},{8,9},{9,8},{10,11... | collective-permute-start | bytes 983048 | tf_op jit(solution)/shard_map/ppermute | solution.py:28
  35.3 2.0 %copy-start.2 = (bf16[640,256]{1,0:T(8,128)(2,1)}, bf16[640,256]{1,0:T(8,128)(2,1)S(1)}, u32[]{:S(2)}) copy-start(bf16[640,256]{1,0:T(8,128)(2,1)S(1)} %collective-permute-done.6.refs_3_) | copy-start | bytes 983044
  35.8 1.5 %copy-start.3 = (bf16[640,256]{1,0:T(8,128)(2,1)}, bf16[640,256]{1,0:T(8,128)(2,1)S(1)}, u32[]{:S(2)}) copy-start(bf16[640,256]{1,0:T(8,128)(2,1)S(1)} %collective-permute-done.5.refs_2_) | copy-start | bytes 983044
  36.8 0.7 copy-start.4
  37.3 0.7 copy-start.5
  42.4 14.0 %copy-start = (bf16[4,272,256]{2,1,0:T(8,128)(2,1)S(1)}, bf16[4,272,256]{2,1,0:T(8,128)(2,1)}, u32[]{:S(2)}) copy-start(bf16[4,272,256]{2,1,0:T(8,128)(2,1)} %get-tuple-element.44) | copy-start | bytes 1671172
  42.5 49.7 %all-to-all-start = ((bf16[8,80,2048]{2,1,0:T(8,128)(2,1)}), bf16[8,80,2048]{2,1,0:T(8,128)(2,1)S(1)}, u32[]{:S(2)}, u32[]{:S(2)}) async-start(bf16[8,80,2048]{2,1,0:T(8,128)(2,1)} %bitcast.21), calls=%async_computation | async-start | bytes 5242880 | tf_op jit(solution)/shard_map/all_to_all | solution.py:283
  46.6 9.9 %collective-permute-start.7 = (bf16[4,272,256]{2,1,0:T(8,128)(2,1)}, bf16[4,272,256]{2,1,0:T(8,128)(2,1)S(1)}, u32[]{:S(2)}, u32[]{:S(2)}) collective-permute-start(bf16[4,272,256]{2,1,0:T(8,128)(2,1)} %get-tuple-element.45), channel_id=1, source_target_pairs={{0,8},{8,0},{16,24},{24,16},{32,40},{40,32},{48,56},{56,48},{64,72... | collective-permute-start | bytes 1671176 | tf_op jit(solution)/shard_map/ppermute | solution.py:32
  56.6 9.3 %collective-permute-start.8 = (bf16[272,256]{1,0:T(8,128)(2,1)S(1)}, bf16[272,256]{1,0:T(8,128)(2,1)S(1)}, u32[]{:S(2)}, u32[]{:S(2)}) collective-permute-start(bf16[272,256]{1,0:T(8,128)(2,1)S(1)} %get-tuple-element.51), channel_id=1, source_target_pairs={{0,48},{8,56},{16,32},{24,40},{32,16},{40,24},{48,0},{56,8},{64,11... | collective-permute-start | bytes 417800 | tf_op jit(solution)/shard_map/ppermute | solution.py:36
  61.7 7.0 %collective-permute-start.10 = (bf16[272,256]{1,0:T(8,128)(2,1)S(1)}, bf16[272,256]{1,0:T(8,128)(2,1)S(1)}, u32[]{:S(2)}, u32[]{:S(2)}) collective-permute-start(bf16[272,256]{1,0:T(8,128)(2,1)S(1)} %get-tuple-element.52), channel_id=1, source_target_pairs={{0,16},{8,24},{16,0},{24,8},{32,48},{40,56},{48,32},{56,40},{64,80... | collective-permute-start | bytes 417800 | tf_op jit(solution)/shard_map/ppermute | solution.py:36
  63.7 10.4 %collective-permute-start.9 = (bf16[272,256]{1,0:T(8,128)(2,1)S(1)}, bf16[272,256]{1,0:T(8,128)(2,1)S(1)}, u32[]{:S(2)}, u32[]{:S(2)}) collective-permute-start(bf16[272,256]{1,0:T(8,128)(2,1)S(1)} %get-tuple-element.53), channel_id=1, source_target_pairs={{0,32},{8,40},{16,48},{24,56},{32,0},{40,8},{48,16},{56,24},{64,96... | collective-permute-start | bytes 417800 | tf_op jit(solution)/shard_map/ppermute | solution.py:36
  74.2 9.3 %collective-permute-start.12 = (bf16[256,256]{1,0:T(8,128)(2,1)S(1)}, bf16[256,256]{1,0:T(8,128)(2,1)S(1)}, u32[]{:S(2)}, u32[]{:S(2)}) collective-permute-start(bf16[256,256]{1,0:T(8,128)(2,1)S(1)} %fusion.2), channel_id=1, source_target_pairs={{0,32},{8,40},{16,48},{24,56},{32,0},{40,8},{48,16},{56,24},{64,96... | collective-permute-start | bytes 393224 | tf_op jit(solution)/shard_map/ppermute | solution.py:36
  76.2 8.6 %collective-permute-start.11 = (bf16[256,256]{1,0:T(8,128)(2,1)S(1)}, bf16[256,256]{1,0:T(8,128)(2,1)S(1)}, u32[]{:S(2)}, u32[]{:S(2)}) collective-permute-start(bf16[256,256]{1,0:T(8,128)(2,1)S(1)} %fusion.2), channel_id=1, source_target_pairs={{0,16},{8,24},{16,0},{24,8},{32,48},{40,56},{48,32},{56,40},{64,80... | collective-permute-start | bytes 393224 | tf_op jit(solution)/shard_map/ppermute | solution.py:36
  78.4 8.7 %collective-permute-start.13 = (bf16[256,256]{1,0:T(8,128)(2,1)S(1)}, bf16[256,256]{1,0:T(8,128)(2,1)S(1)}, u32[]{:S(2)}, u32[]{:S(2)}) collective-permute-start(bf16[256,256]{1,0:T(8,128)(2,1)S(1)} %fusion.2), channel_id=1, source_target_pairs={{0,48},{8,56},{16,32},{24,40},{32,16},{40,24},{48,0},{56,8},{64,11... | collective-permute-start | bytes 393224 | tf_op jit(solution)/shard_map/ppermute | solution.py:36
  87.2 6.6 %copy-start.1 = (bf16[4,256,256]{2,1,0:T(8,128)(2,1)}, bf16[4,256,256]{2,1,0:T(8,128)(2,1)S(1)}, u32[]{:S(2)}) copy-start(bf16[4,256,256]{2,1,0:T(8,128)(2,1)S(1)} %pad_maximum_fusion.mine) | copy-start | bytes 1572868
  87.2 6.6 %collective-permute-start.14 = (bf16[4,256,256]{2,1,0:T(8,128)(2,1)S(1)}, bf16[4,256,256]{2,1,0:T(8,128)(2,1)}, u32[]{:S(2)}, u32[]{:S(2)}) collective-permute-start(bf16[4,256,256]{2,1,0:T(8,128)(2,1)S(1)} %pad_maximum_fusion.mine), channel_id=1, source_target_pairs={{0,8},{8,0},{16,24},{24,16},{32,40},{40,32},{48,56},{56,48},{64,72... | collective-permute-start | bytes 1572872 | tf_op jit(solution)/shard_map/ppermute | solution.py:32

commit v4 on v3

--- a/solution.py
+++ b/solution.py
@@ -238,7 +238,7 @@
         in_specs=[SMEM] + [VMEM] * 4,
         out_specs=ANY,
         scratch_shapes=[pltpu.SemaphoreType.DMA((8,))],
-        compiler_params=PARAMS,
+        compiler_params=pltpu.CompilerParams(vmem_limit_bytes=4 * 1024 * 1024),
         cost_estimate=CHEAP,
     )(info, *parts)
 
@@ -288,14 +288,13 @@
     sums = [(keep[k].astype(f32) + arrived[k].astype(f32)).astype(bf16) for k in range(4)]
     size = sums[0].shape[0] - PAD
     got = sums[0].astype(f32)
-    for k in (3, 2, 1):
+    for k in (2, 3, 1):
         got = got + chip_swap(sums[k], k).astype(f32)
     count = jnp.maximum(got[size : size + 1], 1.0)
     mean = (got[:size] / count).astype(bf16)
-    mine = jnp.stack([mean] + [chip_swap(mean, k) for k in (1, 2, 3)])
+    input_grad = shares.astype(f32).sum(0).astype(bf16)
+    mine = jnp.stack([after(mean, input_grad)] + [chip_swap(mean, k) for k in (1, 2, 3)])
     other = core_swap(mine)
-    input_grad = shares.astype(f32).sum(0).astype(bf16)
-    mine, input_grad = lax.optimization_barrier((mine, input_grad))
     new_weight = place(info, (own_1, own_2, mine, other), weight.shape)
     return new_weight[None], new_momentum[None], input_grad
 

time: 97.1 us -> 96.7 us (level)
  starting transfers between devices: 59.2 us -> 57.3 us
  other arithmetic: 1.58 us -> 3.31 us
  Pallas kernels: 14.9 us -> 13.9 us
    ppermute x2, starting transfers between devices: 13 us -> 10.4 us  [core_swap(): lax.ppermute(value, 'dp', [(r, r ^ 1) for r in range(lax.axis_size('dp'))])]
    reduce_sum x1, other arithmetic: 1.26 us -> 3.02 us  [body(): input_grad = shares.astype(f32).sum(0).astype(bf16)]
    pallas_call x1, Pallas kernels: 2.55 us -> 1.57 us  [place(): pl.pallas_call(place_kernel, out_shape=jax.ShapeDtypeStruct(shape, bf16),...]
  transfers between devices with their start and end apart: 16 -> 16, of which waited for: 10 -> 10; matrix products, arithmetic and copies ran while one was open for 2% -> 4% of each run, Pallas kernels for 8% -> 8%
where the time goes in v4:
time: 96.7 us; the launch traced here: 95.6 us
  starting transfers between devices  57.3 us (59%)
  waiting for transfers between devices  18 us (19%)
  Pallas kernels  13.9 us (14%)
  other arithmetic  3.31 us (3%)
  between operations  1.6 us (2%)
  local copies, waits for them, and re-layouts  1.4 us (1%)
    ppermute x7, starting transfers between devices, tensor_swap(): lax.ppermute(value, 'tensor', [(t, t ^ k) for t in range(lax.axis_size('t...  23.5 us
    ppermute x6, starting transfers between devices, chip_swap(): lax.ppermute(value, 'dp', [(r, r ^ 2 * k) for r in range(lax.axis_size('d...  18.9 us
    ppermute x6, waiting for transfers between devices, chip_swap(): lax.ppermute(value, 'dp', [(r, r ^ 2 * k) for r in range(lax.axis_size('d...  11.1 us
    ppermute x2, starting transfers between devices, core_swap(): lax.ppermute(value, 'dp', [(r, r ^ 1) for r in range(lax.axis_size('dp'))])  10.4 us
    pallas_call x2, Pallas kernels, update(): pl.pallas_call(functools.partial(update_kernel, scale, first), out_shape=...  8.86 us
    all_to_all x1, starting transfers between devices, body(): lax.all_to_all(share.reshape(members, share.shape[0] // members, features...  4.55 us
    ppermute x7, waiting for transfers between devices, tensor_swap(): lax.ppermute(value, 'tensor', [(t, t ^ k) for t in range(lax.axis_size('t...  3.8 us
    pallas_call x1, Pallas kernels, partials(): pl.pallas_call(functools.partial(partial_kernel, scale), out_shape=jax.Sh...  3.49 us
  transfers between devices with their start and end apart: 16, of which 10 were waited for; matrix products, arithmetic and copies ran while one was open for 4% of the time, Pallas kernels for 8%

profile of v4, /device:TPU:1, one launch (start us, length us, event | category | flops | bytes accessed | tf_op | source)
XLA Modules:
  0.0 95.6 jit_solution(813990887673123879)
XLA Ops:
  0.6 0.0 copy-start.9
  0.6 5.3 %collective-permute-start.2 = (bf16[640,256]{1,0:T(8,128)(2,1)}, bf16[640,256]{1,0:T(8,128)(2,1)S(1)}, u32[]{:S(2)}, u32[]{:S(2)}) collective-permute-start(bf16[640,256]{1,0:T(8,128)(2,1)} %refs_0_.1), channel_id=1, source_target_pairs={{0,3},{1,2},{2,1},{3,0},{4,7},{5,6},{6,5},{7,4},{8,11},{9,10},{10,... | collective-permute-start | bytes 983048 | tf_op jit(solution)/shard_map/ppermute | solution.py:28
  6.0 1.9 %collective-permute-start.1 = (bf16[640,256]{1,0:T(8,128)(2,1)}, bf16[640,256]{1,0:T(8,128)(2,1)S(1)}, u32[]{:S(2)}, u32[]{:S(2)}) collective-permute-start(bf16[640,256]{1,0:T(8,128)(2,1)} %refs_0_.1), channel_id=1, source_target_pairs={{0,1},{1,0},{2,3},{3,2},{4,5},{5,4},{6,7},{7,6},{8,9},{9,8},{10,11... | collective-permute-start | bytes 983048 | tf_op jit(solution)/shard_map/ppermute | solution.py:28
  7.9 3.2 %collective-permute-start = (bf16[640,256]{1,0:T(8,128)(2,1)}, bf16[640,256]{1,0:T(8,128)(2,1)S(1)}, u32[]{:S(2)}, u32[]{:S(2)}) collective-permute-start(bf16[640,256]{1,0:T(8,128)(2,1)} %refs_0_.1), channel_id=1, source_target_pairs={{0,4},{1,5},{2,6},{3,7},{4,0},{5,1},{6,2},{7,3},{8,12},{9,13},{10,... | collective-permute-start | bytes 983048 | tf_op jit(solution)/shard_map/ppermute | solution.py:28
  11.1 3.5 %shard_map.76 = bf16[640,2048]{1,0:T(8,128)(2,1)} custom-call(bf16[640,256]{1,0:T(8,128)(2,1)} %refs_4_.3, bf16[2048,256]{1,0:T(8,128)(2,1)} %bitcast.31), custom_call_target="tpu_custom_call" | custom-call | flops 1000 | bytes 1000 | tf_op jit(solution)/shard_map/pallas_call | solution.py:189
  14.6 0.0 collective-permute-done.2.refs_3_
  14.6 0.0 copy-start.10
  14.7 0.0 collective-permute-done.1.refs_2_
  14.7 0.0 copy-start.11
  14.7 1.7 %collective-permute-done.refs_1_ = bf16[640,256]{1,0:T(8,128)(2,1)S(1)} collective-permute-done((bf16[640,256]{1,0:T(8,128)(2,1)}, bf16[640,256]{1,0:T(8,128)(2,1)S(1)}, u32[]{:S(2)}, u32[]{:S(2)}) %collective-permute-start) | collective-permute-done | bytes 327712 | tf_op jit(solution)/shard_map/ppermute | solution.py:28
  16.4 0.0 copy-done.9
  16.4 0.0 copy-start.12
  16.4 4.1 %collective-permute-start.6 = (bf16[640,256]{1,0:T(8,128)(2,1)S(1)}, bf16[640,256]{1,0:T(8,128)(2,1)S(1)}, u32[]{:S(2)}, u32[]{:S(2)}) collective-permute-start(bf16[640,256]{1,0:T(8,128)(2,1)S(1)} %copy-done.9), channel_id=1, source_target_pairs={{0,6},{1,7},{2,4},{3,5},{4,2},{5,3},{6,0},{7,1},{8,14},{9,15},{10,... | collective-permute-start | bytes 983048 | tf_op jit(solution)/shard_map/ppermute | solution.py:28
  20.5 5.1 %collective-permute-start.5 = (bf16[640,256]{1,0:T(8,128)(2,1)S(1)}, bf16[640,256]{1,0:T(8,128)(2,1)S(1)}, u32[]{:S(2)}, u32[]{:S(2)}) collective-permute-start(bf16[640,256]{1,0:T(8,128)(2,1)S(1)} %collective-permute-done.refs_1_), channel_id=1, source_target_pairs={{0,3},{1,2},{2,1},{3,0},{4,7},{5,6},{6,5},{7,4},{8,11},{9,10},{10,... | collective-permute-start | bytes 983048 | tf_op jit(solution)/shard_map/ppermute | solution.py:28
  25.6 1.9 %collective-permute-start.3 = (bf16[640,256]{1,0:T(8,128)(2,1)S(1)}, bf16[640,256]{1,0:T(8,128)(2,1)S(1)}, u32[]{:S(2)}, u32[]{:S(2)}) collective-permute-start(bf16[640,256]{1,0:T(8,128)(2,1)S(1)} %collective-permute-done.1.refs_2_), channel_id=1, source_target_pairs={{0,4},{1,5},{2,6},{3,7},{4,0},{5,1},{6,2},{7,3},{8,12},{9,13},{10,... | collective-permute-start | bytes 983048 | tf_op jit(solution)/shard_map/ppermute | solution.py:28
  27.6 1.9 %collective-permute-start.4 = (bf16[640,256]{1,0:T(8,128)(2,1)S(1)}, bf16[640,256]{1,0:T(8,128)(2,1)S(1)}, u32[]{:S(2)}, u32[]{:S(2)}) collective-permute-start(bf16[640,256]{1,0:T(8,128)(2,1)S(1)} %collective-permute-done.2.refs_3_), channel_id=1, source_target_pairs={{0,1},{1,0},{2,3},{3,2},{4,5},{5,4},{6,7},{7,6},{8,9},{9,8},{10,11... | collective-permute-start | bytes 983048 | tf_op jit(solution)/shard_map/ppermute | solution.py:28
  30.2 0.6 stack.58.info
  30.8 0.0 copy-done.10
  30.8 0.0 copy-done.11
  30.8 0.0 copy-done.12
  30.8 4.4 %shard_map.77 = (bf16[2048,256]{1,0:T(8,128)(2,1)}, bf16[4,272,256]{2,1,0:T(8,128)(2,1)}, bf16[4,272,256]{2,1,0:T(8,128)(2,1)}, bf16[4,256,256]{2,1,0:T(8,128)(2,1)}) custom-call(s32[11]{0:T(128)} %stack.58.info, bf16[640,256]{1,0:T(8,128)(2,1)} %refs_0_.1, bf16[640,256]{1,0:T(8,128)(2,1)} %copy-done.12, bf16[640,256]{1,0:T(8,128)(2,1)} %copy-done.11, ...), custom_call_target="tpu_custom_call" | custom-call | flops 1000 | bytes 1000 | tf_op jit(solution)/shard_map/pallas_call | solution.py:130
  35.2 0.0 collective-permute-done.6.refs_3_
  35.2 0.0 copy-start.5
  35.3 0.5 collective-permute-done.5.refs_2_
  35.8 1.0 %collective-permute-done.3.refs_0_ = bf16[640,256]{1,0:T(8,128)(2,1)S(1)} collective-permute-done((bf16[640,256]{1,0:T(8,128)(2,1)S(1)}, bf16[640,256]{1,0:T(8,128)(2,1)S(1)}, u32[]{:S(2)}, u32[]{:S(2)}) %collective-permute-start.3) | collective-permute-done | bytes 327712 | tf_op jit(solution)/shard_map/ppermute | solution.py:28
  36.8 0.5 collective-permute-done.4.refs_1_
  37.3 0.0 copy-done.5
  37.3 0.0 copy-done.6
  37.3 0.2 copy-done.7
  37.5 0.6 copy-done.8
  38.0 4.4 %shard_map.78 = (bf16[2048,256]{1,0:T(8,128)(2,1)}, bf16[4,272,256]{2,1,0:T(8,128)(2,1)}, bf16[4,272,256]{2,1,0:T(8,128)(2,1)}, bf16[4,256,256]{2,1,0:T(8,128)(2,1)}) custom-call(s32[11]{0:T(128)} %stack.58.info, bf16[640,256]{1,0:T(8,128)(2,1)} %copy-done.7, ...), custom_call_target="tpu_custom_call", output_to_operand_aliasing={{0}: (8, {}), {1}: (9, {}), {2}: (10, {})} | custom-call | flops 1000 | bytes 1000 | tf_op jit(solution)/shard_map/pallas_call | solution.py:130
  42.5 0.0 copy-start.4
  42.5 0.0 copy-start.3
  42.5 4.6 %all-to-all-start = ((bf16[8,80,2048]{2,1,0:T(8,128)(2,1)}), bf16[8,80,2048]{2,1,0:T(8,128)(2,1)}, u32[]{:S(2)}, u32[]{:S(2)}) async-start(bf16[8,80,2048]{2,1,0:T(8,128)(2,1)} %bitcast.17), calls=%async_computation | async-start | bytes 5242880 | tf_op jit(solution)/shard_map/all_to_all | solution.py:283
  47.0 0.0 copy-done.4
  47.1 7.6 %collective-permute-start.7 = (bf16[4,272,256]{2,1,0:T(8,128)(2,1)S(1)}, bf16[4,272,256]{2,1,0:T(8,128)(2,1)S(1)}, u32[]{:S(2)}, u32[]{:S(2)}) collective-permute-start(bf16[4,272,256]{2,1,0:T(8,128)(2,1)S(1)} %copy-done.4), channel_id=1, source_target_pairs={{0,8},{8,0},{16,24},{24,16},{32,40},{40,32},{48,56},{56,48},{64,72... | collective-permute-start | bytes 1671176 | tf_op jit(solution)/shard_map/ppermute | solution.py:32
  54.7 1.6 %collective-permute-done.7 = bf16[4,272,256]{2,1,0:T(8,128)(2,1)S(1)} collective-permute-done((bf16[4,272,256]{2,1,0:T(8,128)(2,1)S(1)}, bf16[4,272,256]{2,1,0:T(8,128)(2,1)S(1)}, u32[]{:S(2)}, u32[]{:S(2)}) %collective-permute-start.7) | collective-permute-done | bytes 557088 | tf_op jit(solution)/shard_map/ppermute | solution.py:32
  56.3 0.0 copy-done.3
  56.3 0.1 fusion.4
  56.4 3.6 %collective-permute-start.8 = (bf16[272,256]{1,0:T(8,128)(2,1)S(1)}, bf16[272,256]{1,0:T(8,128)(2,1)S(1)}, u32[]{:S(2)}, u32[]{:S(2)}) collective-permute-start(bf16[272,256]{1,0:T(8,128)(2,1)S(1)} %get-tuple-element.49), channel_id=1, source_target_pairs={{0,32},{8,40},{16,48},{24,56},{32,0},{40,8},{48,16},{56,24},{64,96... | collective-permute-start | bytes 417800 | tf_op jit(solution)/shard_map/ppermute | solution.py:36
  60.0 4.0 %collective-permute-start.10 = (bf16[272,256]{1,0:T(8,128)(2,1)S(1)}, bf16[272,256]{1,0:T(8,128)(2,1)S(1)}, u32[]{:S(2)}, u32[]{:S(2)}) collective-permute-start(bf16[272,256]{1,0:T(8,128)(2,1)S(1)} %get-tuple-element.50), channel_id=1, source_target_pairs={{0,16},{8,24},{16,0},{24,8},{32,48},{40,56},{48,32},{56,40},{64,80... | collective-permute-start | bytes 417800 | tf_op jit(solution)/shard_map/ppermute | solution.py:36
  64.0 0.0 copy-start
  64.0 0.0 copy-start.1
  64.0 0.0 copy-start.2
  64.0 2.1 %collective-permute-start.9 = (bf16[272,256]{1,0:T(8,128)(2,1)S(1)}, bf16[272,256]{1,0:T(8,128)(2,1)S(1)}, u32[]{:S(2)}, u32[]{:S(2)}) collective-permute-start(bf16[272,256]{1,0:T(8,128)(2,1)S(1)} %get-tuple-element.51), channel_id=1, source_target_pairs={{0,48},{8,56},{16,32},{24,40},{32,16},{40,24},{48,0},{56,8},{64,11... | collective-permute-start | bytes 417800 | tf_op jit(solution)/shard_map/ppermute | solution.py:36
  66.1 1.1 %collective-permute-done.8 = bf16[272,256]{1,0:T(8,128)(2,1)S(1)} collective-permute-done((bf16[272,256]{1,0:T(8,128)(2,1)S(1)}, bf16[272,256]{1,0:T(8,128)(2,1)S(1)}, u32[]{:S(2)}, u32[]{:S(2)}) %collective-permute-start.8) | collective-permute-done | bytes 139296 | tf_op jit(solution)/shard_map/ppermute | solution.py:36
  67.2 2.3 %collective-permute-done.10 = bf16[272,256]{1,0:T(8,128)(2,1)S(1)} collective-permute-done((bf16[272,256]{1,0:T(8,128)(2,1)S(1)}, bf16[272,256]{1,0:T(8,128)(2,1)S(1)}, u32[]{:S(2)}, u32[]{:S(2)}) %collective-permute-start.10) | collective-permute-done | bytes 139296 | tf_op jit(solution)/shard_map/ppermute | solution.py:36
  69.4 2.8 %collective-permute-done.9 = bf16[272,256]{1,0:T(8,128)(2,1)S(1)} collective-permute-done((bf16[272,256]{1,0:T(8,128)(2,1)S(1)}, bf16[272,256]{1,0:T(8,128)(2,1)S(1)}, u32[]{:S(2)}, u32[]{:S(2)}) %collective-permute-start.9) | collective-permute-done | bytes 139296 | tf_op jit(solution)/shard_map/ppermute | solution.py:36
  72.3 0.1 fusion.1
  72.4 3.3 %collective-permute-start.13 = (bf16[256,256]{1,0:T(8,128)(2,1)S(1)}, bf16[256,256]{1,0:T(8,128)(2,1)S(1)}, u32[]{:S(2)}, u32[]{:S(2)}) collective-permute-start(bf16[256,256]{1,0:T(8,128)(2,1)S(1)} %fusion.2), channel_id=1, source_target_pairs={{0,48},{8,56},{16,32},{24,40},{32,16},{40,24},{48,0},{56,8},{64,11... | collective-permute-start | bytes 393224 | tf_op jit(solution)/shard_map/ppermute | solution.py:36
  75.7 3.6 %collective-permute-start.12 = (bf16[256,256]{1,0:T(8,128)(2,1)S(1)}, bf16[256,256]{1,0:T(8,128)(2,1)S(1)}, u32[]{:S(2)}, u32[]{:S(2)}) collective-permute-start(bf16[256,256]{1,0:T(8,128)(2,1)S(1)} %fusion.2), channel_id=1, source_target_pairs={{0,32},{8,40},{16,48},{24,56},{32,0},{40,8},{48,16},{56,24},{64,96... | collective-permute-start | bytes 393224 | tf_op jit(solution)/shard_map/ppermute | solution.py:36
  79.3 2.4 %collective-permute-start.11 = (bf16[256,256]{1,0:T(8,128)(2,1)S(1)}, bf16[256,256]{1,0:T(8,128)(2,1)S(1)}, u32[]{:S(2)}, u32[]{:S(2)}) collective-permute-start(bf16[256,256]{1,0:T(8,128)(2,1)S(1)} %fusion.2), channel_id=1, source_target_pairs={{0,16},{8,24},{16,0},{24,8},{32,48},{40,56},{48,32},{56,40},{64,80... | collective-permute-start | bytes 393224 | tf_op jit(solution)/shard_map/ppermute | solution.py:36
  81.7 0.0 all-to-all-done
  81.7 3.0 %reduce_sum.12 = bf16[80,2048]{1,0:T(8,128)(2,1)} reduce(bf16[8,80,2048]{2,1,0:T(8,128)(2,1)} %all-to-all-done, bf16[]{:T(256)} %constant.41.clone.1), dimensions={0}, to_apply=%region_0.1 | reduce | flops 1146880 | bytes 2949122 | tf_op jit(solution)/shard_map/reduce_sum | solution.py:295
  84.7 0.0 collective-permute-done.13
  84.7 4.9 %collective-permute-done.12 = bf16[256,256]{1,0:T(8,128)(2,1)S(1)} collective-permute-done((bf16[256,256]{1,0:T(8,128)(2,1)S(1)}, bf16[256,256]{1,0:T(8,128)(2,1)S(1)}, u32[]{:S(2)}, u32[]{:S(2)}) %collective-permute-start.12) | collective-permute-done | bytes 131104 | tf_op jit(solution)/shard_map/ppermute | solution.py:36
  89.6 0.0 collective-permute-done.11
  89.6 0.1 pad_maximum_fusion.mine
  89.7 2.7 %collective-permute-start.14 = (bf16[4,256,256]{2,1,0:T(8,128)(2,1)S(1)}, bf16[4,256,256]{2,1,0:T(8,128)(2,1)S(1)}, u32[]{:S(2)}, u32[]{:S(2)}) collective-permute-start(bf16[4,256,256]{2,1,0:T(8,128)(2,1)S(1)} %pad_maximum_fusion.mine), channel_id=1, source_target_pairs={{0,8},{8,0},{16,24},{24,16},{32,40},{40,32},{48,56},{56,48},{64,72... | collective-permute-start | bytes 1572872 | tf_op jit(solution)/shard_map/ppermute | solution.py:32
  92.5 1.5 %collective-permute-done.14.other = bf16[4,256,256]{2,1,0:T(8,128)(2,1)S(1)} collective-permute-done((bf16[4,256,256]{2,1,0:T(8,128)(2,1)S(1)}, bf16[4,256,256]{2,1,0:T(8,128)(2,1)S(1)}, u32[]{:S(2)}, u32[]{:S(2)}) %collective-permute-start.14) | collective-permute-done | bytes 524320 | tf_op jit(solution)/shard_map/ppermute | solution.py:32
  94.0 0.0 copy-done
  94.0 0.0 copy-done.1
  94.0 0.0 copy-done.2
  94.0 1.6 %shard_map.79 = bf16[2048,256]{1,0:T(8,128)(2,1)} custom-call(s32[11]{0:T(128)S(1)} %copy-done.2, bf16[4,256,256]{2,1,0:T(8,128)(2,1)S(1)} %copy-done, bf16[4,256,256]{2,1,0:T(8,128)(2,1)S(1)} %copy-done.1, bf16[4,256,256]{2,1,0:T(8,128)(2,1)S(1)} %pad_maximum_fusion.mine, bf16[4,256,256]{2,1,0:T(8,128)(2,1)S(1)} %collective-permute-done.14.other), custom_call_target="tpu_custom_call" | custom-call | flops 1000 | bytes 1000 | tf_op jit(solution)/shard_map/pallas_call | solution.py:235
  (5 shorter events, 0.0 us)
Async XLA Ops:
  0.6 15.8 %copy-start.9 = (bf16[640,256]{1,0:T(8,128)(2,1)S(1)}, bf16[640,256]{1,0:T(8,128)(2,1)}, u32[]{:S(2)}) copy-start(bf16[640,256]{1,0:T(8,128)(2,1)} %refs_0_.1) | copy-start | bytes 983044
  0.6 14.0 %collective-permute-start.2 = (bf16[640,256]{1,0:T(8,128)(2,1)}, bf16[640,256]{1,0:T(8,128)(2,1)S(1)}, u32[]{:S(2)}, u32[]{:S(2)}) collective-permute-start(bf16[640,256]{1,0:T(8,128)(2,1)} %refs_0_.1), channel_id=1, source_target_pairs={{0,3},{1,2},{2,1},{3,0},{4,7},{5,6},{6,5},{7,4},{8,11},{9,10},{10,... | collective-permute-start | bytes 983048 | tf_op jit(solution)/shard_map/ppermute | solution.py:28
  6.0 8.7 %collective-permute-start.1 = (bf16[640,256]{1,0:T(8,128)(2,1)}, bf16[640,256]{1,0:T(8,128)(2,1)S(1)}, u32[]{:S(2)}, u32[]{:S(2)}) collective-permute-start(bf16[640,256]{1,0:T(8,128)(2,1)} %refs_0_.1), channel_id=1, source_target_pairs={{0,1},{1,0},{2,3},{3,2},{4,5},{5,4},{6,7},{7,6},{8,9},{9,8},{10,11... | collective-permute-start | bytes 983048 | tf_op jit(solution)/shard_map/ppermute | solution.py:28
  7.9 8.5 %collective-permute-start = (bf16[640,256]{1,0:T(8,128)(2,1)}, bf16[640,256]{1,0:T(8,128)(2,1)S(1)}, u32[]{:S(2)}, u32[]{:S(2)}) collective-permute-start(bf16[640,256]{1,0:T(8,128)(2,1)} %refs_0_.1), channel_id=1, source_target_pairs={{0,4},{1,5},{2,6},{3,7},{4,0},{5,1},{6,2},{7,3},{8,12},{9,13},{10,... | collective-permute-start | bytes 983048 | tf_op jit(solution)/shard_map/ppermute | solution.py:28
  14.6 16.1 %copy-start.10 = (bf16[640,256]{1,0:T(8,128)(2,1)}, bf16[640,256]{1,0:T(8,128)(2,1)S(1)}, u32[]{:S(2)}) copy-start(bf16[640,256]{1,0:T(8,128)(2,1)S(1)} %collective-permute-done.2.refs_3_) | copy-start | bytes 983044
  14.7 16.1 %copy-start.11 = (bf16[640,256]{1,0:T(8,128)(2,1)}, bf16[640,256]{1,0:T(8,128)(2,1)S(1)}, u32[]{:S(2)}) copy-start(bf16[640,256]{1,0:T(8,128)(2,1)S(1)} %collective-permute-done.1.refs_2_) | copy-start | bytes 983044
  16.4 14.4 %copy-start.12 = (bf16[640,256]{1,0:T(8,128)(2,1)}, bf16[640,256]{1,0:T(8,128)(2,1)S(1)}, u32[]{:S(2)}) copy-start(bf16[640,256]{1,0:T(8,128)(2,1)S(1)} %collective-permute-done.refs_1_) | copy-start | bytes 983044
  16.4 18.8 %collective-permute-start.6 = (bf16[640,256]{1,0:T(8,128)(2,1)S(1)}, bf16[640,256]{1,0:T(8,128)(2,1)S(1)}, u32[]{:S(2)}, u32[]{:S(2)}) collective-permute-start(bf16[640,256]{1,0:T(8,128)(2,1)S(1)} %copy-done.9), channel_id=1, source_target_pairs={{0,6},{1,7},{2,4},{3,5},{4,2},{5,3},{6,0},{7,1},{8,14},{9,15},{10,... | collective-permute-start | bytes 983048 | tf_op jit(solution)/shard_map/ppermute | solution.py:28
  20.5 15.2 %collective-permute-start.5 = (bf16[640,256]{1,0:T(8,128)(2,1)S(1)}, bf16[640,256]{1,0:T(8,128)(2,1)S(1)}, u32[]{:S(2)}, u32[]{:S(2)}) collective-permute-start(bf16[640,256]{1,0:T(8,128)(2,1)S(1)} %collective-permute-done.refs_1_), channel_id=1, source_target_pairs={{0,3},{1,2},{2,1},{3,0},{4,7},{5,6},{6,5},{7,4},{8,11},{9,10},{10,... | collective-permute-start | bytes 983048 | tf_op jit(solution)/shard_map/ppermute | solution.py:28
  25.6 11.1 %collective-permute-start.3 = (bf16[640,256]{1,0:T(8,128)(2,1)S(1)}, bf16[640,256]{1,0:T(8,128)(2,1)S(1)}, u32[]{:S(2)}, u32[]{:S(2)}) collective-permute-start(bf16[640,256]{1,0:T(8,128)(2,1)S(1)} %collective-permute-done.1.refs_2_), channel_id=1, source_target_pairs={{0,4},{1,5},{2,6},{3,7},{4,0},{5,1},{6,2},{7,3},{8,12},{9,13},{10,... | collective-permute-start | bytes 983048 | tf_op jit(solution)/shard_map/ppermute | solution.py:28
  27.6 9.8 %collective-permute-start.4 = (bf16[640,256]{1,0:T(8,128)(2,1)S(1)}, bf16[640,256]{1,0:T(8,128)(2,1)S(1)}, u32[]{:S(2)}, u32[]{:S(2)}) collective-permute-start(bf16[640,256]{1,0:T(8,128)(2,1)S(1)} %collective-permute-done.2.refs_3_), channel_id=1, source_target_pairs={{0,1},{1,0},{2,3},{3,2},{4,5},{5,4},{6,7},{7,6},{8,9},{9,8},{10,11... | collective-permute-start | bytes 983048 | tf_op jit(solution)/shard_map/ppermute | solution.py:28
  35.2 2.1 %copy-start.5 = (bf16[640,256]{1,0:T(8,128)(2,1)}, bf16[640,256]{1,0:T(8,128)(2,1)S(1)}, u32[]{:S(2)}) copy-start(bf16[640,256]{1,0:T(8,128)(2,1)S(1)} %collective-permute-done.6.refs_3_) | copy-start | bytes 983044
  35.8 1.5 %copy-start.6 = (bf16[640,256]{1,0:T(8,128)(2,1)}, bf16[640,256]{1,0:T(8,128)(2,1)S(1)}, u32[]{:S(2)}) copy-start(bf16[640,256]{1,0:T(8,128)(2,1)S(1)} %collective-permute-done.5.refs_2_) | copy-start | bytes 983044
  36.8 0.7 copy-start.7
  37.3 0.7 copy-start.8
  42.5 4.6 %copy-start.4 = (bf16[4,272,256]{2,1,0:T(8,128)(2,1)S(1)}, bf16[4,272,256]{2,1,0:T(8,128)(2,1)}, u32[]{:S(2)}) copy-start(bf16[4,272,256]{2,1,0:T(8,128)(2,1)} %get-tuple-element.44) | copy-start | bytes 1671172
  42.5 13.8 %copy-start.3 = (bf16[4,272,256]{2,1,0:T(8,128)(2,1)S(1)}, bf16[4,272,256]{2,1,0:T(8,128)(2,1)}, u32[]{:S(2)}) copy-start(bf16[4,272,256]{2,1,0:T(8,128)(2,1)} %get-tuple-element.43) | copy-start | bytes 1671172
  42.5 39.2 %all-to-all-start = ((bf16[8,80,2048]{2,1,0:T(8,128)(2,1)}), bf16[8,80,2048]{2,1,0:T(8,128)(2,1)}, u32[]{:S(2)}, u32[]{:S(2)}) async-start(bf16[8,80,2048]{2,1,0:T(8,128)(2,1)} %bitcast.17), calls=%async_computation | async-start | bytes 5242880 | tf_op jit(solution)/shard_map/all_to_all | solution.py:283
  47.1 9.2 %collective-permute-start.7 = (bf16[4,272,256]{2,1,0:T(8,128)(2,1)S(1)}, bf16[4,272,256]{2,1,0:T(8,128)(2,1)S(1)}, u32[]{:S(2)}, u32[]{:S(2)}) collective-permute-start(bf16[4,272,256]{2,1,0:T(8,128)(2,1)S(1)} %copy-done.4), channel_id=1, source_target_pairs={{0,8},{8,0},{16,24},{24,16},{32,40},{40,32},{48,56},{56,48},{64,72... | collective-permute-start | bytes 1671176 | tf_op jit(solution)/shard_map/ppermute | solution.py:32
  56.4 10.8 %collective-permute-start.8 = (bf16[272,256]{1,0:T(8,128)(2,1)S(1)}, bf16[272,256]{1,0:T(8,128)(2,1)S(1)}, u32[]{:S(2)}, u32[]{:S(2)}) collective-permute-start(bf16[272,256]{1,0:T(8,128)(2,1)S(1)} %get-tuple-element.49), channel_id=1, source_target_pairs={{0,32},{8,40},{16,48},{24,56},{32,0},{40,8},{48,16},{56,24},{64,96... | collective-permute-start | bytes 417800 | tf_op jit(solution)/shard_map/ppermute | solution.py:36
  60.0 9.5 %collective-permute-start.10 = (bf16[272,256]{1,0:T(8,128)(2,1)S(1)}, bf16[272,256]{1,0:T(8,128)(2,1)S(1)}, u32[]{:S(2)}, u32[]{:S(2)}) collective-permute-start(bf16[272,256]{1,0:T(8,128)(2,1)S(1)} %get-tuple-element.50), channel_id=1, source_target_pairs={{0,16},{8,24},{16,0},{24,8},{32,48},{40,56},{48,32},{56,40},{64,80... | collective-permute-start | bytes 417800 | tf_op jit(solution)/shard_map/ppermute | solution.py:36
  64.0 30.0 %copy-start = (bf16[4,256,256]{2,1,0:T(8,128)(2,1)S(1)}, bf16[4,256,256]{2,1,0:T(8,128)(2,1)}, u32[]{:S(2)}) copy-start(bf16[4,256,256]{2,1,0:T(8,128)(2,1)} %get-tuple-element.29.own_1) | copy-start | bytes 1572868
  64.0 30.0 %copy-start.1 = (bf16[4,256,256]{2,1,0:T(8,128)(2,1)S(1)}, bf16[4,256,256]{2,1,0:T(8,128)(2,1)}, u32[]{:S(2)}) copy-start(bf16[4,256,256]{2,1,0:T(8,128)(2,1)} %get-tuple-element.42.own_2) | copy-start | bytes 1572868
  64.0 30.0 %copy-start.2 = (s32[11]{0:T(128)S(1)}, s32[11]{0:T(128)}, u32[]{:S(2)}) copy-start(s32[11]{0:T(128)} %stack.58.info) | copy-start | bytes 136
  64.0 8.3 %collective-permute-start.9 = (bf16[272,256]{1,0:T(8,128)(2,1)S(1)}, bf16[272,256]{1,0:T(8,128)(2,1)S(1)}, u32[]{:S(2)}, u32[]{:S(2)}) collective-permute-start(bf16[272,256]{1,0:T(8,128)(2,1)S(1)} %get-tuple-element.51), channel_id=1, source_target_pairs={{0,48},{8,56},{16,32},{24,40},{32,16},{40,24},{48,0},{56,8},{64,11... | collective-permute-start | bytes 417800 | tf_op jit(solution)/shard_map/ppermute | solution.py:36
  72.4 12.3 %collective-permute-start.13 = (bf16[256,256]{1,0:T(8,128)(2,1)S(1)}, bf16[256,256]{1,0:T(8,128)(2,1)S(1)}, u32[]{:S(2)}, u32[]{:S(2)}) collective-permute-start(bf16[256,256]{1,0:T(8,128)(2,1)S(1)} %fusion.2), channel_id=1, source_target_pairs={{0,48},{8,56},{16,32},{24,40},{32,16},{40,24},{48,0},{56,8},{64,11... | collective-permute-start | bytes 393224 | tf_op jit(solution)/shard_map/ppermute | solution.py:36
  75.7 14.0 %collective-permute-start.12 = (bf16[256,256]{1,0:T(8,128)(2,1)S(1)}, bf16[256,256]{1,0:T(8,128)(2,1)S(1)}, u32[]{:S(2)}, u32[]{:S(2)}) collective-permute-start(bf16[256,256]{1,0:T(8,128)(2,1)S(1)} %fusion.2), channel_id=1, source_target_pairs={{0,32},{8,40},{16,48},{24,56},{32,0},{40,8},{48,16},{56,24},{64,96... | collective-permute-start | bytes 393224 | tf_op jit(solution)/shard_map/ppermute | solution.py:36
  79.3 10.3 %collective-permute-start.11 = (bf16[256,256]{1,0:T(8,128)(2,1)S(1)}, bf16[256,256]{1,0:T(8,128)(2,1)S(1)}, u32[]{:S(2)}, u32[]{:S(2)}) collective-permute-start(bf16[256,256]{1,0:T(8,128)(2,1)S(1)} %fusion.2), channel_id=1, source_target_pairs={{0,16},{8,24},{16,0},{24,8},{32,48},{40,56},{48,32},{56,40},{64,80... | collective-permute-start | bytes 393224 | tf_op jit(solution)/shard_map/ppermute | solution.py:36
  89.7 4.3 %collective-permute-start.14 = (bf16[4,256,256]{2,1,0:T(8,128)(2,1)S(1)}, bf16[4,256,256]{2,1,0:T(8,128)(2,1)S(1)}, u32[]{:S(2)}, u32[]{:S(2)}) collective-permute-start(bf16[4,256,256]{2,1,0:T(8,128)(2,1)S(1)} %pad_maximum_fusion.mine), channel_id=1, source_target_pairs={{0,8},{8,0},{16,24},{24,16},{32,40},{40,32},{48,56},{56,48},{64,72... | collective-permute-start | bytes 1572872 | tf_op jit(solution)/shard_map/ppermute | solution.py:32

commit v5 on v4

--- a/solution.py
+++ b/solution.py
@@ -257,7 +257,7 @@
     a_p = tensor_swap(activations, 1)
     a_q = tensor_swap(activations, 3)
     share = partials(scale, cotangent, weight)
-    a_y, a_p, a_q, share = lax.optimization_barrier((a_y, a_p, a_q, share))
+    a_y, a_p, a_q, share, info = lax.optimization_barrier((a_y, a_p, a_q, share, info))
 
     a_yp = tensor_swap(a_p, 4)
     a_pq = tensor_swap(a_q, 1)

time: 96.7 us -> 96.7 us (level)
  no operation moved by 1% of the time
where the time goes in v5:
time: 96.7 us; the launch traced here: 95.6 us
  starting transfers between devices  57.3 us (59%)
  waiting for transfers between devices  18 us (19%)
  Pallas kernels  13.9 us (14%)
  other arithmetic  3.31 us (3%)
  between operations  1.61 us (2%)
  local copies, waits for them, and re-layouts  1.39 us (1%)
    ppermute x7, starting transfers between devices, tensor_swap(): lax.ppermute(value, 'tensor', [(t, t ^ k) for t in range(lax.axis_size('t...  23.5 us
    ppermute x6, starting transfers between devices, chip_swap(): lax.ppermute(value, 'dp', [(r, r ^ 2 * k) for r in range(lax.axis_size('d...  19.4 us
    ppermute x6, waiting for transfers between devices, chip_swap(): lax.ppermute(value, 'dp', [(r, r ^ 2 * k) for r in range(lax.axis_size('d...  11.1 us
    ppermute x2, starting transfers between devices, core_swap(): lax.ppermute(value, 'dp', [(r, r ^ 1) for r in range(lax.axis_size('dp'))])  9.89 us
    pallas_call x2, Pallas kernels, update(): pl.pallas_call(functools.partial(update_kernel, scale, first), out_shape=...  8.86 us
    all_to_all x1, starting transfers between devices, body(): lax.all_to_all(share.reshape(members, share.shape[0] // members, features...  4.55 us
    ppermute x7, waiting for transfers between devices, tensor_swap(): lax.ppermute(value, 'tensor', [(t, t ^ k) for t in range(lax.axis_size('t...  3.79 us
    pallas_call x1, Pallas kernels, partials(): pl.pallas_call(functools.partial(partial_kernel, scale), out_shape=jax.Sh...  3.49 us
  transfers between devices with their start and end apart: 16, of which 10 were waited for; matrix products, arithmetic and copies ran while one was open for 4% of the time, Pallas kernels for 8%

profile of v5, /device:TPU:1, one launch (start us, length us, event | category | flops | bytes accessed | tf_op | source)
XLA Modules:
  0.0 95.6 jit_solution(18249976068523498634)
XLA Ops:
  0.6 0.0 copy-start.9
  0.6 5.3 %collective-permute-start.2 = (bf16[640,256]{1,0:T(8,128)(2,1)}, bf16[640,256]{1,0:T(8,128)(2,1)S(1)}, u32[]{:S(2)}, u32[]{:S(2)}) collective-permute-start(bf16[640,256]{1,0:T(8,128)(2,1)} %refs_0_.1), channel_id=1, source_target_pairs={{0,3},{1,2},{2,1},{3,0},{4,7},{5,6},{6,5},{7,4},{8,11},{9,10},{10,... | collective-permute-start | bytes 983048 | tf_op jit(solution)/shard_map/ppermute | solution.py:28
  6.0 1.9 %collective-permute-start.1 = (bf16[640,256]{1,0:T(8,128)(2,1)}, bf16[640,256]{1,0:T(8,128)(2,1)S(1)}, u32[]{:S(2)}, u32[]{:S(2)}) collective-permute-start(bf16[640,256]{1,0:T(8,128)(2,1)} %refs_0_.1), channel_id=1, source_target_pairs={{0,1},{1,0},{2,3},{3,2},{4,5},{5,4},{6,7},{7,6},{8,9},{9,8},{10,11... | collective-permute-start | bytes 983048 | tf_op jit(solution)/shard_map/ppermute | solution.py:28
  7.9 3.2 %collective-permute-start = (bf16[640,256]{1,0:T(8,128)(2,1)}, bf16[640,256]{1,0:T(8,128)(2,1)S(1)}, u32[]{:S(2)}, u32[]{:S(2)}) collective-permute-start(bf16[640,256]{1,0:T(8,128)(2,1)} %refs_0_.1), channel_id=1, source_target_pairs={{0,4},{1,5},{2,6},{3,7},{4,0},{5,1},{6,2},{7,3},{8,12},{9,13},{10,... | collective-permute-start | bytes 983048 | tf_op jit(solution)/shard_map/ppermute | solution.py:28
  11.1 3.5 %shard_map.76 = bf16[640,2048]{1,0:T(8,128)(2,1)} custom-call(bf16[640,256]{1,0:T(8,128)(2,1)} %refs_4_.3, bf16[2048,256]{1,0:T(8,128)(2,1)} %bitcast.31), custom_call_target="tpu_custom_call" | custom-call | flops 1000 | bytes 1000 | tf_op jit(solution)/shard_map/pallas_call | solution.py:189
  15.3 0.6 stack.58.info
  15.9 0.0 collective-permute-done.2.refs_3_
  15.9 0.0 copy-start.10
  15.9 0.0 collective-permute-done.1.refs_2_
  15.9 0.0 copy-start.11
  15.9 0.5 collective-permute-done.refs_1_
  16.4 0.0 copy-done.9
  16.4 0.0 copy-start.12
  16.4 4.1 %collective-permute-start.6 = (bf16[640,256]{1,0:T(8,128)(2,1)S(1)}, bf16[640,256]{1,0:T(8,128)(2,1)S(1)}, u32[]{:S(2)}, u32[]{:S(2)}) collective-permute-start(bf16[640,256]{1,0:T(8,128)(2,1)S(1)} %copy-done.9), channel_id=1, source_target_pairs={{0,6},{1,7},{2,4},{3,5},{4,2},{5,3},{6,0},{7,1},{8,14},{9,15},{10,... | collective-permute-start | bytes 983048 | tf_op jit(solution)/shard_map/ppermute | solution.py:28
  20.5 5.1 %collective-permute-start.5 = (bf16[640,256]{1,0:T(8,128)(2,1)S(1)}, bf16[640,256]{1,0:T(8,128)(2,1)S(1)}, u32[]{:S(2)}, u32[]{:S(2)}) collective-permute-start(bf16[640,256]{1,0:T(8,128)(2,1)S(1)} %collective-permute-done.refs_1_), channel_id=1, source_target_pairs={{0,3},{1,2},{2,1},{3,0},{4,7},{5,6},{6,5},{7,4},{8,11},{9,10},{10,... | collective-permute-start | bytes 983048 | tf_op jit(solution)/shard_map/ppermute | solution.py:28
  25.6 1.9 %collective-permute-start.3 = (bf16[640,256]{1,0:T(8,128)(2,1)S(1)}, bf16[640,256]{1,0:T(8,128)(2,1)S(1)}, u32[]{:S(2)}, u32[]{:S(2)}) collective-permute-start(bf16[640,256]{1,0:T(8,128)(2,1)S(1)} %collective-permute-done.1.refs_2_), channel_id=1, source_target_pairs={{0,4},{1,5},{2,6},{3,7},{4,0},{5,1},{6,2},{7,3},{8,12},{9,13},{10,... | collective-permute-start | bytes 983048 | tf_op jit(solution)/shard_map/ppermute | solution.py:28
  27.6 1.9 %collective-permute-start.4 = (bf16[640,256]{1,0:T(8,128)(2,1)S(1)}, bf16[640,256]{1,0:T(8,128)(2,1)S(1)}, u32[]{:S(2)}, u32[]{:S(2)}) collective-permute-start(bf16[640,256]{1,0:T(8,128)(2,1)S(1)} %collective-permute-done.2.refs_3_), channel_id=1, source_target_pairs={{0,1},{1,0},{2,3},{3,2},{4,5},{5,4},{6,7},{7,6},{8,9},{9,8},{10,11... | collective-permute-start | bytes 983048 | tf_op jit(solution)/shard_map/ppermute | solution.py:28
  29.5 0.0 copy-done.10
  29.5 0.0 copy-done.11
  29.5 0.0 copy-done.12
  29.5 4.5 %shard_map.77 = (bf16[2048,256]{1,0:T(8,128)(2,1)}, bf16[4,272,256]{2,1,0:T(8,128)(2,1)}, bf16[4,272,256]{2,1,0:T(8,128)(2,1)}, bf16[4,256,256]{2,1,0:T(8,128)(2,1)}) custom-call(s32[11]{0:T(128)} %stack.58.info, bf16[640,256]{1,0:T(8,128)(2,1)} %refs_0_.1, bf16[640,256]{1,0:T(8,128)(2,1)} %copy-done.12, bf16[640,256]{1,0:T(8,128)(2,1)} %copy-done.11, ...), custom_call_target="tpu_custom_call" | custom-call | flops 1000 | bytes 1000 | tf_op jit(solution)/shard_map/pallas_call | solution.py:130
  34.0 0.0 collective-permute-done.6.refs_3_
  34.0 0.0 copy-start.5
  34.0 1.8 %collective-permute-done.5.refs_2_ = bf16[640,256]{1,0:T(8,128)(2,1)S(1)} collective-permute-done((bf16[640,256]{1,0:T(8,128)(2,1)S(1)}, bf16[640,256]{1,0:T(8,128)(2,1)S(1)}, u32[]{:S(2)}, u32[]{:S(2)}) %collective-permute-start.5) | collective-permute-done | bytes 327712 | tf_op jit(solution)/shard_map/ppermute | solution.py:28
  35.8 1.0 %collective-permute-done.3.refs_0_ = bf16[640,256]{1,0:T(8,128)(2,1)S(1)} collective-permute-done((bf16[640,256]{1,0:T(8,128)(2,1)S(1)}, bf16[640,256]{1,0:T(8,128)(2,1)S(1)}, u32[]{:S(2)}, u32[]{:S(2)}) %collective-permute-start.3) | collective-permute-done | bytes 327712 | tf_op jit(solution)/shard_map/ppermute | solution.py:28
  36.8 0.5 collective-permute-done.4.refs_1_
  37.3 0.0 copy-done.5
  37.3 0.0 copy-done.6
  37.3 0.2 copy-done.7
  37.5 0.6 copy-done.8
  38.0 4.4 %shard_map.78 = (bf16[2048,256]{1,0:T(8,128)(2,1)}, bf16[4,272,256]{2,1,0:T(8,128)(2,1)}, bf16[4,272,256]{2,1,0:T(8,128)(2,1)}, bf16[4,256,256]{2,1,0:T(8,128)(2,1)}) custom-call(s32[11]{0:T(128)} %stack.58.info, bf16[640,256]{1,0:T(8,128)(2,1)} %copy-done.7, ...), custom_call_target="tpu_custom_call", output_to_operand_aliasing={{0}: (8, {}), {1}: (9, {}), {2}: (10, {})} | custom-call | flops 1000 | bytes 1000 | tf_op jit(solution)/shard_map/pallas_call | solution.py:130
  42.5 0.0 copy-start.4
  42.5 0.0 copy-start.3
  42.5 4.6 %all-to-all-start = ((bf16[8,80,2048]{2,1,0:T(8,128)(2,1)}), bf16[8,80,2048]{2,1,0:T(8,128)(2,1)}, u32[]{:S(2)}, u32[]{:S(2)}) async-start(bf16[8,80,2048]{2,1,0:T(8,128)(2,1)} %bitcast.17), calls=%async_computation | async-start | bytes 5242880 | tf_op jit(solution)/shard_map/all_to_all | solution.py:283
  47.0 0.0 copy-done.4
  47.1 7.1 %collective-permute-start.7 = (bf16[4,272,256]{2,1,0:T(8,128)(2,1)S(1)}, bf16[4,272,256]{2,1,0:T(8,128)(2,1)S(1)}, u32[]{:S(2)}, u32[]{:S(2)}) collective-permute-start(bf16[4,272,256]{2,1,0:T(8,128)(2,1)S(1)} %copy-done.4), channel_id=1, source_target_pairs={{0,8},{8,0},{16,24},{24,16},{32,40},{40,32},{48,56},{56,48},{64,72... | collective-permute-start | bytes 1671176 | tf_op jit(solution)/shard_map/ppermute | solution.py:32
  54.2 1.6 %collective-permute-done.7 = bf16[4,272,256]{2,1,0:T(8,128)(2,1)S(1)} collective-permute-done((bf16[4,272,256]{2,1,0:T(8,128)(2,1)S(1)}, bf16[4,272,256]{2,1,0:T(8,128)(2,1)S(1)}, u32[]{:S(2)}, u32[]{:S(2)}) %collective-permute-start.7) | collective-permute-done | bytes 557088 | tf_op jit(solution)/shard_map/ppermute | solution.py:32
  55.8 0.0 copy-done.3
  55.8 0.1 fusion.4
  55.9 4.1 %collective-permute-start.8 = (bf16[272,256]{1,0:T(8,128)(2,1)S(1)}, bf16[272,256]{1,0:T(8,128)(2,1)S(1)}, u32[]{:S(2)}, u32[]{:S(2)}) collective-permute-start(bf16[272,256]{1,0:T(8,128)(2,1)S(1)} %get-tuple-element.51), channel_id=1, source_target_pairs={{0,32},{8,40},{16,48},{24,56},{32,0},{40,8},{48,16},{56,24},{64,96... | collective-permute-start | bytes 417800 | tf_op jit(solution)/shard_map/ppermute | solution.py:36
  60.0 4.0 %collective-permute-start.10 = (bf16[272,256]{1,0:T(8,128)(2,1)S(1)}, bf16[272,256]{1,0:T(8,128)(2,1)S(1)}, u32[]{:S(2)}, u32[]{:S(2)}) collective-permute-start(bf16[272,256]{1,0:T(8,128)(2,1)S(1)} %get-tuple-element.52), channel_id=1, source_target_pairs={{0,16},{8,24},{16,0},{24,8},{32,48},{40,56},{48,32},{56,40},{64,80... | collective-permute-start | bytes 417800 | tf_op jit(solution)/shard_map/ppermute | solution.py:36
  64.0 0.0 copy-start
  64.0 0.0 copy-start.1
  64.0 0.0 copy-start.2
  64.0 2.1 %collective-permute-start.9 = (bf16[272,256]{1,0:T(8,128)(2,1)S(1)}, bf16[272,256]{1,0:T(8,128)(2,1)S(1)}, u32[]{:S(2)}, u32[]{:S(2)}) collective-permute-start(bf16[272,256]{1,0:T(8,128)(2,1)S(1)} %get-tuple-element.53), channel_id=1, source_target_pairs={{0,48},{8,56},{16,32},{24,40},{32,16},{40,24},{48,0},{56,8},{64,11... | collective-permute-start | bytes 417800 | tf_op jit(solution)/shard_map/ppermute | solution.py:36
  66.1 0.6 collective-permute-done.8
  66.7 2.3 %collective-permute-done.10 = bf16[272,256]{1,0:T(8,128)(2,1)S(1)} collective-permute-done((bf16[272,256]{1,0:T(8,128)(2,1)S(1)}, bf16[272,256]{1,0:T(8,128)(2,1)S(1)}, u32[]{:S(2)}, u32[]{:S(2)}) %collective-permute-start.10) | collective-permute-done | bytes 139296 | tf_op jit(solution)/shard_map/ppermute | solution.py:36
  68.9 3.3 %collective-permute-done.9 = bf16[272,256]{1,0:T(8,128)(2,1)S(1)} collective-permute-done((bf16[272,256]{1,0:T(8,128)(2,1)S(1)}, bf16[272,256]{1,0:T(8,128)(2,1)S(1)}, u32[]{:S(2)}, u32[]{:S(2)}) %collective-permute-start.9) | collective-permute-done | bytes 139296 | tf_op jit(solution)/shard_map/ppermute | solution.py:36
  72.3 0.1 fusion.1
  72.4 3.3 %collective-permute-start.13 = (bf16[256,256]{1,0:T(8,128)(2,1)S(1)}, bf16[256,256]{1,0:T(8,128)(2,1)S(1)}, u32[]{:S(2)}, u32[]{:S(2)}) collective-permute-start(bf16[256,256]{1,0:T(8,128)(2,1)S(1)} %fusion.2), channel_id=1, source_target_pairs={{0,48},{8,56},{16,32},{24,40},{32,16},{40,24},{48,0},{56,8},{64,11... | collective-permute-start | bytes 393224 | tf_op jit(solution)/shard_map/ppermute | solution.py:36
  75.7 3.6 %collective-permute-start.12 = (bf16[256,256]{1,0:T(8,128)(2,1)S(1)}, bf16[256,256]{1,0:T(8,128)(2,1)S(1)}, u32[]{:S(2)}, u32[]{:S(2)}) collective-permute-start(bf16[256,256]{1,0:T(8,128)(2,1)S(1)} %fusion.2), channel_id=1, source_target_pairs={{0,32},{8,40},{16,48},{24,56},{32,0},{40,8},{48,16},{56,24},{64,96... | collective-permute-start | bytes 393224 | tf_op jit(solution)/shard_map/ppermute | solution.py:36
  79.3 2.4 %collective-permute-start.11 = (bf16[256,256]{1,0:T(8,128)(2,1)S(1)}, bf16[256,256]{1,0:T(8,128)(2,1)S(1)}, u32[]{:S(2)}, u32[]{:S(2)}) collective-permute-start(bf16[256,256]{1,0:T(8,128)(2,1)S(1)} %fusion.2), channel_id=1, source_target_pairs={{0,16},{8,24},{16,0},{24,8},{32,48},{40,56},{48,32},{56,40},{64,80... | collective-permute-start | bytes 393224 | tf_op jit(solution)/shard_map/ppermute | solution.py:36
  81.7 0.0 all-to-all-done
  81.7 3.0 %reduce_sum.12 = bf16[80,2048]{1,0:T(8,128)(2,1)} reduce(bf16[8,80,2048]{2,1,0:T(8,128)(2,1)} %all-to-all-done, bf16[]{:T(256)} %constant.41.clone.1), dimensions={0}, to_apply=%region_0.1 | reduce | flops 1146880 | bytes 2949122 | tf_op jit(solution)/shard_map/reduce_sum | solution.py:295
  84.7 0.0 collective-permute-done.13
  84.7 4.9 %collective-permute-done.12 = bf16[256,256]{1,0:T(8,128)(2,1)S(1)} collective-permute-done((bf16[256,256]{1,0:T(8,128)(2,1)S(1)}, bf16[256,256]{1,0:T(8,128)(2,1)S(1)}, u32[]{:S(2)}, u32[]{:S(2)}) %collective-permute-start.12) | collective-permute-done | bytes 131104 | tf_op jit(solution)/shard_map/ppermute | solution.py:36
  89.6 0.0 collective-permute-done.11
  89.6 0.1 pad_maximum_fusion.mine
  89.7 2.7 %collective-permute-start.14 = (bf16[4,256,256]{2,1,0:T(8,128)(2,1)S(1)}, bf16[4,256,256]{2,1,0:T(8,128)(2,1)S(1)}, u32[]{:S(2)}, u32[]{:S(2)}) collective-permute-start(bf16[4,256,256]{2,1,0:T(8,128)(2,1)S(1)} %pad_maximum_fusion.mine), channel_id=1, source_target_pairs={{0,8},{8,0},{16,24},{24,16},{32,40},{40,32},{48,56},{56,48},{64,72... | collective-permute-start | bytes 1572872 | tf_op jit(solution)/shard_map/ppermute | solution.py:32
  92.5 1.5 %collective-permute-done.14.other = bf16[4,256,256]{2,1,0:T(8,128)(2,1)S(1)} collective-permute-done((bf16[4,256,256]{2,1,0:T(8,128)(2,1)S(1)}, bf16[4,256,256]{2,1,0:T(8,128)(2,1)S(1)}, u32[]{:S(2)}, u32[]{:S(2)}) %collective-permute-start.14) | collective-permute-done | bytes 524320 | tf_op jit(solution)/shard_map/ppermute | solution.py:32
  94.0 0.0 copy-done
  94.0 0.0 copy-done.1
  94.0 0.0 copy-done.2
  94.0 1.6 %shard_map.79 = bf16[2048,256]{1,0:T(8,128)(2,1)} custom-call(s32[11]{0:T(128)S(1)} %copy-done.2, bf16[4,256,256]{2,1,0:T(8,128)(2,1)S(1)} %copy-done, bf16[4,256,256]{2,1,0:T(8,128)(2,1)S(1)} %copy-done.1, bf16[4,256,256]{2,1,0:T(8,128)(2,1)S(1)} %pad_maximum_fusion.mine, bf16[4,256,256]{2,1,0:T(8,128)(2,1)S(1)} %collective-permute-done.14.other), custom_call_target="tpu_custom_call" | custom-call | flops 1000 | bytes 1000 | tf_op jit(solution)/shard_map/pallas_call | solution.py:235
  (5 shorter events, 0.0 us)
Async XLA Ops:
  0.6 15.8 %copy-start.9 = (bf16[640,256]{1,0:T(8,128)(2,1)S(1)}, bf16[640,256]{1,0:T(8,128)(2,1)}, u32[]{:S(2)}) copy-start(bf16[640,256]{1,0:T(8,128)(2,1)} %refs_0_.1) | copy-start | bytes 983044
  0.6 15.3 %collective-permute-start.2 = (bf16[640,256]{1,0:T(8,128)(2,1)}, bf16[640,256]{1,0:T(8,128)(2,1)S(1)}, u32[]{:S(2)}, u32[]{:S(2)}) collective-permute-start(bf16[640,256]{1,0:T(8,128)(2,1)} %refs_0_.1), channel_id=1, source_target_pairs={{0,3},{1,2},{2,1},{3,0},{4,7},{5,6},{6,5},{7,4},{8,11},{9,10},{10,... | collective-permute-start | bytes 983048 | tf_op jit(solution)/shard_map/ppermute | solution.py:28
  6.0 9.9 %collective-permute-start.1 = (bf16[640,256]{1,0:T(8,128)(2,1)}, bf16[640,256]{1,0:T(8,128)(2,1)S(1)}, u32[]{:S(2)}, u32[]{:S(2)}) collective-permute-start(bf16[640,256]{1,0:T(8,128)(2,1)} %refs_0_.1), channel_id=1, source_target_pairs={{0,1},{1,0},{2,3},{3,2},{4,5},{5,4},{6,7},{7,6},{8,9},{9,8},{10,11... | collective-permute-start | bytes 983048 | tf_op jit(solution)/shard_map/ppermute | solution.py:28
  7.9 8.5 %collective-permute-start = (bf16[640,256]{1,0:T(8,128)(2,1)}, bf16[640,256]{1,0:T(8,128)(2,1)S(1)}, u32[]{:S(2)}, u32[]{:S(2)}) collective-permute-start(bf16[640,256]{1,0:T(8,128)(2,1)} %refs_0_.1), channel_id=1, source_target_pairs={{0,4},{1,5},{2,6},{3,7},{4,0},{5,1},{6,2},{7,3},{8,12},{9,13},{10,... | collective-permute-start | bytes 983048 | tf_op jit(solution)/shard_map/ppermute | solution.py:28
  15.9 13.6 %copy-start.10 = (bf16[640,256]{1,0:T(8,128)(2,1)}, bf16[640,256]{1,0:T(8,128)(2,1)S(1)}, u32[]{:S(2)}) copy-start(bf16[640,256]{1,0:T(8,128)(2,1)S(1)} %collective-permute-done.2.refs_3_) | copy-start | bytes 983044
  15.9 13.6 %copy-start.11 = (bf16[640,256]{1,0:T(8,128)(2,1)}, bf16[640,256]{1,0:T(8,128)(2,1)S(1)}, u32[]{:S(2)}) copy-start(bf16[640,256]{1,0:T(8,128)(2,1)S(1)} %collective-permute-done.1.refs_2_) | copy-start | bytes 983044
  16.4 13.1 %copy-start.12 = (bf16[640,256]{1,0:T(8,128)(2,1)}, bf16[640,256]{1,0:T(8,128)(2,1)S(1)}, u32[]{:S(2)}) copy-start(bf16[640,256]{1,0:T(8,128)(2,1)S(1)} %collective-permute-done.refs_1_) | copy-start | bytes 983044
  16.4 17.6 %collective-permute-start.6 = (bf16[640,256]{1,0:T(8,128)(2,1)S(1)}, bf16[640,256]{1,0:T(8,128)(2,1)S(1)}, u32[]{:S(2)}, u32[]{:S(2)}) collective-permute-start(bf16[640,256]{1,0:T(8,128)(2,1)S(1)} %copy-done.9), channel_id=1, source_target_pairs={{0,6},{1,7},{2,4},{3,5},{4,2},{5,3},{6,0},{7,1},{8,14},{9,15},{10,... | collective-permute-start | bytes 983048 | tf_op jit(solution)/shard_map/ppermute | solution.py:28
  20.5 15.2 %collective-permute-start.5 = (bf16[640,256]{1,0:T(8,128)(2,1)S(1)}, bf16[640,256]{1,0:T(8,128)(2,1)S(1)}, u32[]{:S(2)}, u32[]{:S(2)}) collective-permute-start(bf16[640,256]{1,0:T(8,128)(2,1)S(1)} %collective-permute-done.refs_1_), channel_id=1, source_target_pairs={{0,3},{1,2},{2,1},{3,0},{4,7},{5,6},{6,5},{7,4},{8,11},{9,10},{10,... | collective-permute-start | bytes 983048 | tf_op jit(solution)/shard_map/ppermute | solution.py:28
  25.6 11.1 %collective-permute-start.3 = (bf16[640,256]{1,0:T(8,128)(2,1)S(1)}, bf16[640,256]{1,0:T(8,128)(2,1)S(1)}, u32[]{:S(2)}, u32[]{:S(2)}) collective-permute-start(bf16[640,256]{1,0:T(8,128)(2,1)S(1)} %collective-permute-done.1.refs_2_), channel_id=1, source_target_pairs={{0,4},{1,5},{2,6},{3,7},{4,0},{5,1},{6,2},{7,3},{8,12},{9,13},{10,... | collective-permute-start | bytes 983048 | tf_op jit(solution)/shard_map/ppermute | solution.py:28
  27.6 9.8 %collective-permute-start.4 = (bf16[640,256]{1,0:T(8,128)(2,1)S(1)}, bf16[640,256]{1,0:T(8,128)(2,1)S(1)}, u32[]{:S(2)}, u32[]{:S(2)}) collective-permute-start(bf16[640,256]{1,0:T(8,128)(2,1)S(1)} %collective-permute-done.2.refs_3_), channel_id=1, source_target_pairs={{0,1},{1,0},{2,3},{3,2},{4,5},{5,4},{6,7},{7,6},{8,9},{9,8},{10,11... | collective-permute-start | bytes 983048 | tf_op jit(solution)/shard_map/ppermute | solution.py:28
  34.0 3.3 %copy-start.5 = (bf16[640,256]{1,0:T(8,128)(2,1)}, bf16[640,256]{1,0:T(8,128)(2,1)S(1)}, u32[]{:S(2)}) copy-start(bf16[640,256]{1,0:T(8,128)(2,1)S(1)} %collective-permute-done.6.refs_3_) | copy-start | bytes 983044
  35.8 1.5 %copy-start.6 = (bf16[640,256]{1,0:T(8,128)(2,1)}, bf16[640,256]{1,0:T(8,128)(2,1)S(1)}, u32[]{:S(2)}) copy-start(bf16[640,256]{1,0:T(8,128)(2,1)S(1)} %collective-permute-done.5.refs_2_) | copy-start | bytes 983044
  36.8 0.7 copy-start.7
  37.3 0.7 copy-start.8
  42.5 4.6 %copy-start.4 = (bf16[4,272,256]{2,1,0:T(8,128)(2,1)S(1)}, bf16[4,272,256]{2,1,0:T(8,128)(2,1)}, u32[]{:S(2)}) copy-start(bf16[4,272,256]{2,1,0:T(8,128)(2,1)} %get-tuple-element.46) | copy-start | bytes 1671172
  42.5 13.3 %copy-start.3 = (bf16[4,272,256]{2,1,0:T(8,128)(2,1)S(1)}, bf16[4,272,256]{2,1,0:T(8,128)(2,1)}, u32[]{:S(2)}) copy-start(bf16[4,272,256]{2,1,0:T(8,128)(2,1)} %get-tuple-element.45) | copy-start | bytes 1671172
  42.5 39.2 %all-to-all-start = ((bf16[8,80,2048]{2,1,0:T(8,128)(2,1)}), bf16[8,80,2048]{2,1,0:T(8,128)(2,1)}, u32[]{:S(2)}, u32[]{:S(2)}) async-start(bf16[8,80,2048]{2,1,0:T(8,128)(2,1)} %bitcast.17), calls=%async_computation | async-start | bytes 5242880 | tf_op jit(solution)/shard_map/all_to_all | solution.py:283
  47.1 8.7 %collective-permute-start.7 = (bf16[4,272,256]{2,1,0:T(8,128)(2,1)S(1)}, bf16[4,272,256]{2,1,0:T(8,128)(2,1)S(1)}, u32[]{:S(2)}, u32[]{:S(2)}) collective-permute-start(bf16[4,272,256]{2,1,0:T(8,128)(2,1)S(1)} %copy-done.4), channel_id=1, source_target_pairs={{0,8},{8,0},{16,24},{24,16},{32,40},{40,32},{48,56},{56,48},{64,72... | collective-permute-start | bytes 1671176 | tf_op jit(solution)/shard_map/ppermute | solution.py:32
  55.9 10.8 %collective-permute-start.8 = (bf16[272,256]{1,0:T(8,128)(2,1)S(1)}, bf16[272,256]{1,0:T(8,128)(2,1)S(1)}, u32[]{:S(2)}, u32[]{:S(2)}) collective-permute-start(bf16[272,256]{1,0:T(8,128)(2,1)S(1)} %get-tuple-element.51), channel_id=1, source_target_pairs={{0,32},{8,40},{16,48},{24,56},{32,0},{40,8},{48,16},{56,24},{64,96... | collective-permute-start | bytes 417800 | tf_op jit(solution)/shard_map/ppermute | solution.py:36
  60.0 9.0 %collective-permute-start.10 = (bf16[272,256]{1,0:T(8,128)(2,1)S(1)}, bf16[272,256]{1,0:T(8,128)(2,1)S(1)}, u32[]{:S(2)}, u32[]{:S(2)}) collective-permute-start(bf16[272,256]{1,0:T(8,128)(2,1)S(1)} %get-tuple-element.52), channel_id=1, source_target_pairs={{0,16},{8,24},{16,0},{24,8},{32,48},{40,56},{48,32},{56,40},{64,80... | collective-permute-start | bytes 417800 | tf_op jit(solution)/shard_map/ppermute | solution.py:36
  64.0 30.0 %copy-start = (bf16[4,256,256]{2,1,0:T(8,128)(2,1)S(1)}, bf16[4,256,256]{2,1,0:T(8,128)(2,1)}, u32[]{:S(2)}) copy-start(bf16[4,256,256]{2,1,0:T(8,128)(2,1)} %get-tuple-element.31.own_1) | copy-start | bytes 1572868
  64.0 30.0 %copy-start.1 = (bf16[4,256,256]{2,1,0:T(8,128)(2,1)S(1)}, bf16[4,256,256]{2,1,0:T(8,128)(2,1)}, u32[]{:S(2)}) copy-start(bf16[4,256,256]{2,1,0:T(8,128)(2,1)} %get-tuple-element.44.own_2) | copy-start | bytes 1572868
  64.0 30.0 %copy-start.2 = (s32[11]{0:T(128)S(1)}, s32[11]{0:T(128)}, u32[]{:S(2)}) copy-start(s32[11]{0:T(128)} %stack.58.info) | copy-start | bytes 136
  64.0 8.3 %collective-permute-start.9 = (bf16[272,256]{1,0:T(8,128)(2,1)S(1)}, bf16[272,256]{1,0:T(8,128)(2,1)S(1)}, u32[]{:S(2)}, u32[]{:S(2)}) collective-permute-start(bf16[272,256]{1,0:T(8,128)(2,1)S(1)} %get-tuple-element.53), channel_id=1, source_target_pairs={{0,48},{8,56},{16,32},{24,40},{32,16},{40,24},{48,0},{56,8},{64,11... | collective-permute-start | bytes 417800 | tf_op jit(solution)/shard_map/ppermute | solution.py:36
  72.4 12.3 %collective-permute-start.13 = (bf16[256,256]{1,0:T(8,128)(2,1)S(1)}, bf16[256,256]{1,0:T(8,128)(2,1)S(1)}, u32[]{:S(2)}, u32[]{:S(2)}) collective-permute-start(bf16[256,256]{1,0:T(8,128)(2,1)S(1)} %fusion.2), channel_id=1, source_target_pairs={{0,48},{8,56},{16,32},{24,40},{32,16},{40,24},{48,0},{56,8},{64,11... | collective-permute-start | bytes 393224 | tf_op jit(solution)/shard_map/ppermute | solution.py:36
  75.7 14.0 %collective-permute-start.12 = (bf16[256,256]{1,0:T(8,128)(2,1)S(1)}, bf16[256,256]{1,0:T(8,128)(2,1)S(1)}, u32[]{:S(2)}, u32[]{:S(2)}) collective-permute-start(bf16[256,256]{1,0:T(8,128)(2,1)S(1)} %fusion.2), channel_id=1, source_target_pairs={{0,32},{8,40},{16,48},{24,56},{32,0},{40,8},{48,16},{56,24},{64,96... | collective-permute-start | bytes 393224 | tf_op jit(solution)/shard_map/ppermute | solution.py:36
  79.3 10.3 %collective-permute-start.11 = (bf16[256,256]{1,0:T(8,128)(2,1)S(1)}, bf16[256,256]{1,0:T(8,128)(2,1)S(1)}, u32[]{:S(2)}, u32[]{:S(2)}) collective-permute-start(bf16[256,256]{1,0:T(8,128)(2,1)S(1)} %fusion.2), channel_id=1, source_target_pairs={{0,16},{8,24},{16,0},{24,8},{32,48},{40,56},{48,32},{56,40},{64,80... | collective-permute-start | bytes 393224 | tf_op jit(solution)/shard_map/ppermute | solution.py:36
  89.7 4.3 %collective-permute-start.14 = (bf16[4,256,256]{2,1,0:T(8,128)(2,1)S(1)}, bf16[4,256,256]{2,1,0:T(8,128)(2,1)S(1)}, u32[]{:S(2)}, u32[]{:S(2)}) collective-permute-start(bf16[4,256,256]{2,1,0:T(8,128)(2,1)S(1)} %pad_maximum_fusion.mine), channel_id=1, source_target_pairs={{0,8},{8,0},{16,24},{24,16},{32,40},{40,32},{48,56},{56,48},{64,72... | collective-permute-start | bytes 1572872 | tf_op jit(solution)/shard_map/ppermute | solution.py:32
